TPU v7x, 32 devices: a whole 2x2x4 slice. The times are simulated.
32 devices in a mesh: exp: 16 (over z, y, x), rep: 2 (over core).
Axes of the slice: x: 2, y: 2, z: 4, core: 2. Of those that a mesh axis runs over, the one named last changes fastest.
Arguments:
- latent: bfloat16 [32, 16, 64], P('exp'), may hold values from -6 to 6
- stem_weight: bfloat16 [144, 1536], replicated, may hold values from -0.5 to 0.5
- norm_gain: float32 [1536], replicated, may hold values from 0.4 to 1.6
- router_weight: bfloat16 [1536, 8], replicated, may hold values from -0.15625 to 0.15625
- routes: int32 [2048, 2], P('exp'), may hold values from 0 to 7, all different within a row; in each aligned block of 128 rows (0 to 127, 128 to 255, ...) at most 40 rows name the same one
- gate_weight: bfloat16 [1536, 24576], P('rep', 'exp'), may hold values from -0.15625 to 0.15625
- up_weight: bfloat16 [1536, 24576], P('rep', 'exp'), may hold values from -0.15625 to 0.15625
- down_weight: bfloat16 [24576, 1536], P('exp', 'rep'), may hold values from -0.109375 to 0.109375
- grad_mixed: bfloat16 [2048, 1536], P('exp'), may hold values from -6 to 6
Outputs:
- mixed: bfloat16 [2048, 1536], P('exp')
- grad_latent: float32 [32, 16, 64], P('exp')
- grad_gate: float32 [1536, 24576], P('rep', 'exp')
- grad_up: float32 [1536, 24576], P('rep', 'exp')
- grad_down: float32 [24576, 1536], P('exp', 'rep')
Inputs may be any that keep to these rules, and one draw needn't show every extreme that they name: `routes`: A token's 2 experts differ. Within the 128 tokens of one device, no expert is named more than 40 times, and in every draw some device's tokens name some expert exactly 40 times.
All inputs are finite; a program needn't handle non-finite values.
Results may differ from a plain program's by a relative error of at most 0.023.
Values may be sent and summed in bfloat16 or wider, within the bound.
No kernel may reach another device: no remote copies, remote signals or barrier semaphores. Data moves between devices by JAX's collectives and lax.ppermute only.
A program may use at most 128 MiB of HBM per device.

v0:
```python
import jax
import jax.numpy as jnp
from jax import lax
from jax.sharding import PartitionSpec as P

CAP = 40
F32 = jnp.float32
BF16 = jnp.bfloat16


def dot(a, b, contract, batch=((), ())):
    return lax.dot_general(a, b, (contract, batch), preferred_element_type=F32)


def other_core(values):
    return lax.ppermute(values, "rep", [(0, 1), (1, 0)])


def core_sum(values, wire=BF16):
    if lax.axis_size("rep") == 2:
        return values + other_core(values.astype(wire)).astype(F32)
    return lax.psum(values, "rep")


def core_join(values):
    if lax.axis_size("rep") == 2:
        other = other_core(values)
        first = lax.axis_index("rep") == 0
        return jnp.concatenate(
            [jnp.where(first, values, other), jnp.where(first, other, values)], axis=1
        )
    return lax.all_gather(values, "rep", axis=1, tiled=True)


def exchange(values):
    return lax.all_to_all(values, "exp", split_axis=0, concat_axis=0, tiled=True)


def column_keep(count, width, j):
    column = jnp.arange(count, dtype=jnp.int32) % width + (j - 1)
    return ((column >= 0) & (column < width))[None, :]


def patches_of(cells, width):
    count = cells.shape[1]
    padded = jnp.pad(cells, ((0, 0), (width + 1, width + 1)))
    pieces = []
    for i in range(3):
        for j in range(3):
            start = i * width + j
            piece = padded[:, start : start + count]
            pieces.append(jnp.where(column_keep(count, width, j), piece, 0))
    return jnp.concatenate(pieces, axis=0)


def patches_sum(terms, width):
    channels, count = terms.shape[0] // 9, terms.shape[1]
    padded = jnp.pad(terms, ((0, 0), (width + 1, width + 1)))
    total = 0.0
    for i in range(3):
        for j in range(3):
            start = (2 - i) * width + (2 - j)
            k = 3 * i + j
            piece = padded[k * channels : (k + 1) * channels, start : start + count]
            total = total + jnp.where(column_keep(count, width, 2 - j), piece, 0)
    return total


def selection(named):
    tokens = named.shape[-1]
    order = jnp.arange(tokens, dtype=jnp.int32)
    before = (order[:, None] <= order[None, :]).astype(BF16)
    flat = named.astype(BF16).reshape(-1, tokens)
    place = (dot(flat, before, ((1,), (0,))).astype(jnp.int32) - 1).reshape(named.shape)
    slot = jnp.arange(CAP, dtype=jnp.int32)[:, None]
    return ((place[..., None, :] == slot) & named[..., None, :]).astype(BF16)


def local(
    latent,
    stem_weight,
    norm_gain,
    router_weight,
    routes,
    gate_weight,
    up_weight,
    down_weight,
    grad_mixed,
):
    rows_here, channels, width = latent.shape
    half, hid = gate_weight.shape
    model_width = stem_weight.shape[1]
    experts = router_weight.shape[1]
    top = routes.shape[1]
    tok = rows_here * width
    blocks = lax.axis_size("exp")
    shards = blocks // experts
    slots = blocks * CAP
    me = lax.axis_index("exp")
    mine = me // shards
    column = lax.axis_index("rep") * half

    cells = latent.transpose(1, 0, 2).reshape(channels, tok)
    routes_t = routes.T
    payload = jnp.concatenate([cells, routes_t.astype(BF16)], axis=0)
    image = exchange(jnp.broadcast_to(payload[None], (blocks,) + payload.shape))

    gain_here = lax.dynamic_slice_in_dim(norm_gain, column, half)
    stem_here = lax.dynamic_slice_in_dim(stem_weight, column, half, 1)
    router_here = lax.dynamic_slice_in_dim(router_weight, column, half, 0).astype(F32)
    cot = lax.dynamic_slice_in_dim(grad_mixed, column, half, 1)
    experts_range = jnp.arange(experts, dtype=jnp.int32)
    own_named = jnp.any(routes_t[None] == experts_range[:, None, None], axis=1)
    own_sel = selection(own_named)
    cot_slots = dot(own_sel.reshape(experts * CAP, tok), cot, ((1,), (0,))).astype(BF16)
    cot_slots = jnp.repeat(cot_slots.reshape(experts, CAP, half), shards, axis=0)
    slot_cot = exchange(cot_slots).reshape(slots, half)

    lat_all = image[:, :channels].transpose(1, 0, 2).reshape(channels, blocks * tok)
    routes_all = image[:, channels:].astype(jnp.int32)
    sel = selection(jnp.any(routes_all == mine, axis=1))
    patches = patches_of(lat_all, width)
    slot_patches = dot(
        sel, patches.reshape(-1, blocks, tok), ((2,), (2,)), ((0,), (1,))
    ).astype(BF16)
    stem = dot(slot_patches.reshape(slots, -1), stem_weight, ((1,), (0,))).astype(BF16)
    value = stem.astype(F32)
    scale = lax.rsqrt(jnp.mean(value * value, axis=-1, keepdims=True) + 1e-06)
    normed = (value * scale * norm_gain).astype(BF16)
    logits = dot(normed, router_weight, ((1,), (0,)))
    other = (jnp.sum(routes_all, axis=1) - mine).astype(BF16)
    slot_other = dot(sel, other, ((2,), (1,)), ((0,), (0,))).astype(jnp.int32).reshape(slots, 1)
    is_mine = (experts_range == mine)[None, :].astype(F32)
    is_other = (experts_range[None, :] == slot_other).astype(F32)
    sig_mine = jax.nn.sigmoid(jnp.sum(logits * is_mine, axis=1, keepdims=True))
    sig_other = jax.nn.sigmoid(jnp.sum(logits * is_other, axis=1, keepdims=True))
    gate = sig_mine / (sig_mine + sig_other)
    rest = sig_other / (sig_mine + sig_other)
    normed_here = lax.dynamic_slice_in_dim(normed, column, half, 1)
    value_here = lax.dynamic_slice_in_dim(stem, column, half, 1).astype(F32)
    stem_back = dot(stem, stem_weight, ((1,), (1,)))

    pre_gate = core_sum(dot(normed_here, gate_weight, ((1,), (0,))))
    pre_up = core_sum(dot(normed_here, up_weight, ((1,), (0,))))
    sigma = jax.nn.sigmoid(pre_gate)
    hidden = (pre_gate * sigma * pre_up).astype(BF16)
    part = dot(hidden, down_weight, ((1,), (0,)))
    returned = exchange((gate * part).astype(BF16).reshape(blocks, CAP, half))

    slot_grad = (gate * slot_cot.astype(F32)).astype(BF16)
    grad_hidden = core_sum(dot(slot_grad, down_weight, ((1,), (1,))))
    grad_gate_pre = (grad_hidden * pre_up * sigma * (1.0 + pre_gate * (1.0 - sigma))).astype(BF16)
    grad_up_pre = (grad_hidden * pre_gate * sigma).astype(BF16)
    back = dot(grad_gate_pre, gate_weight, ((1,), (1,)))
    back = back + dot(grad_up_pre, up_weight, ((1,), (1,)))

    grad_gates = core_sum(jnp.sum(slot_cot.astype(F32) * part, axis=1), F32)[:, None]
    to_mine = grad_gates * gate * rest * (1.0 - sig_mine)
    to_other = -grad_gates * gate * rest * (1.0 - sig_other)
    grad_logits = to_mine * is_mine + to_other * is_other
    grad_normed = back + lax.dot_general(
        grad_logits, router_here, (((1,), (1,)), ((), ())), precision=lax.Precision.HIGHEST
    )
    scaled = gain_here * grad_normed
    along = jnp.sum(value_here * scaled, axis=1, keepdims=True) * scale**3 / model_width
    projected = dot((scale * scaled).astype(BF16), stem_here, ((1,), (1,))) - along * stem_back
    terms = dot(
        projected.astype(BF16).reshape(blocks, CAP, -1), sel, ((1,), (1,)), ((0,), (0,))
    )
    own_terms = dot(stem_here, cot, ((1,), (1,)))
    here = (jnp.arange(blocks, dtype=jnp.int32) == me).astype(F32)[:, None, None]
    terms = (terms + here * own_terms).transpose(1, 0, 2).reshape(-1, blocks * tok)
    lat_terms = patches_sum(terms, width).reshape(channels, blocks, tok).transpose(1, 0, 2)
    lat_sum = jnp.sum(exchange(lat_terms), axis=0)
    lat_sum = core_sum(lat_sum, F32)
    grad_latent = lat_sum.reshape(channels, rows_here, width).transpose(1, 0, 2)

    grad_gate = dot(normed_here, grad_gate_pre, ((0,), (0,)))
    grad_up = dot(normed_here, grad_up_pre, ((0,), (0,)))
    grad_down = dot(hidden, slot_grad, ((0,), (0,)))

    own_patches = lax.dynamic_slice_in_dim(patches, me * tok, tok, 1)
    own_stem = dot(own_patches, stem_here, ((0,), (0,))).astype(BF16).astype(F32)
    taken = jnp.repeat(own_sel, shards, axis=0).reshape(slots, tok)
    mixed = own_stem + dot(taken, returned.reshape(slots, half), ((0,), (0,)))
    mixed = core_join(mixed.astype(BF16))
    return (mixed, grad_latent, grad_gate, grad_up, grad_down)


def solution(mesh):
    return jax.shard_map(
        local,
        mesh=mesh,
        in_specs=(
            P("exp", None, None),
            P(),
            P(),
            P(),
            P("exp", None),
            P("rep", "exp"),
            P("rep", "exp"),
            P("exp", "rep"),
            P("exp", None),
        ),
        out_specs=(
            P("exp", None),
            P("exp", None, None),
            P("rep", "exp"),
            P("rep", "exp"),
            P("exp", "rep"),
        ),
        check_vma=False,
    )
```

profile of v0, /device:TPU:0, one launch (start us, length us, event | category | flops | bytes accessed | tf_op | source)
XLA Modules:
  0.0 115.9 jit_solution(4157458171818186202)
XLA Ops:
  0.6 0.8 bitcast_convert_fusion
  1.5 0.7 copy.29
  2.2 0.1 reshape.159
  2.3 0.7 broadcast_in_dim.172
  2.9 8.3 %all-to-all-start = ((bf16[16,18,128]{2,1,0:T(8,128)(2,1)}), bf16[16,18,128]{2,1,0:T(8,128)(2,1)S(1)}, u32[]{:S(2)}, u32[]{:S(2)}) async-start(bf16[16,18,128]{2,1,0:T(8,128)(2,1)} %broadcast_in_dim.172), calls=%async_computation | async-start | bytes 196608 | tf_op jit(solution)/shard_map/all_to_all | solution.py:36
  11.3 0.7 fusion.84
  12.0 0.1 fusion.10
  12.2 0.1 fusion.38
  12.3 1.2 %convolution_convert_fusion.1 = bf16[320,768]{1,0:T(8,128)(2,1)S(1)} fusion(pred[320,128]{1,0:T(32,128)(4,1)S(1)} %fusion.38, bf16[128,1536]{1,0:T(8,128)(2,1)} %param.17, s32[]{:T(128)S(6)} %select_n.180), kind=kOutput, calls=%fused_computation.31 | convolution fusion | flops 63160320 | bytes 729092 | tf_op jit(solution)/shard_map/dot_general | solution.py:12
  13.6 5.4 %all-to-all-done = bf16[16,18,128]{2,1,0:T(8,128)(2,1)S(1)} async-done(((bf16[16,18,128]{2,1,0:T(8,128)(2,1)}), bf16[16,18,128]{2,1,0:T(8,128)(2,1)S(1)}, u32[]{:S(2)}, u32[]{:S(2)}) %all-to-all-start) | async-done | bytes 73760 | tf_op jit(solution)/shard_map/all_to_all | solution.py:36
  18.9 1.0 broadcast_in_dim.177
  20.0 3.6 %all-to-all-start.2 = ((bf16[16,40,768]{2,1,0:T(8,128)(2,1)}), bf16[16,40,768]{2,1,0:T(8,128)(2,1)S(1)}, u32[]{:S(2)}, u32[]{:S(2)}) async-start(bf16[16,40,768]{2,1,0:T(8,128)(2,1)} %bitcast.94), calls=%async_computation.2 | async-start | bytes 1966080 | tf_op jit(solution)/shard_map/all_to_all | solution.py:36
  23.6 0.1 select_dynamic-update-slice_fusion.8
  23.7 0.1 select_dynamic-update-slice_fusion.7
  23.8 0.1 select_dynamic-update-slice_fusion.6
  23.9 0.1 select_dynamic-update-slice_fusion.5
  24.0 0.1 select_dynamic-update-slice_fusion.3
  24.1 0.1 select_dynamic-update-slice_fusion.2
  24.2 0.1 select_dynamic-update-slice_fusion.1
  24.3 0.1 select_dynamic-update-slice_fusion
  24.4 0.8 copy-done.15
  25.3 0.1 fusion.9
  25.5 0.2 fusion.24
  25.6 0.1 eq.128
  25.8 1.5 %convolution_convert_fusion.2 = bf16[16,40,144]{2,1,0:T(8,128)(2,1)S(1)} fusion(s32[16,128]{1,0:T(8,128)S(1)} %fusion.9, pred[16,128]{1,0:T(8,128)(4,1)S(1)} %compare_reduce_fusion, bf16[144,2048]{1,0:T(8,128)(2,1)} %copy-done.15), kind=kOutput, calls=%fused_computation.32 | convolution fusion | flops 23848960 | bytes 784384 | tf_op jit(solution)/shard_map/dot_general | solution.py:12
  27.3 1.8 %fusion = (f32[640]{0:T(1024)S(1)}, bf16[640,1536]{1,0:T(8,128)(2,1)S(1)}) fusion(bf16[640,144]{1,0:T(8,128)(2,1)S(1)} %bitcast.100, bf16[144,1536]{1,0:T(8,128)(2,1)} %param.10), kind=kOutput, calls=%fused_computation.2 | convolution fusion | flops 287047040 | bytes 2595328 | tf_op jit(solution)/shard_map/dot_general | solution.py:12
  29.1 0.5 fusion.2
  29.6 0.7 copy-done.4
  30.3 1.1 copy-done.23
  31.5 4.3 %fusion.101 = (bf16[640,1536]{1,0:T(8,128)(2,1)}, f32[640,1536]{1,0:T(8,128)}) fusion(bf16[768,1536]{1,0:T(8,128)(2,1)S(1)} %copy-done.23, bf16[640,1536]{1,0:T(8,128)(2,1)S(1)} %fusion.2, s32[]{:T(128)S(6)} %select_n.180), kind=kOutput, calls=%fused_computation.174 | convolution fusion | flops 1510932480 | bytes 9240580 | tf_op jit(solution)/shard_map/dot_general | solution.py:12
  35.7 4.3 %fusion.103 = (bf16[640,1536]{1,0:T(8,128)(2,1)}, f32[640,1536]{1,0:T(8,128)}) fusion(bf16[768,1536]{1,0:T(8,128)(2,1)S(1)} %copy-done.25, bf16[640,1536]{1,0:T(8,128)(2,1)S(1)} %fusion.2, s32[]{:T(128)S(6)} %select_n.180), kind=kOutput, calls=%fused_computation.176 | convolution fusion | flops 1510932480 | bytes 9240580 | tf_op jit(solution)/shard_map/dot_general | solution.py:12
  40.1 0.5 collective-permute-start
  40.6 0.6 select_reduce_fusion
  41.2 4.4 %all-to-all-done.2 = bf16[16,40,768]{2,1,0:T(8,128)(2,1)S(1)} async-done(((bf16[16,40,768]{2,1,0:T(8,128)(2,1)}), bf16[16,40,768]{2,1,0:T(8,128)(2,1)S(1)}, u32[]{:S(2)}, u32[]{:S(2)}) %all-to-all-start.2) | async-done | bytes 983072 | tf_op jit(solution)/shard_map/all_to_all | solution.py:36
  45.6 0.3 fusion.3
  45.9 1.7 %fusion.102 = (bf16[640,1536]{1,0:T(8,128)(2,1)S(1)}, f32[640,1536]{1,0:T(8,128)S(1)}) fusion(bf16[640,768]{1,0:T(8,128)(2,1)S(1)} %fusion.3, bf16[1536,768]{1,0:T(8,128)(2,1)S(1)} %copy-done), kind=kOutput, calls=%fused_computation.175 | convolution fusion | flops 1510932480 | bytes 9240576 | tf_op jit(solution)/shard_map/dot_general | solution.py:12
  47.8 0.2 fusion.27
  48.1 3.6 %collective-permute-done.3 = bf16[640,1536]{1,0:T(8,128)(2,1)S(1)} collective-permute-done((bf16[640,1536]{1,0:T(8,128)(2,1)S(1)}, bf16[640,1536]{1,0:T(8,128)(2,1)S(1)}, u32[]{:S(2)}, u32[]{:S(2)}) %collective-permute-start.3) | collective-permute-done | bytes 1966112 | tf_op jit(solution)/shard_map/ppermute | solution.py:16
  51.7 4.7 %multiply_convert_fusion.1 = (bf16[640,1536]{1,0:T(8,128)(2,1)S(1)}, bf16[640,1536]{1,0:T(8,128)(2,1)S(1)}, bf16[640,1536]{1,0:T(8,128)(2,1)S(1)}) fusion(f32[640,1536]{1,0:T(8,128)S(1)} %copy-done.6, bf16[640,1536]{1,0:T(8,128)(2,1)} %collective-permute-done.1, f32[640,1536]{1,0:T(8,128)S(1)} %get-tuple-element.36, ...), kind=kLoop, calls=%fused_computation.6 | loop fusion | flops 21626880 | bytes 23592960 | tf_op jit(solution)/shard_map/convert_element_type | solution.py:152
  56.4 2.7 %fusion.4 = (f32[640]{0:T(1024)S(1)}, bf16[640,768]{1,0:T(8,128)(2,1)}) fusion(bf16[16,40,768]{2,1,0:T(8,128)(2,1)S(1)} %all-to-all-done.2, f32[640]{0:T(1024)S(1)} %multiply_divide_fusion.1, bf16[640,1536]{1,0:T(8,128)(2,1)S(1)} %get-tuple-element.24, bf16[1536,768]{1,0:T(8,128)(2,1)S(1)} %copy-done), kind=kOutput, calls=%fused_computation.16 | convolution fusion | flops 1512406400 | bytes 6296576 | tf_op jit(solution)/shard_map/dot_general | solution.py:12
  59.2 0.1 collective-permute-start.4
  59.3 0.5 copy-done.24
  59.8 1.7 %fusion.104 = f32[640,768]{1,0:T(8,128)S(1)} fusion(bf16[640,1536]{1,0:T(8,128)(2,1)S(1)} %get-tuple-element.23, bf16[768,1536]{1,0:T(8,128)(2,1)S(1)} %copy-done.24), kind=kOutput, calls=%fused_computation.177 | convolution fusion | flops 1509949440 | bytes 6291456 | tf_op jit(solution)/shard_map/dot_general | solution.py:12
  61.6 1.0 fusion.60
  62.7 0.4 copy-done.5
  63.1 2.0 %multiply_reduce_fusion = (f32[640]{0:T(1024)S(1)}, f32[640,768]{1,0:T(8,128)S(1)}) fusion(bf16[640,1536]{1,0:T(8,128)(2,1)S(1)} %copy-done.5, s32[]{:T(128)S(6)} %select_n.180, f32[640,768]{1,0:T(8,128)S(1)} %fusion.60, f32[640,768]{1,0:T(8,128)S(1)} %fusion.104, bf16[640,1536]{1,0:T(8,128)(2,1)S(1)} %get-tuple-element.22, ...), kind=kOutput, calls=%fused_computation.17 | convolution fusion | flops 1512897920 | bytes 11212292 | tf_op jit(solution)/shard_map/dot_general | solution.py:12
  65.1 0.8 convolution_multiply_fusion
  65.9 0.6 fusion.8
  66.5 0.2 copy.32
  66.6 0.4 fusion.5
  67.0 0.1 copy_bitcast_fusion
  67.2 0.3 bitcast_bitcast_fusion
  67.5 13.5 %all_to_all.20 = f32[16,16,128]{2,1,0:T(8,128)S(1)} all-to-all(f32[16,16,128]{2,1,0:T(8,128)S(1)} %bitcast_bitcast_fusion), channel_id=1, replica_groups=mesh['exp'=16,'rep'=2] {'exp'}, dimensions={0} | all-to-all | bytes 262144 | tf_op jit(solution)/shard_map/all_to_all | solution.py:36
  81.0 3.9 %all-to-all-start.1 = ((bf16[16,40,768]{2,1,0:T(8,128)(2,1)}), bf16[16,40,768]{2,1,0:T(8,128)(2,1)S(1)}, u32[]{:S(2)}, u32[]{:S(2)}) async-start(bf16[16,40,768]{2,1,0:T(8,128)(2,1)} %bitcast.98), calls=%async_computation.1 | async-start | bytes 1966080 | tf_op jit(solution)/shard_map/all_to_all | solution.py:36
  84.9 1.2 %fusion.7 = f32[128,768]{1,0:T(8,128)S(1)} fusion(bf16[144,1536]{1,0:T(8,128)(2,1)} %param.10, s32[]{:T(128)S(6)} %select_n.180, bf16[144,2048]{1,0:T(8,128)(2,1)} %copy-done.15, s32[]{:T(128)S(6)} %select_n.179), kind=kOutput, calls=%fused_computation.39 | convolution fusion | flops 28508160 | bytes 651272 | tf_op jit(solution)/shard_map/dot_general | solution.py:12
  86.2 5.9 %fusion.14 = f32[768,1536]{1,0:T(8,128)} fusion(bf16[640,1536]{1,0:T(8,128)(2,1)} %copy-done.12, bf16[640,1536]{1,0:T(8,128)(2,1)S(1)} %copy-done.3, s32[]{:T(128)S(6)} %select_n.180), kind=kOutput, calls=%fused_computation.48 | convolution fusion | flops 1509949440 | bytes 7667716 | tf_op jit(solution)/shard_map/dot_general | solution.py:12
  92.1 4.3 %fusion.105 = f32[1536,768]{1,0:T(8,128)} fusion(bf16[640,1536]{1,0:T(8,128)(2,1)S(1)} %copy-done.11, bf16[640,768]{1,0:T(8,128)(2,1)S(1)} %copy-done.14), kind=kOutput, calls=%fused_computation.178 | convolution fusion | flops 1509949440 | bytes 7667712 | tf_op jit(solution)/shard_map/dot_general | solution.py:12
  96.4 0.6 reduce_sum.69
  97.0 10.0 %all-to-all-done.1 = bf16[16,40,768]{2,1,0:T(8,128)(2,1)S(1)} async-done(((bf16[16,40,768]{2,1,0:T(8,128)(2,1)}), bf16[16,40,768]{2,1,0:T(8,128)(2,1)S(1)}, u32[]{:S(2)}, u32[]{:S(2)}) %all-to-all-start.1) | async-done | bytes 983072 | tf_op jit(solution)/shard_map/all_to_all | solution.py:36
  107.0 0.4 fusion.6
  107.4 6.2 %fusion.12 = f32[768,1536]{1,0:T(8,128)} fusion(bf16[640,1536]{1,0:T(8,128)(2,1)} %copy-done.9, bf16[640,1536]{1,0:T(8,128)(2,1)} %copy-done.2, s32[]{:T(128)S(6)} %select_n.180), kind=kOutput, calls=%fused_computation.46 | convolution fusion | flops 1509949440 | bytes 7667716 | tf_op jit(solution)/shard_map/dot_general | solution.py:12
  113.7 0.7 add.275
  114.5 0.6 copy.36
  115.1 0.8 pad_maximum_fusion
  (80 shorter events, 0.8 us)
Async XLA Ops:
  0.6 45.2 %copy-start = (bf16[1536,768]{1,0:T(8,128)(2,1)S(1)}, bf16[1536,768]{1,0:T(8,128)(2,1)}, u32[]{:S(2)}) copy-start(bf16[1536,768]{1,0:T(8,128)(2,1)} %param.16) | copy-start | bytes 7077892
  2.9 16.0 %all-to-all-start = ((bf16[16,18,128]{2,1,0:T(8,128)(2,1)}), bf16[16,18,128]{2,1,0:T(8,128)(2,1)S(1)}, u32[]{:S(2)}, u32[]{:S(2)}) async-start(bf16[16,18,128]{2,1,0:T(8,128)(2,1)} %broadcast_in_dim.172), calls=%async_computation | async-start | bytes 196608 | tf_op jit(solution)/shard_map/all_to_all | solution.py:36
  12.0 8.0 %copy-start.21 = (pred[8,128]{1,0:T(8,128)(4,1)}, pred[8,128]{1,0:T(8,128)(4,1)S(1)}, u32[]{:S(2)}) copy-start(pred[8,128]{1,0:T(8,128)(4,1)S(1)} %fusion.84) | copy-start | bytes 3076
  12.1 7.8 %copy-start.19 = (s32[8,128]{1,0:T(8,128)}, s32[8,128]{1,0:T(8,128)S(1)}, u32[]{:S(2)}) copy-start(s32[8,128]{1,0:T(8,128)S(1)} %fusion.10) | copy-start | bytes 12292
  20.0 25.6 %all-to-all-start.2 = ((bf16[16,40,768]{2,1,0:T(8,128)(2,1)}), bf16[16,40,768]{2,1,0:T(8,128)(2,1)S(1)}, u32[]{:S(2)}, u32[]{:S(2)}) async-start(bf16[16,40,768]{2,1,0:T(8,128)(2,1)} %bitcast.94), calls=%async_computation.2 | async-start | bytes 1966080 | tf_op jit(solution)/shard_map/all_to_all | solution.py:36
  24.4 0.8 copy-start.15
  27.3 1.8 %copy-start.18 = (f32[1536]{0:T(1024)S(1)}, f32[1536]{0:T(1024)}, u32[]{:S(2)}) copy-start(f32[1536]{0:T(1024)} %param.11) | copy-start | bytes 18436
  29.1 1.3 %copy-start.4 = (bf16[640,1536]{1,0:T(8,128)(2,1)}, bf16[640,1536]{1,0:T(8,128)(2,1)S(1)}, u32[]{:S(2)}) copy-start(bf16[640,1536]{1,0:T(8,128)(2,1)S(1)} %get-tuple-element.32) | copy-start | bytes 5898244
  29.1 2.4 %copy-start.23 = (bf16[768,1536]{1,0:T(8,128)(2,1)S(1)}, bf16[768,1536]{1,0:T(8,128)(2,1)}, u32[]{:S(2)}) copy-start(bf16[768,1536]{1,0:T(8,128)(2,1)} %param.15) | copy-start | bytes 7077892
  31.5 9.1 %copy-start.2 = (bf16[640,1536]{1,0:T(8,128)(2,1)}, bf16[640,1536]{1,0:T(8,128)(2,1)S(1)}, u32[]{:S(2)}) copy-start(bf16[640,1536]{1,0:T(8,128)(2,1)S(1)} %fusion.2) | copy-start | bytes 5898244
  31.5 4.3 %copy-start.25 = (bf16[768,1536]{1,0:T(8,128)(2,1)S(1)}, bf16[768,1536]{1,0:T(8,128)(2,1)}, u32[]{:S(2)}) copy-start(bf16[768,1536]{1,0:T(8,128)(2,1)} %param.14) | copy-start | bytes 7077892
  35.7 4.9 %copy-start.17 = (bf16[1536,8]{0,1:T(8,128)(2,1)S(1)}, bf16[1536,8]{0,1:T(8,128)(2,1)}, u32[]{:S(2)}) copy-start(bf16[1536,8]{0,1:T(8,128)(2,1)} %param.12) | copy-start | bytes 73732
  35.7 12.3 %collective-permute-start.1 = (bf16[640,1536]{1,0:T(8,128)(2,1)}, bf16[640,1536]{1,0:T(8,128)(2,1)}, u32[]{:S(2)}, u32[]{:S(2)}) collective-permute-start(bf16[640,1536]{1,0:T(8,128)(2,1)} %get-tuple-element.33), channel_id=1, source_target_pairs={{0,1},{1,0},{2,3},{3,2},{4,5},{5,4},{6,7},{7,6},{8,9},{9,8},{10,11... | collective-permute-start | bytes 5898248 | tf_op jit(solution)/shard_map/ppermute | solution.py:16
  40.1 8.0 %collective-permute-start = (bf16[640,1536]{1,0:T(8,128)(2,1)}, bf16[640,1536]{1,0:T(8,128)(2,1)}, u32[]{:S(2)}, u32[]{:S(2)}) collective-permute-start(bf16[640,1536]{1,0:T(8,128)(2,1)} %get-tuple-element.37), channel_id=1, source_target_pairs={{0,1},{1,0},{2,3},{3,2},{4,5},{5,4},{6,7},{7,6},{8,9},{9,8},{10,11... | collective-permute-start | bytes 5898248 | tf_op jit(solution)/shard_map/ppermute | solution.py:16
  45.9 1.8 %copy-start.13 = (bf16[640,768]{1,0:T(8,128)(2,1)}, bf16[640,768]{1,0:T(8,128)(2,1)S(1)}, u32[]{:S(2)}) copy-start(bf16[640,768]{1,0:T(8,128)(2,1)S(1)} %fusion.3) | copy-start | bytes 2949124
  45.9 2.0 %copy-start.8 = (bf16[144,1536]{1,0:T(8,128)(2,1)S(1)}, bf16[144,1536]{1,0:T(8,128)(2,1)}, u32[]{:S(2)}) copy-start(bf16[144,1536]{1,0:T(8,128)(2,1)} %param.10) | copy-start | bytes 1327108
  45.9 1.9 %copy-start.16 = (bf16[128,1536]{1,0:T(8,128)(2,1)S(1)}, bf16[128,1536]{1,0:T(8,128)(2,1)}, u32[]{:S(2)}) copy-start(bf16[128,1536]{1,0:T(8,128)(2,1)} %param.17) | copy-start | bytes 1179652
  45.9 5.8 %copy-start.6 = (f32[640,1536]{1,0:T(8,128)S(1)}, f32[640,1536]{1,0:T(8,128)}, u32[]{:S(2)}) copy-start(f32[640,1536]{1,0:T(8,128)} %get-tuple-element.34) | copy-start | bytes 11796484
  45.9 5.8 %copy-start.7 = (f32[640,1536]{1,0:T(8,128)S(1)}, f32[640,1536]{1,0:T(8,128)}, u32[]{:S(2)}) copy-start(f32[640,1536]{1,0:T(8,128)} %get-tuple-element.38) | copy-start | bytes 11796484
  47.7 4.0 %collective-permute-start.3 = (bf16[640,1536]{1,0:T(8,128)(2,1)S(1)}, bf16[640,1536]{1,0:T(8,128)(2,1)S(1)}, u32[]{:S(2)}, u32[]{:S(2)}) collective-permute-start(bf16[640,1536]{1,0:T(8,128)(2,1)S(1)} %get-tuple-element.35), channel_id=1, source_target_pairs={{0,1},{1,0},{2,3},{3,2},{4,5},{5,4},{6,7},{7,6},{8,9},{9,8},{10,11... | collective-permute-start | bytes 5898248 | tf_op jit(solution)/shard_map/ppermute | solution.py:16
  56.4 2.8 %copy-start.10 = (bf16[640,1536]{1,0:T(8,128)(2,1)}, bf16[640,1536]{1,0:T(8,128)(2,1)S(1)}, u32[]{:S(2)}) copy-start(bf16[640,1536]{1,0:T(8,128)(2,1)S(1)} %get-tuple-element.24) | copy-start | bytes 5898244
  56.4 2.9 %copy-start.9 = (bf16[640,1536]{1,0:T(8,128)(2,1)}, bf16[640,1536]{1,0:T(8,128)(2,1)S(1)}, u32[]{:S(2)}) copy-start(bf16[640,1536]{1,0:T(8,128)(2,1)S(1)} %get-tuple-element.23) | copy-start | bytes 5898244
  56.4 6.2 %copy-start.12 = (bf16[640,1536]{1,0:T(8,128)(2,1)}, bf16[640,1536]{1,0:T(8,128)(2,1)S(1)}, u32[]{:S(2)}) copy-start(bf16[640,1536]{1,0:T(8,128)(2,1)S(1)} %get-tuple-element.22) | copy-start | bytes 5898244
  56.4 3.4 %copy-start.24 = (bf16[768,1536]{1,0:T(8,128)(2,1)S(1)}, bf16[768,1536]{1,0:T(8,128)(2,1)}, u32[]{:S(2)}) copy-start(bf16[768,1536]{1,0:T(8,128)(2,1)} %param.15) | copy-start | bytes 7077892
  59.2 2.4 %collective-permute-start.4 = (f32[640]{0:T(1024)S(1)}, f32[640]{0:T(1024)S(1)}, u32[]{:S(2)}, u32[]{:S(2)}) collective-permute-start(f32[640]{0:T(1024)S(1)} %get-tuple-element.25), channel_id=1, source_target_pairs={{0,1},{1,0},{2,3},{3,2},{4,5},{5,4},{6,7},{7,6},{8,9},{9,8},{10,11... | collective-permute-start | bytes 7688 | tf_op jit(solution)/shard_map/ppermute | solution.py:16
  59.8 2.8 %copy-start.26 = (bf16[768,1536]{1,0:T(8,128)(2,1)S(1)}, bf16[768,1536]{1,0:T(8,128)(2,1)}, u32[]{:S(2)}) copy-start(bf16[768,1536]{1,0:T(8,128)(2,1)} %param.14) | copy-start | bytes 7077892
  61.6 1.5 %copy-start.5 = (bf16[640,1536]{1,0:T(8,128)(2,1)S(1)}, bf16[640,1536]{1,0:T(8,128)(2,1)}, u32[]{:S(2)}) copy-start(bf16[640,1536]{1,0:T(8,128)(2,1)} %copy-done.4) | copy-start | bytes 5898244
  67.2 17.7 %copy-start.20 = (s32[8,128]{1,0:T(8,128)S(1)}, s32[8,128]{1,0:T(8,128)}, u32[]{:S(2)}) copy-start(s32[8,128]{1,0:T(8,128)} %copy-done.19) | copy-start | bytes 12292
  67.2 17.7 %copy-start.22 = (pred[8,128]{1,0:T(8,128)(4,1)S(1)}, pred[8,128]{1,0:T(8,128)(4,1)}, u32[]{:S(2)}) copy-start(pred[8,128]{1,0:T(8,128)(4,1)} %copy-done.21) | copy-start | bytes 3076
  67.2 19.0 %copy-start.3 = (bf16[640,1536]{1,0:T(8,128)(2,1)S(1)}, bf16[640,1536]{1,0:T(8,128)(2,1)}, u32[]{:S(2)}) copy-start(bf16[640,1536]{1,0:T(8,128)(2,1)} %copy-done.2) | copy-start | bytes 5898244
  81.0 26.0 %all-to-all-start.1 = ((bf16[16,40,768]{2,1,0:T(8,128)(2,1)}), bf16[16,40,768]{2,1,0:T(8,128)(2,1)S(1)}, u32[]{:S(2)}, u32[]{:S(2)}) async-start(bf16[16,40,768]{2,1,0:T(8,128)(2,1)} %bitcast.98), calls=%async_computation.1 | async-start | bytes 1966080 | tf_op jit(solution)/shard_map/all_to_all | solution.py:36
  86.2 5.9 %copy-start.11 = (bf16[640,1536]{1,0:T(8,128)(2,1)S(1)}, bf16[640,1536]{1,0:T(8,128)(2,1)}, u32[]{:S(2)}) copy-start(bf16[640,1536]{1,0:T(8,128)(2,1)} %copy-done.10) | copy-start | bytes 5898244
  86.2 5.9 %copy-start.14 = (bf16[640,768]{1,0:T(8,128)(2,1)S(1)}, bf16[640,768]{1,0:T(8,128)(2,1)}, u32[]{:S(2)}) copy-start(bf16[640,768]{1,0:T(8,128)(2,1)} %copy-done.13) | copy-start | bytes 2949124
  97.0 16.7 %collective-permute-start.5 = (f32[16,128]{1,0:T(8,128)}, f32[16,128]{1,0:T(8,128)}, u32[]{:S(2)}, u32[]{:S(2)}) collective-permute-start(f32[16,128]{1,0:T(8,128)} %reduce_sum.69), channel_id=1, source_target_pairs={{0,1},{1,0},{2,3},{3,2},{4,5},{5,4},{6,7},{7,6},{8,9},{9,8},{10,11... | collective-permute-start | bytes 24584 | tf_op jit(solution)/shard_map/ppermute | solution.py:16
  107.4 7.7 %collective-permute-start.2 = (bf16[128,768]{1,0:T(8,128)(2,1)S(1)}, bf16[128,768]{1,0:T(8,128)(2,1)S(1)}, u32[]{:S(2)}, u32[]{:S(2)}) collective-permute-start(bf16[128,768]{1,0:T(8,128)(2,1)S(1)} %fusion.6), channel_id=1, source_target_pairs={{0,1},{1,0},{2,3},{3,2},{4,5},{5,4},{6,7},{7,6},{8,9},{9,8},{10,11... | collective-permute-start | bytes 589832 | tf_op jit(solution)/shard_map/ppermute | solution.py:16
  107.4 8.5 %copy-start.1 = (bf16[1536,768]{1,0:T(8,128)(2,1)S(1)}, bf16[1536,768]{1,0:T(8,128)(2,1)}, u32[]{:S(2)}) copy-start(bf16[1536,768]{1,0:T(8,128)(2,1)} %param.16) | copy-start | bytes 7077892
where the time goes:
time: 117 us; the launch traced here: 116 us
  matrix products  43.3 us (37%)
  waiting for transfers between devices  23.3 us (20%)
  starting transfers between devices  16.6 us (14%)
  blocking collectives  13.5 us (12%)
  other arithmetic  10.5 us (9%)
  local copies, waits for them, and re-layouts  7.47 us (6%)
  between operations  1.23 us (1%)
    dot_general x22, matrix products, dot(): return lax.dot_general(a, b, (contract, batch), preferred_element_type=F32)  42.2 us
    all_to_all x3, waiting for transfers between devices, exchange(): lax.all_to_all(values, 'exp', split_axis=0, concat_axis=0, tiled=True)  19.7 us
    all_to_all x3, starting transfers between devices, exchange(): lax.all_to_all(values, 'exp', split_axis=0, concat_axis=0, tiled=True)  15.8 us
    all_to_all x1, blocking collectives, exchange(): lax.all_to_all(values, 'exp', split_axis=0, concat_axis=0, tiled=True)  13.5 us
    convert_element_type x1, other arithmetic, local(): (grad_hidden * pre_up * sigma * (1.0 + pre_gate * (1.0 - sigma))).astype(...  4.68 us
    unnamed x55, local copies, waits for them, and re-layouts  4.33 us
    ppermute x6, waiting for transfers between devices, other_core(): return lax.ppermute(values, 'rep', [(0, 1), (1, 0)])  3.63 us
  transfers between devices with their start and end apart: 9, of which 4 were waited for; matrix products, arithmetic and copies ran while one was open for 35% of the time, Pallas kernels for 0%

commit v1 on v0

v1 whole, which is shorter than its diff:
```python
import functools

import jax
import jax.numpy as jnp
from jax import lax
from jax.experimental import pallas as pl
from jax.experimental.pallas import tpu as pltpu
from jax.sharding import PartitionSpec as P

CAP = 40
LANES = 128
GROUP = 16
F32 = jnp.float32
BF16 = jnp.bfloat16
MIB = 1024 * 1024


def dot(a, b, contract, batch=((), ())):
    return lax.dot_general(a, b, (contract, batch), preferred_element_type=F32)


def mm(a, b):
    return dot(a, b, ((1,), (0,)))


def mm_t(a, b):
    return dot(a, b, ((1,), (1,)))


def t_mm(a, b):
    return dot(a, b, ((0,), (0,)))


def call(kernel, flops, moved, mib=12, **kw):
    return pl.pallas_call(
        kernel,
        compiler_params=pltpu.CompilerParams(vmem_limit_bytes=mib * MIB),
        cost_estimate=pl.CostEstimate(flops=flops, bytes_accessed=moved, transcendentals=0),
        **kw,
    )


def whole(shape):
    return pl.BlockSpec(shape, lambda *_: (0,) * len(shape))


def rows(count, columns, at=0):
    return pl.BlockSpec((count, columns), lambda g, *_: (g, at))


def shape_of(shape, dtype):
    return jax.ShapeDtypeStruct(shape, dtype)


def lane_column(shape, width):
    return lax.broadcasted_iota(jnp.int32, shape, 1) % width


def shifted(window, shift, start, count):
    size = window.shape[1]
    return pltpu.roll(window, (-shift) % size, 1)[:, start : start + count]


def other_core(values):
    return lax.ppermute(values, "rep", [(0, 1), (1, 0)])


def other_shard(values):
    return lax.ppermute(values, "exp", [(i, i ^ 1) for i in range(lax.axis_size("exp"))])


def exchange(values):
    count = lax.axis_size("exp")
    shards = count // values.shape[0]
    groups = None
    if shards > 1:
        groups = [[s + shards * e for e in range(values.shape[0])] for s in range(shards)]
    return lax.all_to_all(
        values, "exp", split_axis=0, concat_axis=0, tiled=True, axis_index_groups=groups
    )


def hbm():
    return pl.BlockSpec(memory_space=pl.ANY)


def vmem():
    return pl.BlockSpec(memory_space=pltpu.VMEM)


def fast(shape, dtype):
    return pltpu.VMEM(shape, dtype)


def near(values):
    return pltpu.with_memory_space_constraint(values, pltpu.VMEM)


def far_off(values):
    return pltpu.with_memory_space_constraint(values, pltpu.HBM)


def kernel_call(kernel, flops, moved, operands, outs, name, mib=12, place=None, steps=1, scratch=(), specs=None, out_specs=None):
    specs = specs or [vmem() for _ in operands]
    out_specs = out_specs or [vmem() for _ in outs]
    return call(
        kernel,
        flops,
        moved,
        mib,
        grid_spec=pltpu.PrefetchScalarGridSpec(
            num_scalar_prefetch=0 if place is None else 1,
            grid=(steps,),
            in_specs=specs,
            out_specs=out_specs,
            scratch_shapes=list(scratch),
        ),
        out_shape=outs,
        name=name,
    )(*(() if place is None else (place,)), *operands)


def tiles_of(columns):
    return -(-columns // LANES)


def stacked(values):
    columns = values.shape[1]
    spare = tiles_of(columns) * LANES - columns
    if spare:
        values = jnp.concatenate([values, jnp.zeros((values.shape[0], spare), F32)], axis=1)
    parts = [values[:, k * LANES : (k + 1) * LANES] for k in range(tiles_of(columns))]
    return jnp.concatenate(parts, axis=0)


def pack_kernel(shards, half, place_ref, latent_ref, routes_ref, cot_ref, out_ref, taken_ref, here_ref):
    rows_here, channels, width = latent_ref.shape
    tok = rows_here * width
    experts = out_ref.shape[0] // shards
    cells = jnp.concatenate([latent_ref[r].astype(F32) for r in range(rows_here)], axis=1)
    routes = routes_ref[...].astype(F32)
    payload = jnp.concatenate([cells, routes], axis=0)
    cot = cot_ref[...]
    if cot.shape[1] != half:
        cot = jnp.where(place_ref[2] == 0, cot[:, :half], cot[:, half:])
    here_ref[...] = cot
    expert = lax.broadcasted_iota(jnp.int32, (experts, tok), 0).astype(F32)
    named = jnp.where((expert == routes[0:1]) | (expert == routes[1:2]), 1.0, 0.0)
    first = lax.broadcasted_iota(jnp.int32, (tok, tok), 0)
    second = lax.broadcasted_iota(jnp.int32, (tok, tok), 1)
    before = jnp.where(first <= second, 1.0, 0.0).astype(BF16)
    at = mm(named.astype(BF16), before) - 1.0
    slot = lax.broadcasted_iota(jnp.int32, (CAP, tok), 0).astype(F32)
    sel = [
        jnp.where((at[e : e + 1] == slot) & (named[e : e + 1] > 0.0), 1.0, 0.0)
        for e in range(experts)
    ]
    cots = mm(jnp.concatenate(sel, axis=0).astype(BF16), cot)
    taken_ref[...] = jnp.concatenate([one for one in sel for _ in range(shards)], axis=0).astype(BF16)
    for e in range(experts):
        slots = stacked(cots[e * CAP : (e + 1) * CAP])
        packed = jnp.concatenate([slots, payload], axis=0).astype(BF16)
        for n in range(shards):
            out_ref[e * shards + n] = packed


def pack(place, latent, routes_t, cot, experts, shards, half):
    rows_here, channels, width = latent.shape
    top, tok = routes_t.shape
    blocks = experts * shards
    depth = tiles_of(half) * CAP + channels + top
    operands = [latent, routes_t, cot]
    return kernel_call(
        functools.partial(pack_kernel, shards, half),
        2 * blocks * CAP * tok * half,
        4 * blocks * depth * LANES,
        [far_off(a) for a in operands],
        [
            shape_of((blocks, depth, LANES), BF16),
            pltpu.HBM((blocks * CAP, tok), BF16),
            pltpu.HBM((tok, half), BF16),
        ],
        "pack",
        place=place,
        specs=[whole(a.shape) for a in operands],
        out_specs=[
            whole((blocks, depth, LANES)),
            whole((blocks * CAP, tok)),
            whole((tok, half)),
        ],
    )


def unpacked(ref, columns):
    tiles = tiles_of(columns)
    blocks = ref.shape[0]
    held = [ref[b, : tiles * CAP, :].astype(F32) for b in range(blocks)]
    parts = [
        jnp.concatenate([one[k * CAP : (k + 1) * CAP] for one in held], axis=0)
        for k in range(tiles)
    ]
    return jnp.concatenate(parts, axis=1)[:, :columns]


def unpack_kernel(packed_ref, cot_ref, image_ref):
    cot_ref[...] = unpacked(packed_ref, cot_ref.shape[1]).astype(BF16)
    top = packed_ref.shape[1] - image_ref.shape[1]
    for b in range(packed_ref.shape[0]):
        image_ref[b] = packed_ref[b, top:, :]


def unpack(packed, half, lines):
    blocks, _, tok = packed.shape
    return kernel_call(
        unpack_kernel,
        0,
        4 * packed.size,
        [near(packed)],
        [fast((blocks * CAP, half), BF16), fast((blocks, lines, tok), BF16)],
        "unpack",
    )


def weave_kernel(place_ref, same_ref, other_ref, after_ref, out_ref):
    even = (place_ref[1] & 1) == 0
    for e in range(same_ref.shape[0]):
        same, other = same_ref[e], other_ref[e]
        out_ref[2 * e] = jnp.where(even, same, other)
        out_ref[2 * e + 1] = jnp.where(even, other, same)


def weave(place, same, other, after):
    shape = (2 * same.shape[0],) + same.shape[1:]
    return kernel_call(
        weave_kernel,
        0,
        8 * same.size,
        [near(same), near(other), near(after)],
        [fast(shape, same.dtype)],
        "weave",
        place=place,
    )[0]


def sum_kernel(a_ref, b_ref, out_ref):
    out_ref[...] = (a_ref[...].astype(F32) + b_ref[...].astype(F32)).astype(out_ref.dtype)


def add_up(a, b):
    return kernel_call(
        sum_kernel, a.size, 6 * a.size, [near(a), near(b)], [fast(a.shape, a.dtype)], "add_up"
    )[0]


def pack_back_kernel(paired, place_ref, a_ref, b_ref, c_ref, terms_ref, out_ref):
    total = a_ref[...].astype(F32) + b_ref[...].astype(F32)
    if paired:
        total = total + c_ref[...].astype(F32)
    side = place_ref[1] & 1
    for b in range(out_ref.shape[0]):
        slots = stacked(total[b * CAP : (b + 1) * CAP])
        if paired:
            terms = [terms_ref[2 * b + side], terms_ref[2 * b + 1 - side]]
        else:
            terms = [terms_ref[b]]
        out_ref[b] = jnp.concatenate([slots] + terms, axis=0).astype(BF16)


def pack_back(place, a, b, c, terms, paired):
    blocks, channels, tok = terms.shape
    depth = tiles_of(a.shape[1]) * CAP + channels
    if paired:
        blocks, depth = blocks // 2, depth + channels
    return kernel_call(
        functools.partial(pack_back_kernel, paired),
        a.size,
        8 * a.size,
        [near(a), near(b), near(c), near(terms)],
        [shape_of((blocks, depth, LANES), BF16)],
        "pack_back",
        place=place,
    )[0]


PIECES = 4


def pieces(source, target, sem, at=0):
    deep = source.shape[0] // PIECES
    bands = [pl.ds(k * deep, deep) for k in range(PIECES)]
    return [
        pltpu.make_async_copy(source.at[band, :], target.at[band, :], sem.at[at + k])
        for k, band in enumerate(bands)
    ]


def far_kernel(place_ref, gate_ref, up_ref, down_ref, gate_out, up_out, down_out, sem):
    size = gate_out.shape[1]
    at = pl.multiple_of((1 - place_ref[2]) * size, LANES)
    copies = (
        pieces(gate_ref.at[:, pl.ds(at, size)], gate_out, sem)
        + pieces(up_ref.at[:, pl.ds(at, size)], up_out, sem, PIECES)
        + pieces(down_ref.at[pl.ds(at, size), :], down_out, sem, 2 * PIECES)
    )
    for copy in copies:
        copy.start()
    for copy in copies:
        copy.wait()


def far_weights(place, gate, up, down):
    half, hid = gate.shape
    size = hid // 2
    return kernel_call(
        far_kernel,
        0,
        LANES,
        [far_off(gate), far_off(up), far_off(down)],
        [fast((half, size), BF16), fast((half, size), BF16), fast((size, half), BF16)],
        "far_weights",
        place=place,
        specs=[hbm()] * 3,
        scratch=[pltpu.SemaphoreType.DMA((3 * PIECES,))],
    )


def cuts(lengths):
    start, out = 0, []
    for n in lengths:
        out.append((start, n))
        start += n
    return out


def weights_kernel(parts, experts, place_ref, *refs):
    weights = refs[: 3 * parts]
    stem_in, gain_in, router_in = refs[3 * parts : 3 * parts + 3]
    inner, outer, stem, gain, sem = refs[3 * parts + 3 :]
    gates, ups, downs = weights[:parts], weights[parts : 2 * parts], weights[2 * parts :]
    size = outer.shape[0]
    copies = []

    def copy(source, target):
        copies.extend(pieces(source, target, sem, len(copies)))

    for n, refs_of in enumerate((gates, ups)):
        for ref, (a, depth) in zip(refs_of, cuts([r.shape[0] for r in refs_of])):
            if ref.shape[1] != size:
                ref = ref.at[:, pl.ds(pl.multiple_of(place_ref[2] * size, LANES), size)]
            copy(ref, inner.at[pl.ds(a, depth), pl.ds(n * size, size)])
    for ref, (a, depth) in zip(downs, cuts([r.shape[1] for r in downs])):
        if ref.shape[0] != size:
            ref = ref.at[pl.ds(pl.multiple_of(place_ref[2] * size, LANES), size), :]
        copy(ref, outer.at[:, pl.ds(a, depth)])
    for one in copies:
        one.start()
    wide = router_in[...].astype(F32)
    model = wide.shape[0]
    blank = jnp.zeros((model, LANES - 2 * experts), F32)
    wide = jnp.concatenate([wide, wide, blank], axis=1)
    values, gains = stem_in[...], gain_in[...]
    if parts == 2:
        half = model // 2
        first = place_ref[2] == 0
        wide = jnp.where(first, wide, jnp.concatenate([wide[half:], wide[:half]], axis=0))
        turned = jnp.concatenate([values[:, half:], values[:, :half]], axis=1)
        values = jnp.where(first, values, turned)
        turned = jnp.concatenate([gains[:, half:], gains[:, :half]], axis=1)
        gains = jnp.where(first, gains, turned)
    stem[...] = values
    gain[...] = gains
    inner[:, 2 * size :] = wide.astype(BF16)
    for one in copies:
        one.wait()


def gather_weights(place, stem, gain, router, gate_parts, up_parts, down_parts):
    parts = len(gate_parts)
    model, experts = router.shape
    size = down_parts[-1].shape[0]
    weights = [far_off(w) for p in (gate_parts, up_parts, down_parts) for w in p]
    small = [far_off(stem), far_off(gain), far_off(router)]
    return kernel_call(
        functools.partial(weights_kernel, parts, experts),
        100_000_000_000,
        12 * model * size,
        weights + small,
        [
            fast((model, 2 * size + LANES), BF16),
            fast((size, model), BF16),
            fast(stem.shape, BF16),
            fast(gain.shape, F32),
        ],
        "gather_weights",
        place=place,
        specs=[hbm()] * (3 * parts) + [whole(a.shape) for a in small],
        scratch=[pltpu.SemaphoreType.DMA((3 * parts * PIECES,))],
    )


def join_kernel(place_ref, own_ref, away_ref, a_ref, b_ref, out_ref, latent_ref):
    half = own_ref.shape[1]
    first = place_ref[2] == 0
    own, away = own_ref[...], away_ref[...]
    out_ref[:, :half] = jnp.where(first, own, away)
    out_ref[:, half:] = jnp.where(first, away, own)
    total = a_ref[...] + b_ref[...]
    width = latent_ref.shape[2]
    for r in range(latent_ref.shape[0]):
        latent_ref[r] = total[:, r * width : (r + 1) * width]


def join(place, own, away, a, b, rows_here):
    count, half = own.shape
    channels, tok = a.shape
    return kernel_call(
        join_kernel,
        0,
        8 * count * half,
        [near(own), near(away), near(a), near(b)],
        [
            shape_of((count, 2 * half), BF16),
            shape_of((rows_here, channels, tok // rows_here), F32),
        ],
        "join",
        place=place,
    )


def pair_selection(named):
    lanes = named.shape[1]
    tok = lanes // 2
    first = lax.broadcasted_iota(jnp.int32, (lanes, lanes), 0)
    second = lax.broadcasted_iota(jnp.int32, (lanes, lanes), 1)
    before = ((first <= second) & (first // tok == second // tok)).astype(F32).astype(BF16)
    wide = jnp.broadcast_to(named, (8, lanes)).astype(BF16)
    place = mm(wide, before)[:1]
    lane = lax.broadcasted_iota(jnp.int32, (1, lanes), 1)
    place = place - 1.0 + jnp.where(lane >= tok, float(CAP), 0.0)
    slot = lax.broadcasted_iota(jnp.int32, (2 * CAP, lanes), 0).astype(F32)
    return jnp.where((place == slot) & (named > 0.0), 1.0, 0.0)


def pair_patches(image_ref, top, first, width, channels):
    blocks = image_ref.shape[0]
    before = image_ref[jnp.maximum(first - 1, 0), top : top + channels, :].astype(F32)
    after = image_ref[jnp.minimum(first + 2, blocks - 1), top : top + channels, :].astype(F32)
    window = jnp.concatenate(
        [
            jnp.where(first > 0, before, 0.0),
            image_ref[first, top : top + channels, :].astype(F32),
            image_ref[first + 1, top : top + channels, :].astype(F32),
            jnp.where(first + 2 < blocks, after, 0.0),
        ],
        axis=1,
    )
    tok = image_ref.shape[2]
    column = lane_column((channels, 2 * tok), width)
    pieces = []
    for i in range(3):
        for j in range(3):
            piece = shifted(window, (i - 1) * width + j - 1, tok, 2 * tok)
            source = column + (j - 1)
            pieces.append(jnp.where((source >= 0) & (source < width), piece, 0.0))
    return jnp.concatenate(pieces, axis=0)


def by_side(pairs, even):
    same = [jnp.where(even, p[:CAP], p[CAP:]) for p in pairs]
    other = [jnp.where(even, p[CAP:], p[:CAP]) for p in pairs]
    return same + other


def forward_kernel(
    paired, width, experts, outs, place_ref, image_ref, stem_ref, gain_ref, inner, outer,
    saved_ref, own_out, normed_ref, value_ref, meta_ref, coef_ref, sel_ref, pg_ref, pu_ref, *refs,
):
    out_refs, (own_ref, save_sem) = refs[:-2], refs[-2:]
    step = pl.program_id(0)
    size = outer.shape[0]
    chunk = GROUP * CAP
    here = pl.ds(pl.multiple_of(step * chunk, chunk), chunk)
    top = 0
    channels = image_ref.shape[1] - 2
    mine = place_ref[0].astype(F32)
    even = (place_ref[1] & 1) == 0
    taken, others = [], []
    for q in range(GROUP // 2):
        first = step * GROUP + 2 * q
        lines = [image_ref[first + n, top + channels :, :].astype(F32) for n in range(2)]
        named_by = [jnp.concatenate([line[k : k + 1] for line in lines], axis=1) for k in range(2)]
        named = jnp.where((named_by[0] == mine) | (named_by[1] == mine), 1.0, 0.0)
        sel = pair_selection(named)
        sel_ref[step * (GROUP // 2) + q] = sel.astype(BF16)
        other = named_by[0] + named_by[1] - mine
        others.append(jnp.sum(sel * other, axis=1, keepdims=True))
        patches = pair_patches(image_ref, top, first, width, channels)
        taken.append(mm_t(sel.astype(BF16), patches.astype(BF16)))
    if paired:
        taken, others = by_side(taken, even), by_side(others, even)
    patches = jnp.concatenate(taken, axis=0).astype(BF16)
    other = jnp.concatenate(others, axis=0)
    stem = mm(patches, stem_ref[...]).astype(BF16)
    value_ref[here, :] = stem
    value = stem.astype(F32)
    scale = lax.rsqrt(jnp.mean(value * value, axis=-1, keepdims=True) + 1e-06)
    normed = (value * scale * gain_ref[...]).astype(BF16)
    normed_ref[...] = normed
    save = pltpu.make_async_copy(normed_ref, saved_ref.at[here, :], save_sem.at[0])
    save.start()
    own_save = pltpu.make_async_copy(own_ref, own_out, save_sem.at[1])

    @pl.when(step == 0)
    def _():
        me = place_ref[1]
        first = me // 2 * 2
        tok = image_ref.shape[2]
        own = pair_patches(image_ref, top, first, width, channels)
        own = jnp.where(me == first, own[:, :tok], own[:, tok:]).astype(BF16)
        own_ref[...] = t_mm(own, stem_ref[:, : own_ref.shape[1]]).astype(BF16)
        own_save.start()

    logits = mm(normed, inner[:, 2 * size :])
    lane = lax.broadcasted_iota(jnp.int32, logits.shape, 1)
    again = jnp.where(lane >= experts, lane - experts, lane).astype(F32)
    lane = lane.astype(F32)
    sig_mine = jax.nn.sigmoid(jnp.sum(jnp.where(lane == mine, logits, 0.0), axis=1, keepdims=True))
    sig_other = jax.nn.sigmoid(jnp.sum(jnp.where(lane == other, logits, 0.0), axis=1, keepdims=True))
    gate = sig_mine / (sig_mine + sig_other)
    rest = sig_other / (sig_mine + sig_other)
    both = gate * rest
    coef_ref[here, :] = jnp.where(again == mine, both * (1.0 - sig_mine), 0.0) - jnp.where(
        again == other, both * (1.0 - sig_other), 0.0
    )
    meta_ref[here, :] = jnp.where(lane == 0.0, gate, scale)
    pre_gate = mm(normed, inner[:, :size])
    pre_up = mm(normed, inner[:, size : 2 * size])
    pg_ref[here, :] = pre_gate.astype(BF16)
    pu_ref[here, :] = pre_up.astype(BF16)
    hidden = (pre_gate * jax.nn.sigmoid(pre_gate) * pre_up).astype(BF16)
    part, at = None, None
    for ref, (a, n, b, m) in zip(out_refs, outs):
        if (b, m) != at:
            part, at = gate * mm(hidden, outer[:, b : b + m]), (b, m)
        if n == chunk:
            ref[here, :] = part.astype(BF16)
        else:
            ref[...] = part[a : a + n].astype(BF16)
    save.wait()

    @pl.when(step == 0)
    def _():
        own_save.wait()


def forward(place, image, stem, gain, inner, outer, half, outs, paired, width, experts):
    blocks, _, tok = image.shape
    slots, chunk = blocks * CAP, GROUP * CAP
    model, size = stem.shape[1], outer.shape[0]
    return kernel_call(
        functools.partial(forward_kernel, paired, width, experts, outs),
        2 * slots * model * size * 4,
        slots * (6 * model + 6 * size) + 6 * model * size,
        [near(a) for a in (image, stem, gain, inner, outer)],
        [
            pltpu.HBM((slots, model), BF16),
            pltpu.HBM((tok, half), BF16),
            fast((chunk, model), BF16),
            fast((slots, model), BF16),
            fast((slots, LANES), F32),
            fast((slots, LANES), F32),
            fast((blocks // 2, 2 * CAP, 2 * tok), BF16),
            fast((slots, size), BF16),
            fast((slots, size), BF16),
        ]
        + [fast((slots if n == chunk else n, m), BF16) for _, n, _, m in outs],
        "forward",
        mib=18,
        place=place,
        steps=blocks // GROUP,
        out_specs=[hbm()] * 2 + [vmem()] * (7 + len(outs)),
        scratch=[pltpu.VMEM((tok, half), BF16), pltpu.SemaphoreType.DMA((2,))],
    )


def backward_kernel(
    parts, bands, experts, stem_ref, gain_ref, inner, outer, value_ref, meta_ref, coef_ref, pg_ref, pu_ref,
    *refs,
):
    cot_refs, refs = refs[: parts * bands], refs[parts * bands :]
    saved, refs = refs[: 3 + parts], refs[3 + parts :]
    proj_ref, ggp_ref, gup_ref, hg_ref, sem = refs
    step = pl.program_id(0)
    model = stem_ref.shape[1]
    chunk = GROUP * CAP
    here = pl.ds(pl.multiple_of(step * chunk, chunk), chunk)
    sources = [ggp_ref, gup_ref, hg_ref]
    targets = [ref.at[here, :] for ref in saved[:3]]
    for n, ref in enumerate(cot_refs):
        if bands == 1:
            sources.append(ref.at[here, :])
            targets.append(saved[3 + n].at[here, :])
        else:
            deep = ref.shape[0]
            sources.append(ref)
            targets.append(saved[3 + n // bands].at[pl.ds(n % bands * deep, deep), :])
    saves = [
        pltpu.make_async_copy(a, b, sem.at[n]) for n, (a, b) in enumerate(zip(sources, targets))
    ]
    for save in saves[3:]:
        save.start()
    gate = meta_ref[here, 0:1]
    scale = meta_ref[here, 1:2]
    raw = 0.0
    for k, (a, n) in enumerate(cuts([r.shape[1] for r in cot_refs[::bands]])):
        if bands == 1:
            cot = cot_refs[k][here, :]
        else:
            cot = jnp.concatenate([r[...] for r in cot_refs[k * bands : (k + 1) * bands]], axis=0)
        raw = raw + mm_t(cot, outer[:, a : a + n])
    pre_gate = pg_ref[here, :].astype(F32)
    pre_up = pu_ref[here, :].astype(F32)
    sigma = jax.nn.sigmoid(pre_gate)
    silu = pre_gate * sigma
    hidden = silu * pre_up
    grad_gates = jnp.sum(raw * hidden, axis=1, keepdims=True)
    hg_ref[...] = (gate * hidden).astype(BF16)
    grad_hidden = gate * raw
    ggp = (grad_hidden * pre_up * sigma * (1.0 + pre_gate - silu)).astype(BF16)
    gup = (grad_hidden * silu).astype(BF16)
    ggp_ref[...] = ggp
    gup_ref[...] = gup
    for save in saves[:3]:
        save.start()
    grad_logits = grad_gates * coef_ref[here, :]
    high = grad_logits.astype(BF16)
    low = (grad_logits - high.astype(F32)).astype(BF16)
    lane = lax.broadcasted_iota(jnp.int32, grad_logits.shape, 1)
    mix = jnp.where(lane < experts, high.astype(F32), low.astype(F32)).astype(BF16)
    back = mm_t(jnp.concatenate([ggp, gup, mix], axis=1), inner[...]) * gain_ref[...]
    value = value_ref[here, :].astype(F32)
    along = jnp.sum(back * value, axis=1, keepdims=True) * (scale * scale * scale) / model
    grad = (scale * back - along * value).astype(BF16)
    proj_ref[here, :] = mm_t(grad, stem_ref[...]).astype(BF16)
    for save in saves:
        save.wait()


def backward(stem, gain, inner, outer, acts, cots, experts):
    slots, model = acts[0].shape
    size, chunk = outer.shape[0], GROUP * CAP
    taps = stem.shape[0]
    parts, bands = len(cots), len(cots[0])
    operands = [stem, gain, inner, outer] + list(acts) + [c for part in cots for c in part]
    return kernel_call(
        functools.partial(backward_kernel, parts, bands, experts),
        2 * slots * model * size * 4,
        slots * (4 * model + 12 * size) + 6 * model * size,
        [near(a) for a in operands],
        [pltpu.HBM((slots, size), BF16)] * 3
        + [pltpu.HBM((slots, part[0].shape[1]), BF16) for part in cots]
        + [fast((slots, taps), BF16)],
        "backward",
        mib=20,
        steps=slots // chunk,
        out_specs=[hbm()] * (3 + parts) + [vmem()],
        scratch=[pltpu.VMEM((chunk, size), BF16)] * 3
        + [pltpu.SemaphoreType.DMA((3 + parts * bands,))],
    )


def image_kernel(paired, width, place_ref, proj_ref, sel_ref, stem_ref, cot_ref, out_ref, terms):
    pairs = sel_ref.shape[0]
    tok = cot_ref.shape[0]
    channels = out_ref.shape[1]
    count = 2 * pairs * tok
    own = mm_t(stem_ref[:, : cot_ref.shape[1]], cot_ref[...])
    me = place_ref[1]
    even = (me & 1) == 0
    proj = proj_ref[...].astype(F32)
    for q in range(pairs):
        if paired:
            same = proj[CAP * q : CAP * (q + 1)]
            other = proj[CAP * (pairs + q) : CAP * (pairs + q + 1)]
            both = [jnp.where(even, same, other), jnp.where(even, other, same)]
            pair = jnp.concatenate(both, axis=0)
        else:
            pair = proj[2 * CAP * q : 2 * CAP * (q + 1)]
        block = t_mm(pair.astype(BF16), sel_ref[q])
        terms[:, 2 * q * tok : (2 * q + 1) * tok] = block[:, :tok] + jnp.where(2 * q == me, own, 0.0)
        terms[:, (2 * q + 1) * tok : (2 * q + 2) * tok] = block[:, tok:] + jnp.where(
            2 * q + 1 == me, own, 0.0
        )
    lane = lax.broadcasted_iota(jnp.int32, (channels, count), 1)
    total = jnp.zeros((channels, count), F32)
    for i in range(3):
        for j in range(3):
            k = (3 * i + j) * channels
            shift = (i - 1) * width + j - 1
            piece = pltpu.roll(terms[k : k + channels, :], shift % count, 1)
            column = lane % width + (1 - j)
            token = lane - shift
            keep = (column >= 0) & (column < width) & (token >= 0) & (token < count)
            total = total + jnp.where(keep, piece, 0.0)
    for b in range(2 * pairs):
        out_ref[b] = total[:, b * tok : (b + 1) * tok]


def to_image(place, proj, sel, stem, cot, paired, width, channels):
    pairs = sel.shape[0]
    blocks, tok = 2 * pairs, cot.shape[0]
    taps, half = stem.shape[0], cot.shape[1]
    return kernel_call(
        functools.partial(image_kernel, paired, width),
        2 * proj.shape[0] * 2 * tok * taps,
        4 * taps * blocks * tok,
        [near(a) for a in (proj, sel, stem, cot)],
        [fast((blocks, channels, tok), F32)],
        "to_image",
        place=place,
        scratch=[pltpu.VMEM((taps, blocks * tok), F32)],
    )[0]


def far_grads_kernel(normed, ggp, gup, hg, near_cot, cot, after, gate_out, up_out, down_out, *refs):
    near_v, ggp_v, gup_v, hg_v, near_cot_v, far_v, cot_v, sem = refs
    half = cot.shape[1]
    sources = (normed.at[:, pl.ds(half, half)], ggp, gup, hg, cot, normed.at[:, pl.ds(0, half)], near_cot)
    targets = (far_v, ggp_v, gup_v, hg_v, cot_v, near_v, near_cot_v)
    loads = [pltpu.make_async_copy(a, b, sem.at[n]) for n, (a, b) in enumerate(zip(sources, targets))]
    for load in loads:
        load.start()
    for load in loads[:2]:
        load.wait()
    gate_out[...] = t_mm(far_v[...], ggp_v[...]).astype(BF16)
    loads[2].wait()
    up_out[...] = t_mm(far_v[...], gup_v[...]).astype(BF16)
    loads[3].wait()
    loads[4].wait()
    down_out[...] = t_mm(hg_v[...], cot_v[...]).astype(BF16)
    loads[5].wait()
    loads[6].wait()


def far_grads(normed, ggp, gup, hg, near_cot, cot, after):
    slots, size = ggp.shape
    half = cot.shape[1]
    held = [(slots, half), (slots, size), (slots, size), (slots, size), (slots, half)]
    return kernel_call(
        far_grads_kernel,
        0,
        LANES,
        [far_off(a) for a in (normed, ggp, gup, hg, near_cot, cot)] + [after],
        [fast((half, size), BF16)] * 2
        + [fast((size, half), BF16)]
        + [fast(shape, BF16) for shape in held],
        "far_grads",
        specs=[hbm()] * 7,
        scratch=[
            pltpu.VMEM((slots, half), BF16),
            pltpu.VMEM((slots, half), BF16),
            pltpu.SemaphoreType.DMA((7,)),
        ],
    )


def near_grads_kernel(
    place_ref, normed, ggp, gup, hg, cot, gate_out, up_out, down_out, done_ref, own, own_sem
):
    size = ggp.shape[1]
    here = pl.multiple_of(place_ref[2] * size, LANES)
    places = (
        gate_out.at[:, pl.ds(here, size)],
        up_out.at[:, pl.ds(here, size)],
        down_out.at[pl.ds(here, size), :],
    )
    results = [pieces(own.at[n], a, own_sem, n * PIECES) for n, a in enumerate(places)]
    done_ref[...] = jnp.zeros(done_ref.shape, F32)
    for n, (left, right) in enumerate(((normed, ggp), (normed, gup), (hg, cot))):
        own[n] = t_mm(left[...], right[...])
        for copy in results[n]:
            copy.start()
    for copy in results[0] + results[1] + results[2]:
        copy.wait()


def near_grads(place, normed, ggp, gup, hg, cot):
    slots, size = ggp.shape
    half = cot.shape[1]
    return kernel_call(
        near_grads_kernel,
        100_000_000_000,
        LANES,
        [near(a) for a in (normed, ggp, gup, hg, cot)],
        [pltpu.HBM((half, 2 * size), F32)] * 2
        + [pltpu.HBM((2 * size, half), F32), fast((8, LANES), F32)],
        "near_grads",
        mib=14,
        place=place,
        out_specs=[hbm()] * 3 + [vmem()],
        scratch=[pltpu.VMEM((3, half, size), F32), pltpu.SemaphoreType.DMA((3 * PIECES,))],
    )


def fill_kernel(
    place_ref, gate_in, up_in, down_in, gate_old, up_old, down_old, gate_out, up_out, down_out, wide, sem
):
    size = gate_in.shape[1]
    there = pl.multiple_of((1 - place_ref[2]) * size, LANES)
    places = (
        gate_out.at[:, pl.ds(there, size)],
        up_out.at[:, pl.ds(there, size)],
        down_out.at[pl.ds(there, size), :],
    )
    results = [pieces(wide.at[n], a, sem, n * PIECES) for n, a in enumerate(places)]
    deep = wide.shape[1] // PIECES
    for n, away in enumerate((gate_in, up_in, down_in)):
        for k in range(PIECES):
            wide[n, k * deep : (k + 1) * deep] = away[k * deep : (k + 1) * deep].astype(F32)
            results[n][k].start()
    for copy in results[0] + results[1] + results[2]:
        copy.wait()


def fill(place, away, grads):
    size = away[0].shape[1]
    return pl.pallas_call(
        fill_kernel,
        compiler_params=pltpu.CompilerParams(vmem_limit_bytes=12 * MIB),
        cost_estimate=pl.CostEstimate(
            flops=0, bytes_accessed=LANES, transcendentals=0
        ),
        grid_spec=pltpu.PrefetchScalarGridSpec(
            num_scalar_prefetch=1,
            grid=(1,),
            in_specs=[vmem()] * 3 + [hbm()] * 3,
            out_specs=[hbm()] * 3,
            scratch_shapes=[
                pltpu.VMEM((3,) + away[0].shape, F32),
                pltpu.SemaphoreType.DMA((3 * PIECES,)),
            ],
        ),
        out_shape=[pltpu.HBM(g.shape, F32) for g in grads],
        input_output_aliases={4: 0, 5: 1, 6: 2},
        name="fill",
    )(place, *[near(a) for a in away], *grads)


def weight_grads(place, column, size, normed, ggp, gup, hg, cots, after):
    if lax.axis_size("rep") == 2:
        *far, a, b, c, d, e = far_grads(normed, ggp, gup, hg, cots[0], cots[1], after)
        away = [other_core(f) for f in far]
        *grads, done = near_grads(place, a, b, c, d, e)
        return fill(place, away, grads), done
    grads = []
    for g in (ggp[:, :size], gup[:, :size]):
        term = jnp.roll(t_mm(normed, g).astype(BF16), column, 0)
        grads.append(lax.all_to_all(term, "rep", split_axis=0, concat_axis=1, tiled=True))
    term = jnp.roll(t_mm(hg[:, :size], cots[0]).astype(BF16), column, 1)
    grads.append(lax.all_to_all(term, "rep", split_axis=1, concat_axis=0, tiled=True))
    return [g.astype(F32) for g in grads], jnp.zeros((8, LANES), F32)


def mixed_kernel(stem_ref, taken_ref, back_ref, after_ref, out_ref, *terms_refs):
    half = out_ref.shape[1]
    back = unpacked(back_ref, half).astype(BF16)
    total = stem_ref[...].astype(F32) + t_mm(taken_ref[...], back)
    out_ref[...] = total.astype(BF16)
    top = tiles_of(half) * CAP
    terms = back_ref[0, top:, :].astype(F32)
    for b in range(1, back_ref.shape[0]):
        terms = terms + back_ref[b, top:, :].astype(F32)
    for n, ref in enumerate(terms_refs):
        ref[...] = terms[n * ref.shape[0] : (n + 1) * ref.shape[0]]


def mix(stem, taken, back, after, channels):
    tok, half = stem.shape
    sides = (back.shape[1] - tiles_of(half) * CAP) // channels
    return kernel_call(
        mixed_kernel,
        2 * taken.shape[0] * tok * half,
        2 * back.size,
        [near(a) for a in (stem, taken, back, after)],
        [fast((tok, half), BF16)] + [fast((channels, tok), F32)] * sides,
        "mixed",
    )


def local(
    latent,
    stem_weight,
    norm_gain,
    router_weight,
    routes,
    gate_weight,
    up_weight,
    down_weight,
    grad_mixed,
):
    rows_here, channels, width = latent.shape
    half = gate_weight.shape[0]
    experts = router_weight.shape[1]
    tok = rows_here * width
    blocks = lax.axis_size("exp")
    cores = lax.axis_size("rep")
    shards = blocks // experts
    slots = blocks * CAP
    me = lax.axis_index("exp")
    core = lax.axis_index("rep")
    column = core * half
    place = jnp.stack([me // shards, me, core]).astype(jnp.int32)

    paired = cores == 2 and shards == 2
    given = grad_mixed
    if cores != 2:
        given = lax.dynamic_slice_in_dim(grad_mixed, column, half, 1)
    copies = 1 if paired else shards
    packed, taken, cot = pack(place, latent, routes.T, given, experts, copies, half)
    packed = exchange(packed)

    stem, gain, router = stem_weight, norm_gain[None, :], router_weight
    if cores == 2:
        far = far_weights(place, gate_weight, up_weight, down_weight)
        gate_parts, up_parts, down_parts = [
            (w, other_core(f)) for w, f in zip((gate_weight, up_weight, down_weight), far)
        ]
    else:
        turned = lax.all_to_all(gate_weight, "rep", split_axis=1, concat_axis=0, tiled=True)
        spare = -turned.shape[1] % LANES
        gate_parts = (jnp.pad(jnp.roll(turned, -column, 0), ((0, 0), (0, spare))),)
        turned = lax.all_to_all(up_weight, "rep", split_axis=1, concat_axis=0, tiled=True)
        up_parts = (jnp.pad(jnp.roll(turned, -column, 0), ((0, 0), (0, spare))),)
        turned = lax.all_to_all(down_weight, "rep", split_axis=0, concat_axis=1, tiled=True)
        down_parts = (jnp.pad(jnp.roll(turned, -column, 1), ((0, spare), (0, 0))),)
        stem = jnp.roll(stem, -column, 1)
        gain = jnp.roll(gain, -column, 1)
        router = jnp.roll(router, -column, 0)

    inner, outer, stem, gain = gather_weights(
        place, stem, gain, router, gate_parts, up_parts, down_parts
    )
    same_cot, image = unpack(packed, half, channels + 2)
    if paired:
        image = weave(place, image, other_shard(image), gain)
        cots = [same_cot, other_shard(same_cot)]
        cots = [cots, [other_core(c) for c in cots]]
        outs = [(k * slots // 2, slots // 2, n * half, half) for n in range(2) for k in range(2)]
    elif cores == 2:
        cots = [[same_cot], [other_core(same_cot)]]
        outs = [(0, GROUP * CAP, n * half, half) for n in range(2)]
    else:
        joined = lax.all_gather(same_cot, "rep", axis=1, tiled=True)
        cots = [[jnp.roll(joined, -column, 1)]]
        outs = [(0, GROUP * CAP, 0, stem.shape[1])]
    normed, own_stem, _, value, meta, coef, sel, pg, pu, *outs = forward(
        place, image, stem, gain, inner, outer, half, outs, paired, width, experts
    )
    if paired:
        over = other_shard(add_up(outs[1], other_core(outs[3])))
        own, away = outs[0], other_core(outs[2])
    elif cores == 2:
        own, away = outs[0], other_core(outs[1])
        over = own
    else:
        turned = jnp.roll(outs[0], column, 1)
        own = lax.psum_scatter(turned, "rep", scatter_dimension=1, tiled=True)
        away = over = jnp.zeros_like(own)
    acts = [value, meta, coef, pg, pu]
    ggp, gup, hg, *cots, proj = backward(stem, gain, inner, outer, acts, cots, experts)
    lat_terms = to_image(place, proj, sel, stem, cot, paired, width, channels)

    sent = pack_back(place, own, away, over, lat_terms, paired)
    back = exchange(sent)

    size = gate_weight.shape[1] // cores
    grads, done = weight_grads(place, column, size, normed, ggp, gup, hg, cots, sent)
    grad_gate, grad_up, grad_down = grads

    mixed, *lat_sums = mix(own_stem, taken, back, done, channels)
    lat_sum = lat_sums[0]
    if paired:
        lat_sum = add_up(lat_sum, other_shard(lat_sums[1]))
    if cores == 2:
        mixed, grad_latent = join(
            place, mixed, other_core(mixed), lat_sum, other_core(lat_sum), rows_here
        )
    else:
        mixed = lax.all_gather(mixed, "rep", axis=1, tiled=True)
        lat_sum = lax.psum(lat_sum, "rep")
        grad_latent = lat_sum.reshape(channels, rows_here, width).transpose(1, 0, 2)
    return (mixed, grad_latent, grad_gate, grad_up, grad_down)


def solution(mesh):
    return jax.shard_map(
        local,
        mesh=mesh,
        in_specs=(
            P("exp", None, None),
            P(),
            P(),
            P(),
            P("exp", None),
            P("rep", "exp"),
            P("rep", "exp"),
            P("exp", "rep"),
            P("exp", None),
        ),
        out_specs=(
            P("exp", None),
            P("exp", None, None),
            P("rep", "exp"),
            P("rep", "exp"),
            P("exp", "rep"),
        ),
        check_vma=False,
    )
```

time: 117 us -> 95.1 us (0.81)
  Pallas kernels: 0 us -> 51.1 us
  matrix products: 43.3 us -> 0 us
  blocking collectives: 13.5 us -> 0 us
  other arithmetic: 10.5 us -> 0.08 us
  local copies, waits for them, and re-layouts: 7.47 us -> 1.54 us
  starting transfers between devices: 16.6 us -> 18.6 us
    pallas_call x0 -> x16, Pallas kernels: none -> 51.1 us  [the longest x15 46.2 us: kernel_call(): call(kernel, flops, moved, mib, grid_spec=pltpu.PrefetchScalarGridSpec(nu...]
    dot_general x23 -> x0, matrix products: 43.3 us -> none  [the longest x22 42.2 us: dot(): return lax.dot_general(a, b, (contract, batch), preferred_element_type=F32)]
    all_to_all x1 -> x0, blocking collectives: 13.5 us -> none  [exchange(): lax.all_to_all(values, 'exp', split_axis=0, concat_axis=0, tiled=True)]
    convert_element_type x9 -> x0, other arithmetic: 6.34 us -> none  [the longest x1 4.68 us: local(): (grad_hidden * pre_up * sigma * (1.0 + pre_gate * (1.0 - sigma))).astype(...]
    all_to_all x3 -> x2, starting transfers between devices: 15.8 us -> 10.5 us  [exchange(): lax.all_to_all(values, 'exp', split_axis=0, concat_axis=0, tiled=True, ax...]
    ppermute x0 -> x4, starting transfers between devices: none -> 5.22 us  [other_shard(): lax.ppermute(values, 'exp', [(i, i ^ 1) for i in range(lax.axis_size('exp...]
    ppermute x0 -> x4, waiting for transfers between devices: none -> 4.77 us  [other_shard(): lax.ppermute(values, 'exp', [(i, i ^ 1) for i in range(lax.axis_size('exp...]
    all_to_all x3 -> x2, waiting for transfers between devices: 19.7 us -> 15.7 us  [exchange(): lax.all_to_all(values, 'exp', split_axis=0, concat_axis=0, tiled=True, ax...]
  transfers between devices with their start and end apart: 9 -> 18, of which waited for: 4 -> 6; matrix products, arithmetic and copies ran while one was open for 35% -> 2% of each run, Pallas kernels for 0% -> 43%
where the time goes in v1:
time: 95.1 us; the launch traced here: 94.7 us
  Pallas kernels  51.1 us (54%)
  waiting for transfers between devices  22.5 us (24%)
  starting transfers between devices  18.6 us (20%)
  local copies, waits for them, and re-layouts  1.54 us (2%)
  between operations  0.96 us (1%)
    pallas_call x15, Pallas kernels, kernel_call(): call(kernel, flops, moved, mib, grid_spec=pltpu.PrefetchScalarGridSpec(nu...  46.2 us
    all_to_all x2, waiting for transfers between devices, exchange(): lax.all_to_all(values, 'exp', split_axis=0, concat_axis=0, tiled=True, ax...  15.7 us
    all_to_all x2, starting transfers between devices, exchange(): lax.all_to_all(values, 'exp', split_axis=0, concat_axis=0, tiled=True, ax...  10.5 us
    ppermute x4, starting transfers between devices, other_shard(): lax.ppermute(values, 'exp', [(i, i ^ 1) for i in range(lax.axis_size('exp...  5.22 us
    pallas_call x1, Pallas kernels, fill(): pl.pallas_call(fill_kernel, compiler_params=pltpu.CompilerParams(vmem_lim...  4.86 us
    ppermute x4, waiting for transfers between devices, other_shard(): lax.ppermute(values, 'exp', [(i, i ^ 1) for i in range(lax.axis_size('exp...  4.77 us
    ppermute x12, starting transfers between devices, other_core(): return lax.ppermute(values, 'rep', [(0, 1), (1, 0)])  2.83 us
    ppermute x12, waiting for transfers between devices, other_core(): return lax.ppermute(values, 'rep', [(0, 1), (1, 0)])  2.03 us
  transfers between devices with their start and end apart: 18, of which 6 were waited for; matrix products, arithmetic and copies ran while one was open for 2% of the time, Pallas kernels for 43%

profile of v1, /device:TPU:0, one launch (start us, length us, event | category | flops | bytes accessed | tf_op | source)
XLA Modules:
  0.0 94.7 jit_solution(8289137834101180875)
XLA Ops:
  0.6 0.1 pad_add_fusion.place_ref
  0.7 0.0 copy-start.4
  0.7 0.0 copy-start.3
  0.7 3.6 %far_weights.1 = (bf16[768,768]{1,0:T(8,128)(2,1)}, bf16[768,768]{1,0:T(8,128)(2,1)S(1)}, bf16[768,768]{1,0:T(8,128)(2,1)S(1)}) custom-call(s32[3]{0:T(128)S(1)} %pad_add_fusion.place_ref, bf16[768,1536]{1,0:T(8,128)(2,1)} %refs_0_.1, bf16[768,1536]{1,0:T(8,128)(2,1)} %refs_2_.1, bf16[1536,768]{1,0:T(8,128)(2,1)} %refs_4_.1), custom_call_target="tpu_custom_call" | custom-call | bytes 128 | tf_op jit(solution)/shard_map/far_weights/pallas_call | solution.py:106
  4.3 0.5 collective-permute-start.1
  4.9 0.1 collective-permute-start.2
  4.9 0.4 collective-permute-start.3
  5.4 2.8 %pack.1 = (bf16[8,258,128]{2,1,0:T(8,128)(2,1)}, bf16[320,128]{1,0:T(8,128)(2,1)}, bf16[128,768]{1,0:T(8,128)(2,1)}) custom-call(s32[3]{0:T(128)S(1)} %pad_add_fusion.place_ref, bf16[2,16,64]{2,1,0:T(8,128)(2,1)} %latent_ref.1, s32[2,128]{1,0:T(2,128)} %bitcast.4, bf16[128,1536]{1,0:T(8,128)(2,1)} %cot_ref.1), custom_call_target="tpu_custom_call" | custom-call | flops 62914560 | bytes 1056768 | tf_op jit(solution)/shard_map/pack/pallas_call | solution.py:106
  8.1 6.9 %all-to-all-start = ((bf16[8,258,128]{2,1,0:T(8,128)(2,1)}), bf16[8,258,128]{2,1,0:T(8,128)(2,1)S(1)}, u32[]{:S(2)}, u32[]{:S(2)}) async-start(bf16[8,258,128]{2,1,0:T(8,128)(2,1)} %get-tuple-element.55), calls=%async_computation | async-start | bytes 1081344 | tf_op jit(solution)/shard_map/all_to_all | solution.py:78
  15.1 0.0 copy-done.4
  15.1 0.6 broadcast_in_dim.3.refs_7_
  15.7 0.0 copy-done.3
  15.7 0.9 copy.17.refs_8_
  16.6 13.9 %all-to-all-done.packed_ref = bf16[8,258,128]{2,1,0:T(8,128)(2,1)S(1)} async-done(((bf16[8,258,128]{2,1,0:T(8,128)(2,1)}), bf16[8,258,128]{2,1,0:T(8,128)(2,1)S(1)}, u32[]{:S(2)}, u32[]{:S(2)}) %all-to-all-start) | async-done | bytes 528416 | tf_op jit(solution)/shard_map/all_to_all | solution.py:78
  30.5 1.6 %collective-permute-start = (bf16[8,18,128]{2,1,0:T(8,128)(2,1)S(1)}, bf16[8,18,128]{2,1,0:T(8,128)(2,1)S(1)}, u32[]{:S(2)}, u32[]{:S(2)}) collective-permute-start(bf16[8,18,128]{2,1,0:T(8,128)(2,1)S(1)} %get-tuple-element.56.same_ref), channel_id=1, source_target_pairs={{0,2},{2,0},{4,6},{6,4},{8,10},{10,8},{12,14},{14,12},{16,18},{18,... | collective-permute-start | bytes 110600 | tf_op jit(solution)/shard_map/ppermute | solution.py:69
  32.1 0.5 collective-permute-start.7
  32.6 0.0 collective-permute-done.1.refs_1_
  32.6 0.0 collective-permute-done.2.refs_3_
  32.6 0.0 collective-permute-done.3.refs_5_
  32.6 4.9 %gather_weights.1 = (bf16[1536,1664]{1,0:T(8,128)(2,1)S(1)}, bf16[768,1536]{1,0:T(8,128)(2,1)S(1)}, bf16[144,1536]{1,0:T(8,128)(2,1)S(1)}, f32[1,1536]{1,0:T(1,128)S(1)}) custom-call(s32[3]{0:T(128)S(1)} %pad_add_fusion.place_ref, bf16[768,1536]{1,0:T(8,128)(2,1)} %refs_0_.1, bf16[768,768]{1,0:T(8,128)(2,1)} %collective-permute-done.1.refs_1_, ...), custom_call_target="tpu_custom_call" | custom-call | flops 99999997952 | bytes 14155776 | tf_op jit(solution)/shard_map/gather_weights/pallas_call | solution.py:106
  37.6 0.0 collective-permute-done.other_ref
  37.6 0.6 weave.1.image_ref
  38.2 9.6 %forward.1 = (bf16[640,1536]{1,0:T(8,128)(2,1)}, bf16[128,768]{1,0:T(8,128)(2,1)}, bf16[640,1536]{1,0:T(8,128)(2,1)}, bf16[640,1536]{1,0:T(8,128)(2,1)S(1)}, f32...) custom-call(s32[3]{0:T(128)S(1)} %pad_add_fusion.place_ref, ...), custom_call_target="tpu_custom_call" | custom-call | flops 6039797760 | bytes 15925248 | tf_op jit(solution)/shard_map/forward/pallas_call | solution.py:106
  47.8 0.1 collective-permute-start.5
  47.8 0.5 collective-permute-start.8
  48.3 0.0 collective-permute-done.7.refs_1_
  48.3 0.1 collective-permute-start.9
  48.4 0.4 collective-permute-start.4
  48.8 0.8 collective-permute-done.5.b_ref
  49.7 0.1 add_up.2
  49.8 1.6 %collective-permute-start.6 = (bf16[320,768]{1,0:T(8,128)(2,1)S(1)}, bf16[320,768]{1,0:T(8,128)(2,1)S(1)}, u32[]{:S(2)}, u32[]{:S(2)}) collective-permute-start(bf16[320,768]{1,0:T(8,128)(2,1)S(1)} %add_up.2), channel_id=1, source_target_pairs={{0,2},{2,0},{4,6},{6,4},{8,10},{10,8},{12,14},{14,12},{16,18},{18,... | collective-permute-start | bytes 1474568 | tf_op jit(solution)/shard_map/ppermute | solution.py:69
  51.4 0.0 collective-permute-done.8.refs_2_
  51.4 0.0 collective-permute-done.9.refs_3_
  51.4 0.0 copy-start.1
  51.4 8.0 %backward.1 = (bf16[640,768]{1,0:T(8,128)(2,1)}, bf16[640,768]{1,0:T(8,128)(2,1)}, bf16[640,768]{1,0:T(8,128)(2,1)}, bf16[640,768]{1,0:T(8,128)(2,1)}, bf16[640,...) custom-call(bf16[144,1536]{1,0:T(8,128)(2,1)S(1)} %get-tuple-element.61.stem_ref, ...), custom_call_target="tpu_custom_call" | custom-call | flops 6039797760 | bytes 16908288 | tf_op jit(solution)/shard_map/backward/pallas_call | solution.py:106
  59.3 0.0 copy-done.1
  59.4 1.1 %to_image.1.terms_ref = f32[16,16,128]{2,1,0:T(8,128)S(1)} custom-call(s32[3]{0:T(128)S(1)} %pad_add_fusion.place_ref, bf16[640,144]{1,0:T(8,128)(2,1)S(1)} %get-tuple-element.76.proj_ref, bf16[8,80,256]{2,1,0:T(8,128)(2,1)S(1)} %get-tuple-element.77.sel_ref, bf16[144,1536]{1,0:T(8,128)(2,1)S(1)} %get-tuple-element.61.stem_ref, bf16[128,768]{1,0:T(8,128)(2,1)S(1)} %copy-done.1), custom_call_target="tpu_custom_call" | custom-call | flops 47185920 | bytes 1179648 | tf_op jit(solution)/shard_map/to_image/pallas_call | solution.py:106
  60.5 0.0 collective-permute-done.4.b_ref
  60.5 2.6 %collective-permute-done.6.c_ref = bf16[320,768]{1,0:T(8,128)(2,1)S(1)} collective-permute-done((bf16[320,768]{1,0:T(8,128)(2,1)S(1)}, bf16[320,768]{1,0:T(8,128)(2,1)S(1)}, u32[]{:S(2)}, u32[]{:S(2)}) %collective-permute-start.6) | collective-permute-done | bytes 491552 | tf_op jit(solution)/shard_map/ppermute | solution.py:69
  63.1 1.5 %pack_back.1.after = bf16[8,272,128]{2,1,0:T(8,128)(2,1)} custom-call(s32[3]{0:T(128)S(1)} %pad_add_fusion.place_ref, bf16[320,768]{1,0:T(8,128)(2,1)S(1)} %get-tuple-element.66.a_ref, bf16[320,768]{1,0:T(8,128)(2,1)S(1)} %collective-permute-done.4.b_ref, bf16[320,768]{1,0:T(8,128)(2,1)S(1)} %collective-permute-done.6.c_ref, ...), custom_call_target="tpu_custom_call" | custom-call | flops 245760 | bytes 1966080 | tf_op jit(solution)/shard_map/pack_back/pallas_call | solution.py:106
  64.6 3.6 %all-to-all-start.1 = ((bf16[8,272,128]{2,1,0:T(8,128)(2,1)}), bf16[8,272,128]{2,1,0:T(8,128)(2,1)S(1)}, u32[]{:S(2)}, u32[]{:S(2)}) async-start(bf16[8,272,128]{2,1,0:T(8,128)(2,1)} %pack_back.1.after), calls=%async_computation.1 | async-start | bytes 1114112 | tf_op jit(solution)/shard_map/all_to_all | solution.py:78
  68.3 7.3 %far_grads.1 = (bf16[768,768]{1,0:T(8,128)(2,1)}, bf16[768,768]{1,0:T(8,128)(2,1)}, bf16[768,768]{1,0:T(8,128)(2,1)}, bf16[640,768]{1,0:T(8,128)(2,1)S(1)}, bf16...) custom-call(bf16[640,1536]{1,0:T(8,128)(2,1)} %get-tuple-element.79., ...), custom_call_target="tpu_custom_call" | custom-call | bytes 128 | tf_op jit(solution)/shard_map/far_grads/pallas_call | solution.py:106
  75.6 0.1 collective-permute-start.13
  75.6 0.5 collective-permute-start.14
  76.1 0.1 collective-permute-start.15
  76.2 0.0 copy-start
  76.2 0.0 copy-start.2
  76.2 5.1 %near_grads.1 = (f32[768,1536]{1,0:T(8,128)}, f32[768,1536]{1,0:T(8,128)}, f32[1536,768]{1,0:T(8,128)}, f32[8,128]{1,0:T(8,128)S(1)}) custom-call(s32[3]{0:T(128)S(1)} %pad_add_fusion.place_ref, bf16[640,768]{1,0:T(8,128)(2,1)S(1)} %get-tuple-element.85.normed, bf16[640,768]{1,0:T(8,128)(2,1)S(1)} %get-tuple-element.86.ggp, ...), custom_call_target="tpu_custom_call" | custom-call | flops 99999997952 | bytes 128 | tf_op jit(solution)/shard_map/near_grads/pallas_call | solution.py:106
  81.3 1.8 %all-to-all-done.1.back_ref = bf16[8,272,128]{2,1,0:T(8,128)(2,1)S(1)} async-done(((bf16[8,272,128]{2,1,0:T(8,128)(2,1)}), bf16[8,272,128]{2,1,0:T(8,128)(2,1)S(1)}, u32[]{:S(2)}, u32[]{:S(2)}) %all-to-all-start.1) | async-done | bytes 557088 | tf_op jit(solution)/shard_map/all_to_all | solution.py:78
  83.1 0.0 copy-done
  83.1 0.0 copy-done.2
  83.1 0.3 mixed.1
  83.4 0.1 collective-permute-start.10
  83.5 1.6 %collective-permute-start.11 = (f32[16,128]{1,0:T(8,128)S(1)}, f32[16,128]{1,0:T(8,128)S(1)}, u32[]{:S(2)}, u32[]{:S(2)}) collective-permute-start(f32[16,128]{1,0:T(8,128)S(1)} %get-tuple-element.93), channel_id=1, source_target_pairs={{0,2},{2,0},{4,6},{6,4},{8,10},{10,8},{12,14},{14,12},{16,18},{18,... | collective-permute-start | bytes 24584 | tf_op jit(solution)/shard_map/ppermute | solution.py:69
  85.0 2.1 %collective-permute-done.11.b_ref = f32[16,128]{1,0:T(8,128)S(1)} collective-permute-done((f32[16,128]{1,0:T(8,128)S(1)}, f32[16,128]{1,0:T(8,128)S(1)}, u32[]{:S(2)}, u32[]{:S(2)}) %collective-permute-start.11) | collective-permute-done | bytes 8224 | tf_op jit(solution)/shard_map/ppermute | solution.py:69
  87.2 0.0 collective-permute-start.12
  87.2 1.2 %collective-permute-done.12.b_ref = f32[16,128]{1,0:T(8,128)S(1)} collective-permute-done((f32[16,128]{1,0:T(8,128)S(1)}, f32[16,128]{1,0:T(8,128)S(1)}, u32[]{:S(2)}, u32[]{:S(2)}) %collective-permute-start.12) | collective-permute-done | bytes 8224 | tf_op jit(solution)/shard_map/ppermute | solution.py:65
  88.4 0.0 collective-permute-done.10.away_ref
  88.4 1.3 %join.1 = (bf16[128,1536]{1,0:T(8,128)(2,1)}, f32[2,16,64]{2,1,0:T(8,128)}) custom-call(s32[3]{0:T(128)S(1)} %pad_add_fusion.place_ref, bf16[128,768]{1,0:T(8,128)(2,1)S(1)} %get-tuple-element.91.own_ref, bf16[128,768]{1,0:T(8,128)(2,1)S(1)} %collective-permute-done.10.away_ref, f32[16,128]{1,0:T(8,128)S(1)} %add_up.3.a_ref, ...), custom_call_target="tpu_custom_call" | custom-call | bytes 786432 | tf_op jit(solution)/shard_map/join/pallas_call | solution.py:106
  89.7 0.0 collective-permute-done.13.gate_in
  89.7 0.0 collective-permute-done.14.up_in
  89.7 0.0 collective-permute-done.15.down_in
  89.7 4.9 %fill.1 = (f32[768,1536]{1,0:T(8,128)}, f32[768,1536]{1,0:T(8,128)}, f32[1536,768]{1,0:T(8,128)}) custom-call(s32[3]{0:T(128)S(1)} %pad_add_fusion.place_ref, bf16[768,768]{1,0:T(8,128)(2,1)S(1)} %collective-permute-done.13.gate_in, bf16[768,768]{1,0:T(8,128)(2,1)S(1)} %collective-permute-done.14.up_in, ...), custom_call_target="tpu_custom_call", output_to_operand_aliasing={{0}: (4, {}), {1}: (5, {}), {2}: (6, {})} | custom-call | bytes 128 | tf_op jit(solution)/shard_map/fill/pallas_call | solution.py:827
  (2 shorter events, 0.0 us)
Async XLA Ops:
  0.7 14.3 %copy-start.4 = (f32[1536]{0:T(1024)S(1)}, f32[1536]{0:T(1024)}, u32[]{:S(2)}) copy-start(f32[1536]{0:T(1024)} %param.11) | copy-start | bytes 18436
  0.7 14.9 %copy-start.3 = (bf16[1536,8]{0,1:T(8,128)(2,1)S(1)}, bf16[1536,8]{0,1:T(8,128)(2,1)}, u32[]{:S(2)}) copy-start(bf16[1536,8]{0,1:T(8,128)(2,1)} %param.12) | copy-start | bytes 73732
  4.3 28.3 %collective-permute-start.1 = (bf16[768,768]{1,0:T(8,128)(2,1)}, bf16[768,768]{1,0:T(8,128)(2,1)}, u32[]{:S(2)}, u32[]{:S(2)}) collective-permute-start(bf16[768,768]{1,0:T(8,128)(2,1)} %get-tuple-element.57), channel_id=1, source_target_pairs={{0,1},{1,0},{2,3},{3,2},{4,5},{5,4},{6,7},{7,6},{8,9},{9,8},{10,11... | collective-permute-start | bytes 3538952 | tf_op jit(solution)/shard_map/ppermute | solution.py:65
  4.9 27.8 %collective-permute-start.2 = (bf16[768,768]{1,0:T(8,128)(2,1)S(1)}, bf16[768,768]{1,0:T(8,128)(2,1)}, u32[]{:S(2)}, u32[]{:S(2)}) collective-permute-start(bf16[768,768]{1,0:T(8,128)(2,1)S(1)} %get-tuple-element.58), channel_id=1, source_target_pairs={{0,1},{1,0},{2,3},{3,2},{4,5},{5,4},{6,7},{7,6},{8,9},{9,8},{10,11... | collective-permute-start | bytes 3538952 | tf_op jit(solution)/shard_map/ppermute | solution.py:65
  4.9 27.7 %collective-permute-start.3 = (bf16[768,768]{1,0:T(8,128)(2,1)S(1)}, bf16[768,768]{1,0:T(8,128)(2,1)}, u32[]{:S(2)}, u32[]{:S(2)}) collective-permute-start(bf16[768,768]{1,0:T(8,128)(2,1)S(1)} %get-tuple-element.59), channel_id=1, source_target_pairs={{0,1},{1,0},{2,3},{3,2},{4,5},{5,4},{6,7},{7,6},{8,9},{9,8},{10,11... | collective-permute-start | bytes 3538952 | tf_op jit(solution)/shard_map/ppermute | solution.py:65
  8.1 22.4 %all-to-all-start = ((bf16[8,258,128]{2,1,0:T(8,128)(2,1)}), bf16[8,258,128]{2,1,0:T(8,128)(2,1)S(1)}, u32[]{:S(2)}, u32[]{:S(2)}) async-start(bf16[8,258,128]{2,1,0:T(8,128)(2,1)} %get-tuple-element.55), calls=%async_computation | async-start | bytes 1081344 | tf_op jit(solution)/shard_map/all_to_all | solution.py:78
  30.5 7.1 %collective-permute-start = (bf16[8,18,128]{2,1,0:T(8,128)(2,1)S(1)}, bf16[8,18,128]{2,1,0:T(8,128)(2,1)S(1)}, u32[]{:S(2)}, u32[]{:S(2)}) collective-permute-start(bf16[8,18,128]{2,1,0:T(8,128)(2,1)S(1)} %get-tuple-element.56.same_ref), channel_id=1, source_target_pairs={{0,2},{2,0},{4,6},{6,4},{8,10},{10,8},{12,14},{14,12},{16,18},{18,... | collective-permute-start | bytes 110600 | tf_op jit(solution)/shard_map/ppermute | solution.py:69
  32.1 16.2 %collective-permute-start.7 = (bf16[320,768]{1,0:T(8,128)(2,1)S(1)}, bf16[320,768]{1,0:T(8,128)(2,1)S(1)}, u32[]{:S(2)}, u32[]{:S(2)}) collective-permute-start(bf16[320,768]{1,0:T(8,128)(2,1)S(1)} %get-tuple-element.75.refs_0_), channel_id=1, source_target_pairs={{0,2},{2,0},{4,6},{6,4},{8,10},{10,8},{12,14},{14,12},{16,18},{18,... | collective-permute-start | bytes 1474568 | tf_op jit(solution)/shard_map/ppermute | solution.py:69
  47.8 1.9 %collective-permute-start.5 = (bf16[320,768]{1,0:T(8,128)(2,1)S(1)}, bf16[320,768]{1,0:T(8,128)(2,1)S(1)}, u32[]{:S(2)}, u32[]{:S(2)}) collective-permute-start(bf16[320,768]{1,0:T(8,128)(2,1)S(1)} %get-tuple-element.69), channel_id=1, source_target_pairs={{0,1},{1,0},{2,3},{3,2},{4,5},{5,4},{6,7},{7,6},{8,9},{9,8},{10,11... | collective-permute-start | bytes 1474568 | tf_op jit(solution)/shard_map/ppermute | solution.py:65
  47.8 3.5 %collective-permute-start.8 = (bf16[320,768]{1,0:T(8,128)(2,1)S(1)}, bf16[320,768]{1,0:T(8,128)(2,1)S(1)}, u32[]{:S(2)}, u32[]{:S(2)}) collective-permute-start(bf16[320,768]{1,0:T(8,128)(2,1)S(1)} %get-tuple-element.75.refs_0_), channel_id=1, source_target_pairs={{0,1},{1,0},{2,3},{3,2},{4,5},{5,4},{6,7},{7,6},{8,9},{9,8},{10,11... | collective-permute-start | bytes 1474568 | tf_op jit(solution)/shard_map/ppermute | solution.py:65
  48.3 3.0 %collective-permute-start.9 = (bf16[320,768]{1,0:T(8,128)(2,1)S(1)}, bf16[320,768]{1,0:T(8,128)(2,1)S(1)}, u32[]{:S(2)}, u32[]{:S(2)}) collective-permute-start(bf16[320,768]{1,0:T(8,128)(2,1)S(1)} %collective-permute-done.7.refs_1_), channel_id=1, source_target_pairs={{0,1},{1,0},{2,3},{3,2},{4,5},{5,4},{6,7},{7,6},{8,9},{9,8},{10,11... | collective-permute-start | bytes 1474568 | tf_op jit(solution)/shard_map/ppermute | solution.py:65
  48.4 12.1 %collective-permute-start.4 = (bf16[320,768]{1,0:T(8,128)(2,1)S(1)}, bf16[320,768]{1,0:T(8,128)(2,1)S(1)}, u32[]{:S(2)}, u32[]{:S(2)}) collective-permute-start(bf16[320,768]{1,0:T(8,128)(2,1)S(1)} %get-tuple-element.67), channel_id=1, source_target_pairs={{0,1},{1,0},{2,3},{3,2},{4,5},{5,4},{6,7},{7,6},{8,9},{9,8},{10,11... | collective-permute-start | bytes 1474568 | tf_op jit(solution)/shard_map/ppermute | solution.py:65
  49.8 13.3 %collective-permute-start.6 = (bf16[320,768]{1,0:T(8,128)(2,1)S(1)}, bf16[320,768]{1,0:T(8,128)(2,1)S(1)}, u32[]{:S(2)}, u32[]{:S(2)}) collective-permute-start(bf16[320,768]{1,0:T(8,128)(2,1)S(1)} %add_up.2), channel_id=1, source_target_pairs={{0,2},{2,0},{4,6},{6,4},{8,10},{10,8},{12,14},{14,12},{16,18},{18,... | collective-permute-start | bytes 1474568 | tf_op jit(solution)/shard_map/ppermute | solution.py:69
  51.4 8.0 %copy-start.1 = (bf16[128,768]{1,0:T(8,128)(2,1)S(1)}, bf16[128,768]{1,0:T(8,128)(2,1)}, u32[]{:S(2)}) copy-start(bf16[128,768]{1,0:T(8,128)(2,1)} %get-tuple-element.78.cot_ref) | copy-start | bytes 589828
  64.6 18.4 %all-to-all-start.1 = ((bf16[8,272,128]{2,1,0:T(8,128)(2,1)}), bf16[8,272,128]{2,1,0:T(8,128)(2,1)S(1)}, u32[]{:S(2)}, u32[]{:S(2)}) async-start(bf16[8,272,128]{2,1,0:T(8,128)(2,1)} %pack_back.1.after), calls=%async_computation.1 | async-start | bytes 1114112 | tf_op jit(solution)/shard_map/all_to_all | solution.py:78
  75.6 14.2 %collective-permute-start.13 = (bf16[768,768]{1,0:T(8,128)(2,1)}, bf16[768,768]{1,0:T(8,128)(2,1)S(1)}, u32[]{:S(2)}, u32[]{:S(2)}) collective-permute-start(bf16[768,768]{1,0:T(8,128)(2,1)} %get-tuple-element.96), channel_id=1, source_target_pairs={{0,1},{1,0},{2,3},{3,2},{4,5},{5,4},{6,7},{7,6},{8,9},{9,8},{10,11... | collective-permute-start | bytes 3538952 | tf_op jit(solution)/shard_map/ppermute | solution.py:65
  75.6 14.1 %collective-permute-start.14 = (bf16[768,768]{1,0:T(8,128)(2,1)}, bf16[768,768]{1,0:T(8,128)(2,1)S(1)}, u32[]{:S(2)}, u32[]{:S(2)}) collective-permute-start(bf16[768,768]{1,0:T(8,128)(2,1)} %get-tuple-element.97), channel_id=1, source_target_pairs={{0,1},{1,0},{2,3},{3,2},{4,5},{5,4},{6,7},{7,6},{8,9},{9,8},{10,11... | collective-permute-start | bytes 3538952 | tf_op jit(solution)/shard_map/ppermute | solution.py:65
  76.1 13.6 %collective-permute-start.15 = (bf16[768,768]{1,0:T(8,128)(2,1)}, bf16[768,768]{1,0:T(8,128)(2,1)}, u32[]{:S(2)}, u32[]{:S(2)}) collective-permute-start(bf16[768,768]{1,0:T(8,128)(2,1)} %get-tuple-element.98), channel_id=1, source_target_pairs={{0,1},{1,0},{2,3},{3,2},{4,5},{5,4},{6,7},{7,6},{8,9},{9,8},{10,11... | collective-permute-start | bytes 3538952 | tf_op jit(solution)/shard_map/ppermute | solution.py:65
  76.2 6.9 %copy-start = (bf16[128,768]{1,0:T(8,128)(2,1)S(1)}, bf16[128,768]{1,0:T(8,128)(2,1)}, u32[]{:S(2)}) copy-start(bf16[128,768]{1,0:T(8,128)(2,1)} %get-tuple-element.64.stem_ref) | copy-start | bytes 589828
  76.2 6.9 %copy-start.2 = (bf16[320,128]{1,0:T(8,128)(2,1)S(1)}, bf16[320,128]{1,0:T(8,128)(2,1)}, u32[]{:S(2)}) copy-start(bf16[320,128]{1,0:T(8,128)(2,1)} %get-tuple-element.65.taken_ref) | copy-start | bytes 245764
  83.4 5.0 %collective-permute-start.10 = (bf16[128,768]{1,0:T(8,128)(2,1)S(1)}, bf16[128,768]{1,0:T(8,128)(2,1)S(1)}, u32[]{:S(2)}, u32[]{:S(2)}) collective-permute-start(bf16[128,768]{1,0:T(8,128)(2,1)S(1)} %get-tuple-element.91.own_ref), channel_id=1, source_target_pairs={{0,1},{1,0},{2,3},{3,2},{4,5},{5,4},{6,7},{7,6},{8,9},{9,8},{10,11... | collective-permute-start | bytes 589832 | tf_op jit(solution)/shard_map/ppermute | solution.py:65
  83.5 3.7 %collective-permute-start.11 = (f32[16,128]{1,0:T(8,128)S(1)}, f32[16,128]{1,0:T(8,128)S(1)}, u32[]{:S(2)}, u32[]{:S(2)}) collective-permute-start(f32[16,128]{1,0:T(8,128)S(1)} %get-tuple-element.93), channel_id=1, source_target_pairs={{0,2},{2,0},{4,6},{6,4},{8,10},{10,8},{12,14},{14,12},{16,18},{18,... | collective-permute-start | bytes 24584 | tf_op jit(solution)/shard_map/ppermute | solution.py:69
  87.2 1.2 %collective-permute-start.12 = (f32[16,128]{1,0:T(8,128)S(1)}, f32[16,128]{1,0:T(8,128)S(1)}, u32[]{:S(2)}, u32[]{:S(2)}) collective-permute-start(f32[16,128]{1,0:T(8,128)S(1)} %add_up.3.a_ref), channel_id=1, source_target_pairs={{0,1},{1,0},{2,3},{3,2},{4,5},{5,4},{6,7},{7,6},{8,9},{9,8},{10,11... | collective-permute-start | bytes 24584 | tf_op jit(solution)/shard_map/ppermute | solution.py:65

commit v2 on v1

--- a/solution.py
+++ b/solution.py
@@ -10,6 +10,7 @@
 CAP = 40
 LANES = 128
 GROUP = 16
+FORWARD_FLOPS = 100_000_000_000
 F32 = jnp.float32
 BF16 = jnp.bfloat16
 MIB = 1024 * 1024
@@ -202,26 +203,27 @@
     return jnp.concatenate(parts, axis=1)[:, :columns]
 
 
-def unpack_kernel(packed_ref, cot_ref, image_ref):
+def unpack_kernel(packed_ref, after_ref, cot_ref, image_ref):
     cot_ref[...] = unpacked(packed_ref, cot_ref.shape[1]).astype(BF16)
     top = packed_ref.shape[1] - image_ref.shape[1]
     for b in range(packed_ref.shape[0]):
         image_ref[b] = packed_ref[b, top:, :]
 
 
-def unpack(packed, half, lines):
+def unpack(packed, half, lines, after):
     blocks, _, tok = packed.shape
     return kernel_call(
         unpack_kernel,
-        0,
+        100_000_000_000,
         4 * packed.size,
-        [near(packed)],
+        [near(packed), far_off(after)],
         [fast((blocks * CAP, half), BF16), fast((blocks, lines, tok), BF16)],
         "unpack",
-    )
-
-
-def weave_kernel(place_ref, same_ref, other_ref, after_ref, out_ref):
+        specs=[vmem(), hbm()],
+    )
+
+
+def weave_kernel(place_ref, same_ref, other_ref, after_ref, then_ref, out_ref):
     even = (place_ref[1] & 1) == 0
     for e in range(same_ref.shape[0]):
         same, other = same_ref[e], other_ref[e]
@@ -229,56 +231,51 @@
         out_ref[2 * e + 1] = jnp.where(even, other, same)
 
 
-def weave(place, same, other, after):
+def weave(place, same, other, after, then):
     shape = (2 * same.shape[0],) + same.shape[1:]
     return kernel_call(
         weave_kernel,
         0,
         8 * same.size,
-        [near(same), near(other), near(after)],
+        [near(same), near(other), near(after), near(then)],
         [fast(shape, same.dtype)],
         "weave",
         place=place,
     )[0]
 
 
-def sum_kernel(a_ref, b_ref, out_ref):
+def sum_kernel(a_ref, b_ref, after_ref, out_ref):
     out_ref[...] = (a_ref[...].astype(F32) + b_ref[...].astype(F32)).astype(out_ref.dtype)
 
 
-def add_up(a, b):
-    return kernel_call(
-        sum_kernel, a.size, 6 * a.size, [near(a), near(b)], [fast(a.shape, a.dtype)], "add_up"
-    )[0]
-
-
-def pack_back_kernel(paired, place_ref, a_ref, b_ref, c_ref, terms_ref, out_ref):
+def add_up(a, b, after):
+    operands = [near(a), near(b), near(after)]
+    outs = [fast(a.shape, a.dtype)]
+    return kernel_call(sum_kernel, a.size, 6 * a.size, operands, outs, "add_up")[0]
+
+
+def pack_back_kernel(paired, a_ref, b_ref, c_ref, terms_ref, over_ref, after_ref, out_ref):
     total = a_ref[...].astype(F32) + b_ref[...].astype(F32)
     if paired:
         total = total + c_ref[...].astype(F32)
-    side = place_ref[1] & 1
     for b in range(out_ref.shape[0]):
         slots = stacked(total[b * CAP : (b + 1) * CAP])
+        terms = terms_ref[b]
         if paired:
-            terms = [terms_ref[2 * b + side], terms_ref[2 * b + 1 - side]]
-        else:
-            terms = [terms_ref[b]]
-        out_ref[b] = jnp.concatenate([slots] + terms, axis=0).astype(BF16)
-
-
-def pack_back(place, a, b, c, terms, paired):
+            terms = terms + over_ref[b].astype(F32)
+        out_ref[b] = jnp.concatenate([slots, terms], axis=0).astype(BF16)
+
+
+def pack_back(a, b, c, terms, over, after, paired):
     blocks, channels, tok = terms.shape
     depth = tiles_of(a.shape[1]) * CAP + channels
-    if paired:
-        blocks, depth = blocks // 2, depth + channels
     return kernel_call(
         functools.partial(pack_back_kernel, paired),
         a.size,
         8 * a.size,
-        [near(a), near(b), near(c), near(terms)],
+        [near(x) for x in (a, b, c, terms, over, after)],
         [shape_of((blocks, depth, LANES), BF16)],
         "pack_back",
-        place=place,
     )[0]
 
 
@@ -294,7 +291,7 @@
     ]
 
 
-def far_kernel(place_ref, gate_ref, up_ref, down_ref, gate_out, up_out, down_out, sem):
+def far_kernel(place_ref, gate_ref, up_ref, down_ref, after_ref, gate_out, up_out, down_out, sem):
     size = gate_out.shape[1]
     at = pl.multiple_of((1 - place_ref[2]) * size, LANES)
     copies = (
@@ -308,18 +305,18 @@
         copy.wait()
 
 
-def far_weights(place, gate, up, down):
+def far_weights(place, gate, up, down, after):
     half, hid = gate.shape
     size = hid // 2
     return kernel_call(
         far_kernel,
         0,
         LANES,
-        [far_off(gate), far_off(up), far_off(down)],
+        [far_off(gate), far_off(up), far_off(down), after],
         [fast((half, size), BF16), fast((half, size), BF16), fast((size, half), BF16)],
         "far_weights",
         place=place,
-        specs=[hbm()] * 3,
+        specs=[hbm()] * 4,
         scratch=[pltpu.SemaphoreType.DMA((3 * PIECES,))],
     )
 
@@ -332,34 +329,13 @@
     return out
 
 
-def weights_kernel(parts, experts, place_ref, *refs):
-    weights = refs[: 3 * parts]
-    stem_in, gain_in, router_in = refs[3 * parts : 3 * parts + 3]
-    inner, outer, stem, gain, sem = refs[3 * parts + 3 :]
-    gates, ups, downs = weights[:parts], weights[parts : 2 * parts], weights[2 * parts :]
-    size = outer.shape[0]
-    copies = []
-
-    def copy(source, target):
-        copies.extend(pieces(source, target, sem, len(copies)))
-
-    for n, refs_of in enumerate((gates, ups)):
-        for ref, (a, depth) in zip(refs_of, cuts([r.shape[0] for r in refs_of])):
-            if ref.shape[1] != size:
-                ref = ref.at[:, pl.ds(pl.multiple_of(place_ref[2] * size, LANES), size)]
-            copy(ref, inner.at[pl.ds(a, depth), pl.ds(n * size, size)])
-    for ref, (a, depth) in zip(downs, cuts([r.shape[1] for r in downs])):
-        if ref.shape[0] != size:
-            ref = ref.at[pl.ds(pl.multiple_of(place_ref[2] * size, LANES), size), :]
-        copy(ref, outer.at[:, pl.ds(a, depth)])
-    for one in copies:
-        one.start()
+def params_kernel(turn, experts, place_ref, stem_in, gain_in, router_in, after, stem, gain, router):
     wide = router_in[...].astype(F32)
     model = wide.shape[0]
     blank = jnp.zeros((model, LANES - 2 * experts), F32)
     wide = jnp.concatenate([wide, wide, blank], axis=1)
     values, gains = stem_in[...], gain_in[...]
-    if parts == 2:
+    if turn:
         half = model // 2
         first = place_ref[2] == 0
         wide = jnp.where(first, wide, jnp.concatenate([wide[half:], wide[:half]], axis=0))
@@ -369,32 +345,82 @@
         gains = jnp.where(first, gains, turned)
     stem[...] = values
     gain[...] = gains
-    inner[:, 2 * size :] = wide.astype(BF16)
-    for one in copies:
-        one.wait()
-
-
-def gather_weights(place, stem, gain, router, gate_parts, up_parts, down_parts):
-    parts = len(gate_parts)
+    router[...] = wide.astype(BF16)
+
+
+def small_params(place, stem, gain, router, after, turn):
     model, experts = router.shape
-    size = down_parts[-1].shape[0]
-    weights = [far_off(w) for p in (gate_parts, up_parts, down_parts) for w in p]
     small = [far_off(stem), far_off(gain), far_off(router)]
-    return kernel_call(
-        functools.partial(weights_kernel, parts, experts),
-        100_000_000_000,
-        12 * model * size,
-        weights + small,
+    shapes = [(stem.shape, BF16), (gain.shape, F32), ((model, LANES), BF16)]
+    return kernel_call(
+        functools.partial(params_kernel, turn, experts),
+        0,
+        LANES,
+        small + [after],
+        [pltpu.HBM(*a) for a in shapes],
+        "params",
+        place=place,
+        specs=[whole(a.shape) for a in small] + [hbm()],
+        out_specs=[whole(shape) for shape, _ in shapes],
+    )
+
+
+def inner_copies(place_ref, refs, inner, size, at, sem):
+    copies = []
+    for n, (ref, (a, depth)) in enumerate(zip(refs, cuts([r.shape[0] for r in refs]))):
+        if ref.shape[1] != size:
+            ref = ref.at[:, pl.ds(pl.multiple_of(place_ref[2] * size, LANES), size)]
+        copies += pieces(ref, inner.at[pl.ds(a, depth), pl.ds(at, size)], sem, n * PIECES)
+    return copies
+
+
+def outer_copies(place_ref, refs, outer, sem):
+    copies = []
+    size = outer.shape[0]
+    for n, (ref, (a, depth)) in enumerate(zip(refs, cuts([r.shape[1] for r in refs]))):
+        if ref.shape[0] != size:
+            ref = ref.at[pl.ds(pl.multiple_of(place_ref[2] * size, LANES), size), :]
+        copies += pieces(ref, outer.at[:, pl.ds(a, depth)], sem, n * PIECES)
+    return copies
+
+
+def gather_kernel(parts, place_ref, *refs):
+    gates, (stem_in, gain_in, router_in) = refs[:parts], refs[parts : parts + 3]
+    stem, gain, inner, small_sem, sem = refs[parts + 3 :]
+    size = (inner.shape[1] - LANES) // 2
+    copies = [
+        pltpu.make_async_copy(stem_in, stem, small_sem.at[0]),
+        pltpu.make_async_copy(gain_in, gain, small_sem.at[1]),
+        pltpu.make_async_copy(router_in, inner.at[:, pl.ds(2 * size, LANES)], small_sem.at[2]),
+    ]
+    copies += inner_copies(place_ref, gates, inner, size, 0, sem)
+    for copy in copies:
+        copy.start()
+    for copy in copies:
+        copy.wait()
+
+
+def gather(place, small, gates, size):
+    stem, gain, router = small
+    model = router.shape[0]
+    operands = [far_off(a) for a in list(gates) + list(small)]
+    return kernel_call(
+        functools.partial(gather_kernel, len(gates)),
+        0,
+        LANES,
+        operands,
         [
-            fast((model, 2 * size + LANES), BF16),
-            fast((size, model), BF16),
             fast(stem.shape, BF16),
             fast(gain.shape, F32),
+            fast((model, 2 * size + LANES), BF16),
         ],
-        "gather_weights",
+        "gather",
         place=place,
-        specs=[hbm()] * (3 * parts) + [whole(a.shape) for a in small],
-        scratch=[pltpu.SemaphoreType.DMA((3 * parts * PIECES,))],
+        specs=[hbm()] * len(operands),
+        scratch=[
+            pltpu.SemaphoreType.DMA((3,)),
+            pltpu.SemaphoreType.DMA((len(gates) * PIECES,)),
+        ],
     )
 
 
@@ -472,12 +498,28 @@
 
 
 def forward_kernel(
-    paired, width, experts, outs, place_ref, image_ref, stem_ref, gain_ref, inner, outer,
-    saved_ref, own_out, normed_ref, value_ref, meta_ref, coef_ref, sel_ref, pg_ref, pu_ref, *refs,
+    paired, parts, width, experts, outs, place_ref, image_ref, stem_ref, gain_ref, _, *refs
 ):
-    out_refs, (own_ref, save_sem) = refs[:-2], refs[-2:]
+    weights, refs = refs[: 2 * parts], refs[2 * parts :]
+    saved_ref, own_out, normed_ref, value_ref, meta_ref, coef_ref, sel_ref, pg_ref, pu_ref = refs[:9]
+    hidden_ref, inner, outer, *out_refs = refs[9:-4]
+    own_ref, save_sem, up_sem, down_sem = refs[-4:]
     step = pl.program_id(0)
     size = outer.shape[0]
+    up_copies = inner_copies(place_ref, weights[:parts], inner, size, size, up_sem)
+    down_copies = outer_copies(place_ref, weights[parts:], outer, down_sem)
+
+    def arrive(copies):
+        @pl.when(step == 0)
+        def _():
+            for copy in copies:
+                copy.wait()
+
+    @pl.when(step == 0)
+    def _():
+        for copy in up_copies + down_copies:
+            copy.start()
+
     chunk = GROUP * CAP
     here = pl.ds(pl.multiple_of(step * chunk, chunk), chunk)
     top = 0
@@ -534,18 +576,21 @@
     )
     meta_ref[here, :] = jnp.where(lane == 0.0, gate, scale)
     pre_gate = mm(normed, inner[:, :size])
+    arrive(up_copies)
     pre_up = mm(normed, inner[:, size : 2 * size])
     pg_ref[here, :] = pre_gate.astype(BF16)
     pu_ref[here, :] = pre_up.astype(BF16)
     hidden = (pre_gate * jax.nn.sigmoid(pre_gate) * pre_up).astype(BF16)
-    part, at = None, None
-    for ref, (a, n, b, m) in zip(out_refs, outs):
-        if (b, m) != at:
-            part, at = gate * mm(hidden, outer[:, b : b + m]), (b, m)
-        if n == chunk:
-            ref[here, :] = part.astype(BF16)
-        else:
-            ref[...] = part[a : a + n].astype(BF16)
+    hidden_ref[here, :] = hidden
+    arrive(down_copies)
+    if paired:
+        half_rows = chunk // 2
+        for ref, (a, n) in zip(out_refs, cuts([r.shape[1] for r in out_refs])):
+            part = mm(hidden[half_rows:], outer[:, a : a + n])
+            ref[...] = (gate[half_rows:] * part).astype(BF16)
+    else:
+        for ref, (a, n) in zip(out_refs, cuts([r.shape[1] for r in out_refs])):
+            ref[here, :] = (gate * mm(hidden, outer[:, a : a + n])).astype(BF16)
     save.wait()
 
     @pl.when(step == 0)
@@ -553,33 +598,69 @@
         own_save.wait()
 
 
-def forward(place, image, stem, gain, inner, outer, half, outs, paired, width, experts):
+def forward(place, image, gathered, weights, size, half, columns, paired, width, experts):
     blocks, _, tok = image.shape
     slots, chunk = blocks * CAP, GROUP * CAP
-    model, size = stem.shape[1], outer.shape[0]
-    return kernel_call(
-        functools.partial(forward_kernel, paired, width, experts, outs),
-        2 * slots * model * size * 4,
-        slots * (6 * model + 6 * size) + 6 * model * size,
-        [near(a) for a in (image, stem, gain, inner, outer)],
-        [
-            pltpu.HBM((slots, model), BF16),
-            pltpu.HBM((tok, half), BF16),
-            fast((chunk, model), BF16),
-            fast((slots, model), BF16),
-            fast((slots, LANES), F32),
-            fast((slots, LANES), F32),
-            fast((blocks // 2, 2 * CAP, 2 * tok), BF16),
-            fast((slots, size), BF16),
-            fast((slots, size), BF16),
-        ]
-        + [fast((slots if n == chunk else n, m), BF16) for _, n, _, m in outs],
-        "forward",
-        mib=18,
-        place=place,
-        steps=blocks // GROUP,
-        out_specs=[hbm()] * 2 + [vmem()] * (7 + len(outs)),
-        scratch=[pltpu.VMEM((tok, half), BF16), pltpu.SemaphoreType.DMA((2,))],
+    stem, gain, inner = gathered
+    model = stem.shape[1]
+    parts = len(weights) // 2
+    operands = [near(image), near(stem), near(gain), near(inner)] + [far_off(w) for w in weights]
+    outs = [
+        pltpu.HBM((slots, model), BF16),
+        pltpu.HBM((tok, half), BF16),
+        fast((chunk, model), BF16),
+        fast((slots, model), BF16),
+        fast((slots, LANES), F32),
+        fast((slots, LANES), F32),
+        fast((blocks // 2, 2 * CAP, 2 * tok), BF16),
+        fast((slots, size), BF16),
+        fast((slots, size), BF16),
+        fast((slots, size), BF16),
+        fast(inner.shape, BF16),
+        fast((size, model), BF16),
+    ]
+    outs += [fast((slots // 2 if paired else slots, n), BF16) for n in columns]
+    return pl.pallas_call(
+        functools.partial(forward_kernel, paired, parts, width, experts, columns),
+        compiler_params=pltpu.CompilerParams(vmem_limit_bytes=20 * MIB),
+        cost_estimate=pl.CostEstimate(
+            flops=FORWARD_FLOPS, bytes_accessed=LANES, transcendentals=0
+        ),
+        grid_spec=pltpu.PrefetchScalarGridSpec(
+            num_scalar_prefetch=1,
+            grid=(blocks // GROUP,),
+            in_specs=[vmem()] * 4 + [hbm()] * len(weights),
+            out_specs=[hbm()] * 2 + [vmem()] * (len(outs) - 2),
+            scratch_shapes=[
+                pltpu.VMEM((tok, half), BF16),
+                pltpu.SemaphoreType.DMA((2,)),
+                pltpu.SemaphoreType.DMA((parts * PIECES,)),
+                pltpu.SemaphoreType.DMA((parts * PIECES,)),
+            ],
+        ),
+        out_shape=outs,
+        input_output_aliases={4: 10},
+        name="forward",
+    )(place, *operands)
+
+
+def outputs_kernel(meta_ref, hidden_ref, outer, near_ref, far_ref):
+    count, half = near_ref.shape
+    gate = meta_ref[:count, 0:1]
+    hidden = hidden_ref[:count, :]
+    near_ref[...] = (gate * mm(hidden, outer[:, :half])).astype(BF16)
+    far_ref[...] = (gate * mm(hidden, outer[:, half:])).astype(BF16)
+
+
+def outputs(meta, hidden, outer):
+    count, half = hidden.shape[0] // 2, outer.shape[1] // 2
+    return kernel_call(
+        outputs_kernel,
+        0,
+        LANES,
+        [near(meta), near(hidden), near(outer)],
+        [fast((count, half), BF16)] * 2,
+        "outputs",
     )
 
 
@@ -659,20 +740,21 @@
         [near(a) for a in operands],
         [pltpu.HBM((slots, size), BF16)] * 3
         + [pltpu.HBM((slots, part[0].shape[1]), BF16) for part in cots]
-        + [fast((slots, taps), BF16)],
+        + [fast((slots, taps), BF16)]
+        + [fast((chunk, size), BF16)] * 3,
         "backward",
         mib=20,
         steps=slots // chunk,
-        out_specs=[hbm()] * (3 + parts) + [vmem()],
-        scratch=[pltpu.VMEM((chunk, size), BF16)] * 3
-        + [pltpu.SemaphoreType.DMA((3 + parts * bands,))],
-    )
-
-
-def image_kernel(paired, width, place_ref, proj_ref, sel_ref, stem_ref, cot_ref, out_ref, terms):
+        out_specs=[hbm()] * (3 + parts) + [vmem()] * 4,
+        scratch=[pltpu.SemaphoreType.DMA((3 + parts * bands,))],
+    )
+
+
+def image_kernel(paired, width, place_ref, proj_ref, sel_ref, stem_ref, cot_ref, *refs):
+    out_refs, terms = refs[:-1], refs[-1]
     pairs = sel_ref.shape[0]
     tok = cot_ref.shape[0]
-    channels = out_ref.shape[1]
+    channels = out_refs[0].shape[1]
     count = 2 * pairs * tok
     own = mm_t(stem_ref[:, : cot_ref.shape[1]], cot_ref[...])
     me = place_ref[1]
@@ -702,8 +784,15 @@
             token = lane - shift
             keep = (column >= 0) & (column < width) & (token >= 0) & (token < count)
             total = total + jnp.where(keep, piece, 0.0)
-    for b in range(2 * pairs):
-        out_ref[b] = total[:, b * tok : (b + 1) * tok]
+    for q in range(pairs):
+        low = total[:, 2 * q * tok : (2 * q + 1) * tok]
+        high = total[:, (2 * q + 1) * tok : (2 * q + 2) * tok]
+        if paired:
+            out_refs[0][q] = jnp.where(even, low, high)
+            out_refs[1][q] = jnp.where(even, high, low).astype(BF16)
+        else:
+            out_refs[0][2 * q] = low
+            out_refs[0][2 * q + 1] = high
 
 
 def to_image(place, proj, sel, stem, cot, paired, width, channels):
@@ -715,95 +804,102 @@
         2 * proj.shape[0] * 2 * tok * taps,
         4 * taps * blocks * tok,
         [near(a) for a in (proj, sel, stem, cot)],
-        [fast((blocks, channels, tok), F32)],
+        [fast((pairs, channels, tok), F32), fast((pairs, channels, tok), BF16)]
+        if paired
+        else [fast((blocks, channels, tok), F32)],
         "to_image",
         place=place,
         scratch=[pltpu.VMEM((taps, blocks * tok), F32)],
-    )[0]
-
-
-def far_grads_kernel(normed, ggp, gup, hg, near_cot, cot, after, gate_out, up_out, down_out, *refs):
-    near_v, ggp_v, gup_v, hg_v, near_cot_v, far_v, cot_v, sem = refs
+    )
+
+
+def far_grads_kernel(normed, ggp, gup, hg, *refs):
+    cots, (gate_out, up_out, down_out) = refs[:-3], refs[-3:]
+    half = cots[0].shape[1]
+    far = normed[:, half:]
+    gate_out[...] = t_mm(far, ggp[...]).astype(BF16)
+    up_out[...] = t_mm(far, gup[...]).astype(BF16)
+    cot = jnp.concatenate([ref[...] for ref in cots], axis=0)
+    down_out[...] = t_mm(hg[...], cot).astype(BF16)
+
+
+def far_grads(normed, ggp, gup, hg, cots):
+    slots, size = ggp.shape
+    half = cots[0].shape[1]
+    return kernel_call(
+        far_grads_kernel,
+        6 * slots * size * half,
+        20 * slots * size,
+        [near(a) for a in [normed, ggp, gup, hg] + list(cots)],
+        [fast((half, size), BF16)] * 2 + [fast((size, half), BF16)],
+        "far_grads",
+    )
+
+
+def near_grads_kernel(
+    place_ref, normed, ggp, gup, hg, cot, after_ref, gate_out, up_out, down_out,
+    left, right, own, sem, own_sem,
+):
     half = cot.shape[1]
-    sources = (normed.at[:, pl.ds(half, half)], ggp, gup, hg, cot, normed.at[:, pl.ds(0, half)], near_cot)
-    targets = (far_v, ggp_v, gup_v, hg_v, cot_v, near_v, near_cot_v)
+    size = ggp.shape[1]
+    here = pl.multiple_of(place_ref[2] * size, LANES)
+    sources = (normed.at[:, pl.ds(0, half)], ggp, gup, hg, cot)
+    targets = (left.at[0], right.at[0], right.at[1], left.at[1], right.at[2])
     loads = [pltpu.make_async_copy(a, b, sem.at[n]) for n, (a, b) in enumerate(zip(sources, targets))]
+    places = (
+        gate_out.at[:, pl.ds(here, size)],
+        up_out.at[:, pl.ds(here, size)],
+        down_out.at[pl.ds(here, size), :],
+    )
+    results = [pieces(own.at[n], a, own_sem, n * PIECES) for n, a in enumerate(places)]
     for load in loads:
         load.start()
     for load in loads[:2]:
         load.wait()
-    gate_out[...] = t_mm(far_v[...], ggp_v[...]).astype(BF16)
+    own[0] = t_mm(left[0], right[0])
+    for copy in results[0]:
+        copy.start()
     loads[2].wait()
-    up_out[...] = t_mm(far_v[...], gup_v[...]).astype(BF16)
+    own[1] = t_mm(left[0], right[1])
+    for copy in results[1]:
+        copy.start()
     loads[3].wait()
     loads[4].wait()
-    down_out[...] = t_mm(hg_v[...], cot_v[...]).astype(BF16)
-    loads[5].wait()
-    loads[6].wait()
-
-
-def far_grads(normed, ggp, gup, hg, near_cot, cot, after):
-    slots, size = ggp.shape
-    half = cot.shape[1]
-    held = [(slots, half), (slots, size), (slots, size), (slots, size), (slots, half)]
-    return kernel_call(
-        far_grads_kernel,
-        0,
-        LANES,
-        [far_off(a) for a in (normed, ggp, gup, hg, near_cot, cot)] + [after],
-        [fast((half, size), BF16)] * 2
-        + [fast((size, half), BF16)]
-        + [fast(shape, BF16) for shape in held],
-        "far_grads",
-        specs=[hbm()] * 7,
-        scratch=[
-            pltpu.VMEM((slots, half), BF16),
-            pltpu.VMEM((slots, half), BF16),
-            pltpu.SemaphoreType.DMA((7,)),
-        ],
-    )
-
-
-def near_grads_kernel(
-    place_ref, normed, ggp, gup, hg, cot, gate_out, up_out, down_out, done_ref, own, own_sem
-):
-    size = ggp.shape[1]
-    here = pl.multiple_of(place_ref[2] * size, LANES)
-    places = (
-        gate_out.at[:, pl.ds(here, size)],
-        up_out.at[:, pl.ds(here, size)],
-        down_out.at[pl.ds(here, size), :],
-    )
-    results = [pieces(own.at[n], a, own_sem, n * PIECES) for n, a in enumerate(places)]
-    done_ref[...] = jnp.zeros(done_ref.shape, F32)
-    for n, (left, right) in enumerate(((normed, ggp), (normed, gup), (hg, cot))):
-        own[n] = t_mm(left[...], right[...])
-        for copy in results[n]:
-            copy.start()
+    own[2] = t_mm(left[1], right[2])
+    for copy in results[2]:
+        copy.start()
     for copy in results[0] + results[1] + results[2]:
         copy.wait()
 
 
-def near_grads(place, normed, ggp, gup, hg, cot):
+def near_grads(place, normed, ggp, gup, hg, cot, after):
     slots, size = ggp.shape
     half = cot.shape[1]
     return kernel_call(
         near_grads_kernel,
         100_000_000_000,
         LANES,
-        [near(a) for a in (normed, ggp, gup, hg, cot)],
+        [far_off(a) for a in (normed, ggp, gup, hg, cot)] + [after],
         [pltpu.HBM((half, 2 * size), F32)] * 2
-        + [pltpu.HBM((2 * size, half), F32), fast((8, LANES), F32)],
+        + [pltpu.HBM((2 * size, half), F32)],
         "near_grads",
-        mib=14,
+        mib=20,
         place=place,
-        out_specs=[hbm()] * 3 + [vmem()],
-        scratch=[pltpu.VMEM((3, half, size), F32), pltpu.SemaphoreType.DMA((3 * PIECES,))],
+        specs=[hbm()] * 6,
+        out_specs=[hbm()] * 3,
+        scratch=[
+            pltpu.VMEM((2, slots, half), BF16),
+            pltpu.VMEM((3, slots, half), BF16),
+            pltpu.VMEM((3, half, size), F32),
+            pltpu.SemaphoreType.DMA((5,)),
+            pltpu.SemaphoreType.DMA((3 * PIECES,)),
+        ],
     )
 
 
 def fill_kernel(
-    place_ref, gate_in, up_in, down_in, gate_old, up_old, down_old, gate_out, up_out, down_out, wide, sem
+    place_ref, gate_in, up_in, down_in, gate_old, up_old, down_old,
+    gate_out, up_out, down_out, done_ref, away, wide, in_sem, sem,
 ):
     size = gate_in.shape[1]
     there = pl.multiple_of((1 - place_ref[2]) * size, LANES)
@@ -812,53 +908,57 @@
         up_out.at[:, pl.ds(there, size)],
         down_out.at[pl.ds(there, size), :],
     )
+    loads = [
+        pieces(a, away.at[n], in_sem, n * PIECES) for n, a in enumerate((gate_in, up_in, down_in))
+    ]
     results = [pieces(wide.at[n], a, sem, n * PIECES) for n, a in enumerate(places)]
     deep = wide.shape[1] // PIECES
-    for n, away in enumerate((gate_in, up_in, down_in)):
+    done_ref[...] = jnp.zeros(done_ref.shape, F32)
+    for load in loads[0] + loads[1] + loads[2]:
+        load.start()
+    for n in range(3):
         for k in range(PIECES):
-            wide[n, k * deep : (k + 1) * deep] = away[k * deep : (k + 1) * deep].astype(F32)
+            loads[n][k].wait()
+            wide[n, k * deep : (k + 1) * deep] = away[n, k * deep : (k + 1) * deep].astype(F32)
             results[n][k].start()
     for copy in results[0] + results[1] + results[2]:
         copy.wait()
 
 
 def fill(place, away, grads):
-    size = away[0].shape[1]
+    shape = away[0].shape
     return pl.pallas_call(
         fill_kernel,
-        compiler_params=pltpu.CompilerParams(vmem_limit_bytes=12 * MIB),
+        compiler_params=pltpu.CompilerParams(vmem_limit_bytes=16 * MIB),
         cost_estimate=pl.CostEstimate(
-            flops=0, bytes_accessed=LANES, transcendentals=0
+            flops=100_000_000_000, bytes_accessed=LANES, transcendentals=0
         ),
         grid_spec=pltpu.PrefetchScalarGridSpec(
             num_scalar_prefetch=1,
             grid=(1,),
-            in_specs=[vmem()] * 3 + [hbm()] * 3,
-            out_specs=[hbm()] * 3,
+            in_specs=[hbm()] * 6,
+            out_specs=[hbm()] * 3 + [vmem()],
             scratch_shapes=[
-                pltpu.VMEM((3,) + away[0].shape, F32),
+                pltpu.VMEM((3,) + shape, BF16),
+                pltpu.VMEM((3,) + shape, F32),
+                pltpu.SemaphoreType.DMA((3 * PIECES,)),
                 pltpu.SemaphoreType.DMA((3 * PIECES,)),
             ],
         ),
-        out_shape=[pltpu.HBM(g.shape, F32) for g in grads],
+        out_shape=[pltpu.HBM(g.shape, F32) for g in grads] + [fast((8, LANES), F32)],
         input_output_aliases={4: 0, 5: 1, 6: 2},
         name="fill",
-    )(place, *[near(a) for a in away], *grads)
-
-
-def weight_grads(place, column, size, normed, ggp, gup, hg, cots, after):
-    if lax.axis_size("rep") == 2:
-        *far, a, b, c, d, e = far_grads(normed, ggp, gup, hg, cots[0], cots[1], after)
-        away = [other_core(f) for f in far]
-        *grads, done = near_grads(place, a, b, c, d, e)
-        return fill(place, away, grads), done
+    )(place, *[far_off(a) for a in away], *grads)
+
+
+def gathered_grads(column, size, normed, ggp, gup, hg, cot):
     grads = []
     for g in (ggp[:, :size], gup[:, :size]):
         term = jnp.roll(t_mm(normed, g).astype(BF16), column, 0)
         grads.append(lax.all_to_all(term, "rep", split_axis=0, concat_axis=1, tiled=True))
-    term = jnp.roll(t_mm(hg[:, :size], cots[0]).astype(BF16), column, 1)
+    term = jnp.roll(t_mm(hg[:, :size], cot).astype(BF16), column, 1)
     grads.append(lax.all_to_all(term, "rep", split_axis=1, concat_axis=0, tiled=True))
-    return [g.astype(F32) for g in grads], jnp.zeros((8, LANES), F32)
+    return [g.astype(F32) for g in grads]
 
 
 def mixed_kernel(stem_ref, taken_ref, back_ref, after_ref, out_ref, *terms_refs):
@@ -917,11 +1017,11 @@
         given = lax.dynamic_slice_in_dim(grad_mixed, column, half, 1)
     copies = 1 if paired else shards
     packed, taken, cot = pack(place, latent, routes.T, given, experts, copies, half)
-    packed = exchange(packed)
+    arrived = exchange(packed)
 
     stem, gain, router = stem_weight, norm_gain[None, :], router_weight
     if cores == 2:
-        far = far_weights(place, gate_weight, up_weight, down_weight)
+        far = far_weights(place, gate_weight, up_weight, down_weight, packed)
         gate_parts, up_parts, down_parts = [
             (w, other_core(f)) for w, f in zip((gate_weight, up_weight, down_weight), far)
         ]
@@ -937,28 +1037,30 @@
         gain = jnp.roll(gain, -column, 1)
         router = jnp.roll(router, -column, 0)
 
-    inner, outer, stem, gain = gather_weights(
-        place, stem, gain, router, gate_parts, up_parts, down_parts
-    )
-    same_cot, image = unpack(packed, half, channels + 2)
+    small = small_params(place, stem, gain, router, packed, cores == 2)
+    same_cot, image = unpack(arrived, half, channels + 2, small[1])
+    size = down_parts[-1].shape[0]
+    gathered = gather(place, small, gate_parts, size)
     if paired:
-        image = weave(place, image, other_shard(image), gain)
+        joined = other_core(same_cot)
+        image = weave(place, image, other_shard(image), joined, gathered[1])
         cots = [same_cot, other_shard(same_cot)]
-        cots = [cots, [other_core(c) for c in cots]]
-        outs = [(k * slots // 2, slots // 2, n * half, half) for n in range(2) for k in range(2)]
+        cots = [cots, [joined, other_core(cots[1])]]
     elif cores == 2:
         cots = [[same_cot], [other_core(same_cot)]]
-        outs = [(0, GROUP * CAP, n * half, half) for n in range(2)]
     else:
         joined = lax.all_gather(same_cot, "rep", axis=1, tiled=True)
         cots = [[jnp.roll(joined, -column, 1)]]
-        outs = [(0, GROUP * CAP, 0, stem.shape[1])]
-    normed, own_stem, _, value, meta, coef, sel, pg, pu, *outs = forward(
-        place, image, stem, gain, inner, outer, half, outs, paired, width, experts
-    )
+    weights = list(up_parts) + list(down_parts)
+    columns = [w.shape[1] for w in down_parts]
+    kept, own_stem, normed, value, meta, coef, sel, pg, pu, hidden, inner, outer, *outs = forward(
+        place, image, gathered, weights, size, half, columns, paired, width, experts
+    )
+    stem, gain, _ = gathered
     if paired:
-        over = other_shard(add_up(outs[1], other_core(outs[3])))
-        own, away = outs[0], other_core(outs[2])
+        own, away = outputs(meta, hidden, outer)
+        over = other_shard(add_up(outs[0], other_core(outs[1]), own))
+        away = other_core(away)
     elif cores == 2:
         own, away = outs[0], other_core(outs[1])
         over = own
@@ -967,20 +1069,29 @@
         own = lax.psum_scatter(turned, "rep", scatter_dimension=1, tiled=True)
         away = over = jnp.zeros_like(own)
     acts = [value, meta, coef, pg, pu]
-    ggp, gup, hg, *cots, proj = backward(stem, gain, inner, outer, acts, cots, experts)
-    lat_terms = to_image(place, proj, sel, stem, cot, paired, width, channels)
-
-    sent = pack_back(place, own, away, over, lat_terms, paired)
+    ggp, gup, hg, *held, proj, ggp_here, gup_here, hg_here = backward(
+        stem, gain, inner, outer, acts, cots, experts
+    )
+    terms = to_image(place, proj, sel, stem, cot, paired, width, channels)
+    terms_over = other_shard(terms[1]) if paired else terms[0]
+    if cores == 2:
+        far = far_grads(normed, ggp_here, gup_here, hg_here, cots[1])
+        away_grads = [other_core(f) for f in far]
+
+    after = far[0] if cores == 2 else own
+    sent = pack_back(own, away, over, terms[0], terms_over, after, paired)
     back = exchange(sent)
 
-    size = gate_weight.shape[1] // cores
-    grads, done = weight_grads(place, column, size, normed, ggp, gup, hg, cots, sent)
+    if cores == 2:
+        grads = near_grads(place, kept, ggp, gup, hg, held[0], sent)
+        *grads, done = fill(place, away_grads, grads)
+    else:
+        done = jnp.zeros((8, LANES), F32)
+        size = gate_weight.shape[1] // cores
+        grads = gathered_grads(column, size, kept, ggp, gup, hg, held[0])
     grad_gate, grad_up, grad_down = grads
 
-    mixed, *lat_sums = mix(own_stem, taken, back, done, channels)
-    lat_sum = lat_sums[0]
-    if paired:
-        lat_sum = add_up(lat_sum, other_shard(lat_sums[1]))
+    mixed, lat_sum = mix(own_stem, taken, back, done, channels)
     if cores == 2:
         mixed, grad_latent = join(
             place, mixed, other_core(mixed), lat_sum, other_core(lat_sum), rows_here

time: 95.1 us -> 83.3 us (0.88)
  waiting for transfers between devices: 22.5 us -> 11.7 us
    pallas_call x15, Pallas kernels: 46.2 us -> 37.5 us  [kernel_call(): call(kernel, flops, moved, mib, grid_spec=pltpu.PrefetchScalarGridSpec(nu...]
    pallas_call x0 -> x1, Pallas kernels: none -> 8.18 us  [forward(): pl.pallas_call(functools.partial(forward_kernel, paired, parts, width, ex...]
    all_to_all x2, waiting for transfers between devices: 15.7 us -> 9.35 us  [exchange(): lax.all_to_all(values, 'exp', split_axis=0, concat_axis=0, tiled=True, ax...]
    ppermute x4, waiting for transfers between devices: 4.77 us -> 1.4 us  [other_shard(): lax.ppermute(values, 'exp', [(i, i ^ 1) for i in range(lax.axis_size('exp...]
    ppermute x12, waiting for transfers between devices: 2.03 us -> 0.97 us  [other_core(): return lax.ppermute(values, 'rep', [(0, 1), (1, 0)])]
    ppermute x4, starting transfers between devices: 5.22 us -> 4.25 us  [other_shard(): lax.ppermute(values, 'exp', [(i, i ^ 1) for i in range(lax.axis_size('exp...]
  transfers between devices with their start and end apart: 18 -> 18, of which waited for: 6 -> 4; matrix products, arithmetic and copies ran while one was open for 2% -> 2% of each run, Pallas kernels for 43% -> 54%
where the time goes in v2:
time: 83.3 us; the launch traced here: 82.9 us
  Pallas kernels  50.4 us (61%)
  starting transfers between devices  18.3 us (22%)
  waiting for transfers between devices  11.7 us (14%)
  local copies, waits for them, and re-layouts  1.54 us (2%)
  between operations  0.89 us (1%)
    pallas_call x15, Pallas kernels, kernel_call(): call(kernel, flops, moved, mib, grid_spec=pltpu.PrefetchScalarGridSpec(nu...  37.5 us
    all_to_all x2, starting transfers between devices, exchange(): lax.all_to_all(values, 'exp', split_axis=0, concat_axis=0, tiled=True, ax...  11.4 us
    all_to_all x2, waiting for transfers between devices, exchange(): lax.all_to_all(values, 'exp', split_axis=0, concat_axis=0, tiled=True, ax...  9.35 us
    pallas_call x1, Pallas kernels, forward(): pl.pallas_call(functools.partial(forward_kernel, paired, parts, width, ex...  8.18 us
    pallas_call x1, Pallas kernels, fill(): pl.pallas_call(fill_kernel, compiler_params=pltpu.CompilerParams(vmem_lim...  4.65 us
    ppermute x4, starting transfers between devices, other_shard(): lax.ppermute(values, 'exp', [(i, i ^ 1) for i in range(lax.axis_size('exp...  4.25 us
    ppermute x12, starting transfers between devices, other_core(): return lax.ppermute(values, 'rep', [(0, 1), (1, 0)])  2.58 us
  transfers between devices with their start and end apart: 18, of which 4 were waited for; matrix products, arithmetic and copies ran while one was open for 2% of the time, Pallas kernels for 54%

profile of v2, /device:TPU:0, one launch (start us, length us, event | category | flops | bytes accessed | tf_op | source)
XLA Modules:
  0.0 82.9 jit_solution(4188148129071794579)
XLA Ops:
  0.6 0.1 pad_add_fusion.place_ref
  0.7 2.8 %pack.1 = (bf16[8,258,128]{2,1,0:T(8,128)(2,1)}, bf16[320,128]{1,0:T(8,128)(2,1)}, bf16[128,768]{1,0:T(8,128)(2,1)}) custom-call(s32[3]{0:T(128)S(1)} %pad_add_fusion.place_ref, bf16[2,16,64]{2,1,0:T(8,128)(2,1)} %latent_ref.1, s32[2,128]{1,0:T(2,128)} %bitcast.4, bf16[128,1536]{1,0:T(8,128)(2,1)} %cot_ref.1), custom_call_target="tpu_custom_call" | custom-call | flops 62914560 | bytes 1056768 | tf_op jit(solution)/shard_map/pack/pallas_call | solution.py:107
  3.5 7.3 %all-to-all-start = ((bf16[8,258,128]{2,1,0:T(8,128)(2,1)}), bf16[8,258,128]{2,1,0:T(8,128)(2,1)S(1)}, u32[]{:S(2)}, u32[]{:S(2)}) async-start(bf16[8,258,128]{2,1,0:T(8,128)(2,1)} %get-tuple-element.59.after.after_ref), calls=%async_computation | async-start | bytes 1081344 | tf_op jit(solution)/shard_map/all_to_all | solution.py:79
  10.8 0.0 copy-start.4
  10.8 0.0 copy-start.3
  10.8 3.6 %far_weights.1 = (bf16[768,768]{1,0:T(8,128)(2,1)}, bf16[768,768]{1,0:T(8,128)(2,1)S(1)}, bf16[768,768]{1,0:T(8,128)(2,1)S(1)}) custom-call(s32[3]{0:T(128)S(1)} %pad_add_fusion.place_ref, bf16[768,1536]{1,0:T(8,128)(2,1)} %refs_0_.2, bf16[768,1536]{1,0:T(8,128)(2,1)} %refs_0_.3, bf16[1536,768]{1,0:T(8,128)(2,1)} %refs_2_.1, ...), custom_call_target="tpu_custom_call" | custom-call | bytes 128 | tf_op jit(solution)/shard_map/far_weights/pallas_call | solution.py:107
  14.4 0.1 collective-permute-start.2
  14.5 0.5 collective-permute-start.3
  15.0 0.1 collective-permute-start.4
  15.1 0.0 copy-done.4
  15.1 0.6 broadcast_in_dim.3.gain_in
  15.7 0.0 copy-done.3
  15.7 0.9 %copy.18.router_in = bf16[1536,8]{1,0:T(8,128)(2,1)} copy(bf16[1536,8]{0,1:T(8,128)(2,1)S(1)} %copy-done.3) | data formatting | bytes 49152 | tf_op args[3]
  16.6 2.8 %params.1 = (bf16[144,1536]{1,0:T(8,128)(2,1)}, f32[1,1536]{1,0:T(1,128)}, bf16[1536,128]{1,0:T(8,128)(2,1)}) custom-call(s32[3]{0:T(128)S(1)} %pad_add_fusion.place_ref, bf16[144,1536]{1,0:T(8,128)(2,1)} %stem_in.1, f32[1,1536]{1,0:T(1,128)} %broadcast_in_dim.3.gain_in, bf16[1536,8]{1,0:T(8,128)(2,1)} %copy.18.router_in, ...), custom_call_target="tpu_custom_call" | custom-call | bytes 128 | tf_op jit(solution)/shard_map/params/pallas_call | solution.py:107
  19.4 6.2 %all-to-all-done.packed_ref = bf16[8,258,128]{2,1,0:T(8,128)(2,1)S(1)} async-done(((bf16[8,258,128]{2,1,0:T(8,128)(2,1)}), bf16[8,258,128]{2,1,0:T(8,128)(2,1)S(1)}, u32[]{:S(2)}, u32[]{:S(2)}) %all-to-all-start) | async-done | bytes 528416 | tf_op jit(solution)/shard_map/all_to_all | solution.py:79
  25.7 0.1 collective-permute-start.1
  25.7 1.6 %collective-permute-start = (bf16[8,18,128]{2,1,0:T(8,128)(2,1)S(1)}, bf16[8,18,128]{2,1,0:T(8,128)(2,1)S(1)}, u32[]{:S(2)}, u32[]{:S(2)}) collective-permute-start(bf16[8,18,128]{2,1,0:T(8,128)(2,1)S(1)} %get-tuple-element.61.same_ref), channel_id=1, source_target_pairs={{0,2},{2,0},{4,6},{6,4},{8,10},{10,8},{12,14},{14,12},{16,18},{18,... | collective-permute-start | bytes 110600 | tf_op jit(solution)/shard_map/ppermute | solution.py:70
  27.3 0.0 collective-permute-done.2.refs_1_
  27.3 0.5 collective-permute-start.8
  27.8 2.5 %gather.1 = (bf16[144,1536]{1,0:T(8,128)(2,1)S(1)}, f32[1,1536]{1,0:T(1,128)S(1)}, bf16[1536,1664]{1,0:T(8,128)(2,1)S(1)}) custom-call(s32[3]{0:T(128)S(1)} %pad_add_fusion.place_ref, bf16[768,1536]{1,0:T(8,128)(2,1)} %refs_0_.2, bf16[768,768]{1,0:T(8,128)(2,1)} %collective-permute-done.2.refs_1_, bf16[144,1536]{1,0:T(8,128)(2,1)} %get-tuple-element.64.refs_2_, ...), custom_call_target="tpu_custom_call" | custom-call | bytes 128 | tf_op jit(solution)/shard_map/gather/pallas_call | solution.py:107
  30.3 0.0 collective-permute-done.other_ref
  30.3 0.0 collective-permute-done.1.after_ref.refs_2_.refs_0_
  30.3 0.6 weave.1.image_ref
  30.9 0.0 collective-permute-done.3.refs_1_
  30.9 0.0 collective-permute-done.4.refs_3_
  30.9 8.2 %forward.1 = (bf16[640,1536]{1,0:T(8,128)(2,1)}, bf16[128,768]{1,0:T(8,128)(2,1)}, bf16[640,1536]{1,0:T(8,128)(2,1)S(1)}, bf16[640,1536]{1,0:T(8,128)(2,1)S(1)},...) custom-call(s32[3]{0:T(128)S(1)} %pad_add_fusion.place_ref, ...), custom_call_target="tpu_custom_call", output_to_operand_aliasing={{10}: (4, {})} | custom-call | flops 99999997952 | bytes 128 | tf_op jit(solution)/shard_map/forward/pallas_call | solution.py:623
  39.1 0.1 collective-permute-start.6
  39.2 1.4 %collective-permute-done.8.refs_1_ = bf16[320,768]{1,0:T(8,128)(2,1)S(1)} collective-permute-done((bf16[320,768]{1,0:T(8,128)(2,1)S(1)}, bf16[320,768]{1,0:T(8,128)(2,1)S(1)}, u32[]{:S(2)}, u32[]{:S(2)}) %collective-permute-start.8) | collective-permute-done | bytes 491552 | tf_op jit(solution)/shard_map/ppermute | solution.py:70
  40.6 0.0 collective-permute-start.9
  40.6 0.9 %outputs.1 = (bf16[320,768]{1,0:T(8,128)(2,1)S(1)}, bf16[320,768]{1,0:T(8,128)(2,1)S(1)}) custom-call(f32[640,128]{1,0:T(8,128)S(1)} %get-tuple-element.73.meta_ref, bf16[640,768]{1,0:T(8,128)(2,1)S(1)} %get-tuple-element.74.hidden_ref, bf16[768,1536]{1,0:T(8,128)(2,1)S(1)} %get-tuple-element.75.outer), custom_call_target="tpu_custom_call" | custom-call | bytes 128 | tf_op jit(solution)/shard_map/outputs/pallas_call | solution.py:107
  41.5 0.6 collective-permute-start.5
  42.1 0.0 collective-permute-done.6.b_ref
  42.1 0.1 add_up.1
  42.2 1.4 %collective-permute-start.7 = (bf16[320,768]{1,0:T(8,128)(2,1)S(1)}, bf16[320,768]{1,0:T(8,128)(2,1)S(1)}, u32[]{:S(2)}, u32[]{:S(2)}) collective-permute-start(bf16[320,768]{1,0:T(8,128)(2,1)S(1)} %add_up.1), channel_id=1, source_target_pairs={{0,2},{2,0},{4,6},{6,4},{8,10},{10,8},{12,14},{14,12},{16,18},{18,... | collective-permute-start | bytes 1474568 | tf_op jit(solution)/shard_map/ppermute | solution.py:70
  43.6 0.0 collective-permute-done.9.refs_3_.refs_1_
  43.6 8.9 %backward.1 = (bf16[640,768]{1,0:T(8,128)(2,1)}, bf16[640,768]{1,0:T(8,128)(2,1)}, bf16[640,768]{1,0:T(8,128)(2,1)}, bf16[640,768]{1,0:T(8,128)(2,1)}, bf16[640,...) custom-call(bf16[144,1536]{1,0:T(8,128)(2,1)S(1)} %get-tuple-element, ...), custom_call_target="tpu_custom_call" | custom-call | flops 6039797760 | bytes 16908288 | tf_op jit(solution)/shard_map/backward/pallas_call | solution.py:107
  52.5 0.0 copy-done
  52.6 1.1 %to_image.1 = (f32[8,16,128]{2,1,0:T(8,128)S(1)}, bf16[8,16,128]{2,1,0:T(8,128)(2,1)S(1)}) custom-call(s32[3]{0:T(128)S(1)} %pad_add_fusion.place_ref, bf16[640,144]{1,0:T(8,128)(2,1)S(1)} %get-tuple-element.85.proj_ref, bf16[8,80,256]{2,1,0:T(8,128)(2,1)S(1)} %get-tuple-element.86.sel_ref, bf16[144,1536]{1,0:T(8,128)(2,1)S(1)} %get-tuple-element.67.stem_ref, ...), custom_call_target="tpu_custom_call" | custom-call | flops 47185920 | bytes 1179648 | tf_op jit(solution)/shard_map/to_image/pallas_call | solution.py:107
  53.7 0.8 collective-permute-start.10
  54.5 3.0 %far_grads.1 = (bf16[768,768]{1,0:T(8,128)(2,1)S(1)}, bf16[768,768]{1,0:T(8,128)(2,1)S(1)}, bf16[768,768]{1,0:T(8,128)(2,1)S(1)}) custom-call(bf16[640,1536]{1,0:T(8,128)(2,1)S(1)} %get-tuple-element.90.normed, bf16[640,768]{1,0:T(8,128)(2,1)S(1)} %get-tuple-element.91.ggp, bf16[640,768]{1,0:T(8,128)(2,1)S(1)} %get-tuple-element.92.gup, ...), custom_call_target="tpu_custom_call" | custom-call | flops 2264924160 | bytes 9830400 | tf_op jit(solution)/shard_map/far_grads/pallas_call | solution.py:107
  57.4 0.1 collective-permute-start.12
  57.5 0.5 collective-permute-start.13
  58.0 0.0 collective-permute-done.5.b_ref
  58.0 0.1 collective-permute-start.11
  58.1 0.0 collective-permute-done.10.over_ref
  58.1 0.0 collective-permute-done.7.c_ref
  58.1 1.0 %pack_back.1.after_ref = bf16[8,256,128]{2,1,0:T(8,128)(2,1)} custom-call(bf16[320,768]{1,0:T(8,128)(2,1)S(1)} %get-tuple-element.76.after_ref.a_ref, bf16[320,768]{1,0:T(8,128)(2,1)S(1)} %collective-permute-done.5.b_ref, bf16[320,768]{1,0:T(8,128)(2,1)S(1)} %collective-permute-done.7.c_ref, f32[8,16,128]{2,1,0:T(8,128)S(1)} %get-tuple-element.88.terms_ref, ...), custom_call_target="tpu_custom_call" | custom-call | flops 245760 | bytes 1966080 | tf_op jit(solution)/shard_map/pack_back/pallas_call | solution.py:107
  59.1 4.2 %all-to-all-start.1 = ((bf16[8,256,128]{2,1,0:T(8,128)(2,1)}), bf16[8,256,128]{2,1,0:T(8,128)(2,1)}, u32[]{:S(2)}, u32[]{:S(2)}) async-start(bf16[8,256,128]{2,1,0:T(8,128)(2,1)} %pack_back.1.after_ref), calls=%async_computation.1 | async-start | bytes 1048576 | tf_op jit(solution)/shard_map/all_to_all | solution.py:79
  63.3 7.5 %near_grads.1 = (f32[768,1536]{1,0:T(8,128)}, f32[768,1536]{1,0:T(8,128)}, f32[1536,768]{1,0:T(8,128)}) custom-call(s32[3]{0:T(128)S(1)} %pad_add_fusion.place_ref, bf16[640,1536]{1,0:T(8,128)(2,1)} %get-tuple-element.97.normed, bf16[640,768]{1,0:T(8,128)(2,1)} %get-tuple-element.98.ggp, bf16[640,768]{1,0:T(8,128)(2,1)} %get-tuple-element.99.gup, ...), custom_call_target="tpu_custom_call" | custom-call | flops 99999997952 | bytes 128 | tf_op jit(solution)/shard_map/near_grads/pallas_call | solution.py:107
  70.8 0.0 collective-permute-done.12.up_in
  70.8 0.0 collective-permute-done.13.down_in
  70.8 0.0 collective-permute-done.11.gate_in
  70.8 0.0 copy-start.1
  70.9 0.0 copy-start.2
  70.9 4.7 %fill.1 = (f32[768,1536]{1,0:T(8,128)}, f32[768,1536]{1,0:T(8,128)}, f32[1536,768]{1,0:T(8,128)}, f32[8,128]{1,0:T(8,128)S(1)}) custom-call(s32[3]{0:T(128)S(1)} %pad_add_fusion.place_ref, bf16[768,768]{1,0:T(8,128)(2,1)} %collective-permute-done.11.gate_in, ...), custom_call_target="tpu_custom_call", output_to_operand_aliasing={{0}: (4, {}), {1}: (5, {}), {2}: (6, {})} | custom-call | flops 99999997952 | bytes 128 | tf_op jit(solution)/shard_map/fill/pallas_call | solution.py:930
  75.5 3.1 %all-to-all-done.1.back_ref = bf16[8,256,128]{2,1,0:T(8,128)(2,1)} async-done(((bf16[8,256,128]{2,1,0:T(8,128)(2,1)}), bf16[8,256,128]{2,1,0:T(8,128)(2,1)}, u32[]{:S(2)}, u32[]{:S(2)}) %all-to-all-start.1) | async-done | bytes 524320 | tf_op jit(solution)/shard_map/all_to_all | solution.py:79
  78.7 0.0 copy-done.1
  78.7 0.0 copy-done.2
  78.7 1.3 %mixed.1 = (bf16[128,768]{1,0:T(8,128)(2,1)S(1)}, f32[16,128]{1,0:T(8,128)S(1)}) custom-call(bf16[128,768]{1,0:T(8,128)(2,1)S(1)} %copy-done.1, bf16[320,128]{1,0:T(8,128)(2,1)S(1)} %copy-done.2, bf16[8,256,128]{2,1,0:T(8,128)(2,1)} %all-to-all-done.1.back_ref, f32[8,128]{1,0:T(8,128)S(1)} %get-tuple-element.105.after_ref), custom_call_target="tpu_custom_call" | custom-call | flops 62914560 | bytes 524288 | tf_op jit(solution)/shard_map/mixed/pallas_call | solution.py:107
  80.0 0.1 collective-permute-start.14
  80.1 0.5 collective-permute-start.15
  80.6 0.9 %collective-permute-done.15.b_ref = f32[16,128]{1,0:T(8,128)S(1)} collective-permute-done((f32[16,128]{1,0:T(8,128)S(1)}, f32[16,128]{1,0:T(8,128)S(1)}, u32[]{:S(2)}, u32[]{:S(2)}) %collective-permute-start.15) | collective-permute-done | bytes 8224 | tf_op jit(solution)/shard_map/ppermute | solution.py:66
  81.5 0.0 collective-permute-done.14.away_ref
  81.5 1.3 %join.1 = (bf16[128,1536]{1,0:T(8,128)(2,1)}, f32[2,16,64]{2,1,0:T(8,128)}) custom-call(s32[3]{0:T(128)S(1)} %pad_add_fusion.place_ref, bf16[128,768]{1,0:T(8,128)(2,1)S(1)} %get-tuple-element.106.own_ref, bf16[128,768]{1,0:T(8,128)(2,1)S(1)} %collective-permute-done.14.away_ref, f32[16,128]{1,0:T(8,128)S(1)} %get-tuple-element.107.a_ref, ...), custom_call_target="tpu_custom_call" | custom-call | bytes 786432 | tf_op jit(solution)/shard_map/join/pallas_call | solution.py:107
  (2 shorter events, 0.0 us)
Async XLA Ops:
  3.5 22.1 %all-to-all-start = ((bf16[8,258,128]{2,1,0:T(8,128)(2,1)}), bf16[8,258,128]{2,1,0:T(8,128)(2,1)S(1)}, u32[]{:S(2)}, u32[]{:S(2)}) async-start(bf16[8,258,128]{2,1,0:T(8,128)(2,1)} %get-tuple-element.59.after.after_ref), calls=%async_computation | async-start | bytes 1081344 | tf_op jit(solution)/shard_map/all_to_all | solution.py:79
  10.8 4.3 %copy-start.4 = (f32[1536]{0:T(1024)S(1)}, f32[1536]{0:T(1024)}, u32[]{:S(2)}) copy-start(f32[1536]{0:T(1024)} %param.11) | copy-start | bytes 18436
  10.8 4.9 %copy-start.3 = (bf16[1536,8]{0,1:T(8,128)(2,1)S(1)}, bf16[1536,8]{0,1:T(8,128)(2,1)}, u32[]{:S(2)}) copy-start(bf16[1536,8]{0,1:T(8,128)(2,1)} %param.12) | copy-start | bytes 73732
  14.4 12.9 %collective-permute-start.2 = (bf16[768,768]{1,0:T(8,128)(2,1)}, bf16[768,768]{1,0:T(8,128)(2,1)}, u32[]{:S(2)}, u32[]{:S(2)}) collective-permute-start(bf16[768,768]{1,0:T(8,128)(2,1)} %get-tuple-element.63), channel_id=1, source_target_pairs={{0,1},{1,0},{2,3},{3,2},{4,5},{5,4},{6,7},{7,6},{8,9},{9,8},{10,11... | collective-permute-start | bytes 3538952 | tf_op jit(solution)/shard_map/ppermute | solution.py:66
  14.5 16.4 %collective-permute-start.3 = (bf16[768,768]{1,0:T(8,128)(2,1)S(1)}, bf16[768,768]{1,0:T(8,128)(2,1)}, u32[]{:S(2)}, u32[]{:S(2)}) collective-permute-start(bf16[768,768]{1,0:T(8,128)(2,1)S(1)} %get-tuple-element.69), channel_id=1, source_target_pairs={{0,1},{1,0},{2,3},{3,2},{4,5},{5,4},{6,7},{7,6},{8,9},{9,8},{10,11... | collective-permute-start | bytes 3538952 | tf_op jit(solution)/shard_map/ppermute | solution.py:66
  15.0 15.9 %collective-permute-start.4 = (bf16[768,768]{1,0:T(8,128)(2,1)S(1)}, bf16[768,768]{1,0:T(8,128)(2,1)}, u32[]{:S(2)}, u32[]{:S(2)}) collective-permute-start(bf16[768,768]{1,0:T(8,128)(2,1)S(1)} %get-tuple-element.70), channel_id=1, source_target_pairs={{0,1},{1,0},{2,3},{3,2},{4,5},{5,4},{6,7},{7,6},{8,9},{9,8},{10,11... | collective-permute-start | bytes 3538952 | tf_op jit(solution)/shard_map/ppermute | solution.py:66
  25.7 4.7 %collective-permute-start.1 = (bf16[320,768]{1,0:T(8,128)(2,1)S(1)}, bf16[320,768]{1,0:T(8,128)(2,1)S(1)}, u32[]{:S(2)}, u32[]{:S(2)}) collective-permute-start(bf16[320,768]{1,0:T(8,128)(2,1)S(1)} %get-tuple-element.62.refs_0_), channel_id=1, source_target_pairs={{0,1},{1,0},{2,3},{3,2},{4,5},{5,4},{6,7},{7,6},{8,9},{9,8},{10,11... | collective-permute-start | bytes 1474568 | tf_op jit(solution)/shard_map/ppermute | solution.py:66
  25.7 4.6 %collective-permute-start = (bf16[8,18,128]{2,1,0:T(8,128)(2,1)S(1)}, bf16[8,18,128]{2,1,0:T(8,128)(2,1)S(1)}, u32[]{:S(2)}, u32[]{:S(2)}) collective-permute-start(bf16[8,18,128]{2,1,0:T(8,128)(2,1)S(1)} %get-tuple-element.61.same_ref), channel_id=1, source_target_pairs={{0,2},{2,0},{4,6},{6,4},{8,10},{10,8},{12,14},{14,12},{16,18},{18,... | collective-permute-start | bytes 110600 | tf_op jit(solution)/shard_map/ppermute | solution.py:70
  27.3 13.3 %collective-permute-start.8 = (bf16[320,768]{1,0:T(8,128)(2,1)S(1)}, bf16[320,768]{1,0:T(8,128)(2,1)S(1)}, u32[]{:S(2)}, u32[]{:S(2)}) collective-permute-start(bf16[320,768]{1,0:T(8,128)(2,1)S(1)} %get-tuple-element.62.refs_0_), channel_id=1, source_target_pairs={{0,2},{2,0},{4,6},{6,4},{8,10},{10,8},{12,14},{14,12},{16,18},{18,... | collective-permute-start | bytes 1474568 | tf_op jit(solution)/shard_map/ppermute | solution.py:70
  39.1 3.0 %collective-permute-start.6 = (bf16[320,768]{1,0:T(8,128)(2,1)S(1)}, bf16[320,768]{1,0:T(8,128)(2,1)S(1)}, u32[]{:S(2)}, u32[]{:S(2)}) collective-permute-start(bf16[320,768]{1,0:T(8,128)(2,1)S(1)} %get-tuple-element.79), channel_id=1, source_target_pairs={{0,1},{1,0},{2,3},{3,2},{4,5},{5,4},{6,7},{7,6},{8,9},{9,8},{10,11... | collective-permute-start | bytes 1474568 | tf_op jit(solution)/shard_map/ppermute | solution.py:66
  40.6 3.0 %collective-permute-start.9 = (bf16[320,768]{1,0:T(8,128)(2,1)S(1)}, bf16[320,768]{1,0:T(8,128)(2,1)S(1)}, u32[]{:S(2)}, u32[]{:S(2)}) collective-permute-start(bf16[320,768]{1,0:T(8,128)(2,1)S(1)} %collective-permute-done.8.refs_1_), channel_id=1, source_target_pairs={{0,1},{1,0},{2,3},{3,2},{4,5},{5,4},{6,7},{7,6},{8,9},{9,8},{10,11... | collective-permute-start | bytes 1474568 | tf_op jit(solution)/shard_map/ppermute | solution.py:66
  41.5 16.5 %collective-permute-start.5 = (bf16[320,768]{1,0:T(8,128)(2,1)S(1)}, bf16[320,768]{1,0:T(8,128)(2,1)S(1)}, u32[]{:S(2)}, u32[]{:S(2)}) collective-permute-start(bf16[320,768]{1,0:T(8,128)(2,1)S(1)} %get-tuple-element.77), channel_id=1, source_target_pairs={{0,1},{1,0},{2,3},{3,2},{4,5},{5,4},{6,7},{7,6},{8,9},{9,8},{10,11... | collective-permute-start | bytes 1474568 | tf_op jit(solution)/shard_map/ppermute | solution.py:66
  42.2 15.9 %collective-permute-start.7 = (bf16[320,768]{1,0:T(8,128)(2,1)S(1)}, bf16[320,768]{1,0:T(8,128)(2,1)S(1)}, u32[]{:S(2)}, u32[]{:S(2)}) collective-permute-start(bf16[320,768]{1,0:T(8,128)(2,1)S(1)} %add_up.1), channel_id=1, source_target_pairs={{0,2},{2,0},{4,6},{6,4},{8,10},{10,8},{12,14},{14,12},{16,18},{18,... | collective-permute-start | bytes 1474568 | tf_op jit(solution)/shard_map/ppermute | solution.py:70
  43.6 8.9 %copy-start = (bf16[128,768]{1,0:T(8,128)(2,1)S(1)}, bf16[128,768]{1,0:T(8,128)(2,1)}, u32[]{:S(2)}) copy-start(bf16[128,768]{1,0:T(8,128)(2,1)} %get-tuple-element.87.cot_ref) | copy-start | bytes 589828
  53.7 4.4 %collective-permute-start.10 = (bf16[8,16,128]{2,1,0:T(8,128)(2,1)S(1)}, bf16[8,16,128]{2,1,0:T(8,128)(2,1)S(1)}, u32[]{:S(2)}, u32[]{:S(2)}) collective-permute-start(bf16[8,16,128]{2,1,0:T(8,128)(2,1)S(1)} %get-tuple-element.89), channel_id=1, source_target_pairs={{0,2},{2,0},{4,6},{6,4},{8,10},{10,8},{12,14},{14,12},{16,18},{18,... | collective-permute-start | bytes 98312 | tf_op jit(solution)/shard_map/ppermute | solution.py:70
  57.4 13.4 %collective-permute-start.12 = (bf16[768,768]{1,0:T(8,128)(2,1)S(1)}, bf16[768,768]{1,0:T(8,128)(2,1)}, u32[]{:S(2)}, u32[]{:S(2)}) collective-permute-start(bf16[768,768]{1,0:T(8,128)(2,1)S(1)} %get-tuple-element.95), channel_id=1, source_target_pairs={{0,1},{1,0},{2,3},{3,2},{4,5},{5,4},{6,7},{7,6},{8,9},{9,8},{10,11... | collective-permute-start | bytes 3538952 | tf_op jit(solution)/shard_map/ppermute | solution.py:66
  57.5 13.3 %collective-permute-start.13 = (bf16[768,768]{1,0:T(8,128)(2,1)S(1)}, bf16[768,768]{1,0:T(8,128)(2,1)}, u32[]{:S(2)}, u32[]{:S(2)}) collective-permute-start(bf16[768,768]{1,0:T(8,128)(2,1)S(1)} %get-tuple-element.96), channel_id=1, source_target_pairs={{0,1},{1,0},{2,3},{3,2},{4,5},{5,4},{6,7},{7,6},{8,9},{9,8},{10,11... | collective-permute-start | bytes 3538952 | tf_op jit(solution)/shard_map/ppermute | solution.py:66
  58.0 12.8 %collective-permute-start.11 = (bf16[768,768]{1,0:T(8,128)(2,1)S(1)}, bf16[768,768]{1,0:T(8,128)(2,1)}, u32[]{:S(2)}, u32[]{:S(2)}) collective-permute-start(bf16[768,768]{1,0:T(8,128)(2,1)S(1)} %get-tuple-element.94.after_ref), channel_id=1, source_target_pairs={{0,1},{1,0},{2,3},{3,2},{4,5},{5,4},{6,7},{7,6},{8,9},{9,8},{10,11... | collective-permute-start | bytes 3538952 | tf_op jit(solution)/shard_map/ppermute | solution.py:66
  59.1 19.6 %all-to-all-start.1 = ((bf16[8,256,128]{2,1,0:T(8,128)(2,1)}), bf16[8,256,128]{2,1,0:T(8,128)(2,1)}, u32[]{:S(2)}, u32[]{:S(2)}) async-start(bf16[8,256,128]{2,1,0:T(8,128)(2,1)} %pack_back.1.after_ref), calls=%async_computation.1 | async-start | bytes 1048576 | tf_op jit(solution)/shard_map/all_to_all | solution.py:79
  70.8 7.8 %copy-start.1 = (bf16[128,768]{1,0:T(8,128)(2,1)S(1)}, bf16[128,768]{1,0:T(8,128)(2,1)}, u32[]{:S(2)}) copy-start(bf16[128,768]{1,0:T(8,128)(2,1)} %get-tuple-element.71.stem_ref) | copy-start | bytes 589828
  70.9 7.8 %copy-start.2 = (bf16[320,128]{1,0:T(8,128)(2,1)S(1)}, bf16[320,128]{1,0:T(8,128)(2,1)}, u32[]{:S(2)}) copy-start(bf16[320,128]{1,0:T(8,128)(2,1)} %get-tuple-element.72.taken_ref) | copy-start | bytes 245764
  80.0 1.5 %collective-permute-start.14 = (bf16[128,768]{1,0:T(8,128)(2,1)S(1)}, bf16[128,768]{1,0:T(8,128)(2,1)S(1)}, u32[]{:S(2)}, u32[]{:S(2)}) collective-permute-start(bf16[128,768]{1,0:T(8,128)(2,1)S(1)} %get-tuple-element.106.own_ref), channel_id=1, source_target_pairs={{0,1},{1,0},{2,3},{3,2},{4,5},{5,4},{6,7},{7,6},{8,9},{9,8},{10,11... | collective-permute-start | bytes 589832 | tf_op jit(solution)/shard_map/ppermute | solution.py:66
  80.1 1.4 %collective-permute-start.15 = (f32[16,128]{1,0:T(8,128)S(1)}, f32[16,128]{1,0:T(8,128)S(1)}, u32[]{:S(2)}, u32[]{:S(2)}) collective-permute-start(f32[16,128]{1,0:T(8,128)S(1)} %get-tuple-element.107.a_ref), channel_id=1, source_target_pairs={{0,1},{1,0},{2,3},{3,2},{4,5},{5,4},{6,7},{7,6},{8,9},{9,8},{10,11... | collective-permute-start | bytes 24584 | tf_op jit(solution)/shard_map/ppermute | solution.py:66

commit v3 on v2

--- a/solution.py
+++ b/solution.py
@@ -134,17 +134,8 @@
     return jnp.concatenate(parts, axis=0)
 
 
-def pack_kernel(shards, half, place_ref, latent_ref, routes_ref, cot_ref, out_ref, taken_ref, here_ref):
-    rows_here, channels, width = latent_ref.shape
-    tok = rows_here * width
-    experts = out_ref.shape[0] // shards
-    cells = jnp.concatenate([latent_ref[r].astype(F32) for r in range(rows_here)], axis=1)
-    routes = routes_ref[...].astype(F32)
-    payload = jnp.concatenate([cells, routes], axis=0)
-    cot = cot_ref[...]
-    if cot.shape[1] != half:
-        cot = jnp.where(place_ref[2] == 0, cot[:, :half], cot[:, half:])
-    here_ref[...] = cot
+def own_selection(routes, experts):
+    tok = routes.shape[1]
     expert = lax.broadcasted_iota(jnp.int32, (experts, tok), 0).astype(F32)
     named = jnp.where((expert == routes[0:1]) | (expert == routes[1:2]), 1.0, 0.0)
     first = lax.broadcasted_iota(jnp.int32, (tok, tok), 0)
@@ -152,20 +143,40 @@
     before = jnp.where(first <= second, 1.0, 0.0).astype(BF16)
     at = mm(named.astype(BF16), before) - 1.0
     slot = lax.broadcasted_iota(jnp.int32, (CAP, tok), 0).astype(F32)
-    sel = [
+    return [
         jnp.where((at[e : e + 1] == slot) & (named[e : e + 1] > 0.0), 1.0, 0.0)
         for e in range(experts)
     ]
+
+
+def own_columns(cot, half):
+    if cot.shape[1] == half:
+        return cot
+    return jnp.where(lax.axis_index("rep") == 0, cot[:, :half], cot[:, half:])
+
+
+def pack_kernel(shards, half, latent_ref, routes_ref, cot_ref, out_ref, held, sem):
+    rows_here = latent_ref.shape[0]
+    experts = held.shape[0]
+    cells = jnp.concatenate([latent_ref[r].astype(F32) for r in range(rows_here)], axis=1)
+    routes = routes_ref[...].astype(F32)
+    payload = jnp.concatenate([cells, routes], axis=0)
+    sel = own_selection(routes, experts)
+    cot = own_columns(cot_ref[...], half)
     cots = mm(jnp.concatenate(sel, axis=0).astype(BF16), cot)
-    taken_ref[...] = jnp.concatenate([one for one in sel for _ in range(shards)], axis=0).astype(BF16)
+    copies = []
     for e in range(experts):
         slots = stacked(cots[e * CAP : (e + 1) * CAP])
-        packed = jnp.concatenate([slots, payload], axis=0).astype(BF16)
+        held[e] = jnp.concatenate([slots, payload], axis=0).astype(BF16)
         for n in range(shards):
-            out_ref[e * shards + n] = packed
-
-
-def pack(place, latent, routes_t, cot, experts, shards, half):
+            block = e * shards + n
+            copies.append(pltpu.make_async_copy(held.at[e], out_ref.at[block], sem.at[block]))
+            copies[-1].start()
+    for copy in copies:
+        copy.wait()
+
+
+def pack(latent, routes_t, cot, experts, shards, half):
     rows_here, channels, width = latent.shape
     top, tok = routes_t.shape
     blocks = experts * shards
@@ -176,20 +187,12 @@
         2 * blocks * CAP * tok * half,
         4 * blocks * depth * LANES,
         [far_off(a) for a in operands],
-        [
-            shape_of((blocks, depth, LANES), BF16),
-            pltpu.HBM((blocks * CAP, tok), BF16),
-            pltpu.HBM((tok, half), BF16),
-        ],
+        [pltpu.HBM((blocks, depth, LANES), BF16)],
         "pack",
-        place=place,
         specs=[whole(a.shape) for a in operands],
-        out_specs=[
-            whole((blocks, depth, LANES)),
-            whole((blocks * CAP, tok)),
-            whole((tok, half)),
-        ],
-    )
+        out_specs=[hbm()],
+        scratch=[pltpu.VMEM((experts, depth, LANES), BF16), pltpu.SemaphoreType.DMA((blocks,))],
+    )[0]
 
 
 def unpacked(ref, columns):
@@ -312,7 +315,7 @@
         far_kernel,
         0,
         LANES,
-        [far_off(gate), far_off(up), far_off(down), after],
+        [far_off(gate), far_off(up), far_off(down), far_off(after)],
         [fast((half, size), BF16), fast((half, size), BF16), fast((size, half), BF16)],
         "far_weights",
         place=place,
@@ -329,7 +332,10 @@
     return out
 
 
-def params_kernel(turn, experts, place_ref, stem_in, gain_in, router_in, after, stem, gain, router):
+def params_kernel(
+    turn, experts, shards, place_ref, stem_in, gain_in, router_in, routes_ref, cot_ref, after,
+    stem, gain, router, taken, cot,
+):
     wide = router_in[...].astype(F32)
     model = wide.shape[0]
     blank = jnp.zeros((model, LANES - 2 * experts), F32)
@@ -346,17 +352,22 @@
     stem[...] = values
     gain[...] = gains
     router[...] = wide.astype(BF16)
-
-
-def small_params(place, stem, gain, router, after, turn):
+    sel = own_selection(routes_ref[...].astype(F32), experts)
+    taken[...] = jnp.concatenate([one for one in sel for _ in range(shards)], axis=0).astype(BF16)
+    cot[...] = own_columns(cot_ref[...], cot.shape[1])
+
+
+def small_params(place, stem, gain, router, routes_t, cot, half, shards, after, turn):
     model, experts = router.shape
-    small = [far_off(stem), far_off(gain), far_off(router)]
+    tok = cot.shape[0]
+    small = [far_off(a) for a in (stem, gain, router, routes_t, cot)]
     shapes = [(stem.shape, BF16), (gain.shape, F32), ((model, LANES), BF16)]
-    return kernel_call(
-        functools.partial(params_kernel, turn, experts),
+    shapes += [((experts * shards * CAP, tok), BF16), ((tok, half), BF16)]
+    return kernel_call(
+        functools.partial(params_kernel, turn, experts, shards),
         0,
         LANES,
-        small + [after],
+        small + [far_off(after)],
         [pltpu.HBM(*a) for a in shapes],
         "params",
         place=place,
@@ -538,17 +549,29 @@
         others.append(jnp.sum(sel * other, axis=1, keepdims=True))
         patches = pair_patches(image_ref, top, first, width, channels)
         taken.append(mm_t(sel.astype(BF16), patches.astype(BF16)))
+    bands = 2 if paired else 1
+    deep = chunk // bands
+    lines = [pl.ds(pl.multiple_of(step * chunk + k * deep, deep), deep) for k in range(bands)]
+    held = [slice(k * deep, (k + 1) * deep) for k in range(bands)]
     if paired:
         taken, others = by_side(taken, even), by_side(others, even)
-    patches = jnp.concatenate(taken, axis=0).astype(BF16)
-    other = jnp.concatenate(others, axis=0)
-    stem = mm(patches, stem_ref[...]).astype(BF16)
-    value_ref[here, :] = stem
-    value = stem.astype(F32)
-    scale = lax.rsqrt(jnp.mean(value * value, axis=-1, keepdims=True) + 1e-06)
-    normed = (value * scale * gain_ref[...]).astype(BF16)
-    normed_ref[...] = normed
-    save = pltpu.make_async_copy(normed_ref, saved_ref.at[here, :], save_sem.at[0])
+    each = len(taken) // bands
+    patches = [
+        jnp.concatenate(taken[k * each : (k + 1) * each], axis=0).astype(BF16) for k in range(bands)
+    ]
+    others = [jnp.concatenate(others[k * each : (k + 1) * each], axis=0) for k in range(bands)]
+    stems = [mm(one, stem_ref[...]).astype(BF16) for one in patches]
+    normeds, scales, gates, gated, upped, hiddens = [], [], [], [], [], []
+    for line, band, stem in zip(lines, held, stems):
+        value_ref[line, :] = stem
+        value = stem.astype(F32)
+        scale = lax.rsqrt(jnp.mean(value * value, axis=-1, keepdims=True) + 1e-06)
+        normed = (value * scale * gain_ref[...]).astype(BF16)
+        normed_ref[band, :] = normed
+        normeds.append(normed)
+        scales.append(scale)
+    own_part = normed_ref.at[:, pl.ds(0, saved_ref.shape[1])]
+    save = pltpu.make_async_copy(own_part, saved_ref.at[here, :], save_sem.at[0])
     save.start()
     own_save = pltpu.make_async_copy(own_ref, own_out, save_sem.at[1])
 
@@ -562,35 +585,40 @@
         own_ref[...] = t_mm(own, stem_ref[:, : own_ref.shape[1]]).astype(BF16)
         own_save.start()
 
-    logits = mm(normed, inner[:, 2 * size :])
-    lane = lax.broadcasted_iota(jnp.int32, logits.shape, 1)
-    again = jnp.where(lane >= experts, lane - experts, lane).astype(F32)
-    lane = lane.astype(F32)
-    sig_mine = jax.nn.sigmoid(jnp.sum(jnp.where(lane == mine, logits, 0.0), axis=1, keepdims=True))
-    sig_other = jax.nn.sigmoid(jnp.sum(jnp.where(lane == other, logits, 0.0), axis=1, keepdims=True))
-    gate = sig_mine / (sig_mine + sig_other)
-    rest = sig_other / (sig_mine + sig_other)
-    both = gate * rest
-    coef_ref[here, :] = jnp.where(again == mine, both * (1.0 - sig_mine), 0.0) - jnp.where(
-        again == other, both * (1.0 - sig_other), 0.0
-    )
-    meta_ref[here, :] = jnp.where(lane == 0.0, gate, scale)
-    pre_gate = mm(normed, inner[:, :size])
+    for normed in normeds:
+        gated.append(mm(normed, inner[:, :size]))
+    for line, normed, other, scale in zip(lines, normeds, others, scales):
+        logits = mm(normed, inner[:, 2 * size :])
+        lane = lax.broadcasted_iota(jnp.int32, logits.shape, 1)
+        again = jnp.where(lane >= experts, lane - experts, lane).astype(F32)
+        lane = lane.astype(F32)
+        mine_logit = jnp.sum(jnp.where(lane == mine, logits, 0.0), axis=1, keepdims=True)
+        other_logit = jnp.sum(jnp.where(lane == other, logits, 0.0), axis=1, keepdims=True)
+        sig_mine, sig_other = jax.nn.sigmoid(mine_logit), jax.nn.sigmoid(other_logit)
+        gate = sig_mine / (sig_mine + sig_other)
+        rest = sig_other / (sig_mine + sig_other)
+        both = gate * rest
+        coef_ref[line, :] = jnp.where(again == mine, both * (1.0 - sig_mine), 0.0) - jnp.where(
+            again == other, both * (1.0 - sig_other), 0.0
+        )
+        meta_ref[line, :] = jnp.where(lane == 0.0, gate, scale)
+        gates.append(gate)
     arrive(up_copies)
-    pre_up = mm(normed, inner[:, size : 2 * size])
-    pg_ref[here, :] = pre_gate.astype(BF16)
-    pu_ref[here, :] = pre_up.astype(BF16)
-    hidden = (pre_gate * jax.nn.sigmoid(pre_gate) * pre_up).astype(BF16)
-    hidden_ref[here, :] = hidden
+    for normed in normeds:
+        upped.append(mm(normed, inner[:, size : 2 * size]))
     arrive(down_copies)
-    if paired:
-        half_rows = chunk // 2
-        for ref, (a, n) in zip(out_refs, cuts([r.shape[1] for r in out_refs])):
-            part = mm(hidden[half_rows:], outer[:, a : a + n])
-            ref[...] = (gate[half_rows:] * part).astype(BF16)
-    else:
-        for ref, (a, n) in zip(out_refs, cuts([r.shape[1] for r in out_refs])):
-            ref[here, :] = (gate * mm(hidden, outer[:, a : a + n])).astype(BF16)
+    for line, pre_gate, pre_up in zip(lines, gated, upped):
+        pg_ref[line, :] = pre_gate.astype(BF16)
+        pu_ref[line, :] = pre_up.astype(BF16)
+        hidden = (pre_gate * jax.nn.sigmoid(pre_gate) * pre_up).astype(BF16)
+        hidden_ref[line, :] = hidden
+        hiddens.append(hidden)
+    for ref, (a, n) in zip(out_refs, cuts([r.shape[1] for r in out_refs])):
+        part = (gates[-1] * mm(hiddens[-1], outer[:, a : a + n])).astype(BF16)
+        if paired:
+            ref[...] = part
+        else:
+            ref[here, :] = part
     save.wait()
 
     @pl.when(step == 0)
@@ -606,7 +634,7 @@
     parts = len(weights) // 2
     operands = [near(image), near(stem), near(gain), near(inner)] + [far_off(w) for w in weights]
     outs = [
-        pltpu.HBM((slots, model), BF16),
+        pltpu.HBM((slots, columns[0]), BF16),
         pltpu.HBM((tok, half), BF16),
         fast((chunk, model), BF16),
         fast((slots, model), BF16),
@@ -669,7 +697,7 @@
     *refs,
 ):
     cot_refs, refs = refs[: parts * bands], refs[parts * bands :]
-    saved, refs = refs[: 3 + parts], refs[3 + parts :]
+    saved, refs = refs[:4], refs[4:]
     proj_ref, ggp_ref, gup_ref, hg_ref, sem = refs
     step = pl.program_id(0)
     model = stem_ref.shape[1]
@@ -677,52 +705,61 @@
     here = pl.ds(pl.multiple_of(step * chunk, chunk), chunk)
     sources = [ggp_ref, gup_ref, hg_ref]
     targets = [ref.at[here, :] for ref in saved[:3]]
-    for n, ref in enumerate(cot_refs):
+    for n, ref in enumerate(cot_refs[:bands]):
         if bands == 1:
             sources.append(ref.at[here, :])
-            targets.append(saved[3 + n].at[here, :])
+            targets.append(saved[3].at[here, :])
         else:
-            deep = ref.shape[0]
             sources.append(ref)
-            targets.append(saved[3 + n // bands].at[pl.ds(n % bands * deep, deep), :])
+            targets.append(saved[3].at[pl.ds(n * ref.shape[0], ref.shape[0]), :])
     saves = [
         pltpu.make_async_copy(a, b, sem.at[n]) for n, (a, b) in enumerate(zip(sources, targets))
     ]
     for save in saves[3:]:
         save.start()
-    gate = meta_ref[here, 0:1]
-    scale = meta_ref[here, 1:2]
-    raw = 0.0
-    for k, (a, n) in enumerate(cuts([r.shape[1] for r in cot_refs[::bands]])):
-        if bands == 1:
-            cot = cot_refs[k][here, :]
-        else:
-            cot = jnp.concatenate([r[...] for r in cot_refs[k * bands : (k + 1) * bands]], axis=0)
-        raw = raw + mm_t(cot, outer[:, a : a + n])
-    pre_gate = pg_ref[here, :].astype(F32)
-    pre_up = pu_ref[here, :].astype(F32)
-    sigma = jax.nn.sigmoid(pre_gate)
-    silu = pre_gate * sigma
-    hidden = silu * pre_up
-    grad_gates = jnp.sum(raw * hidden, axis=1, keepdims=True)
-    hg_ref[...] = (gate * hidden).astype(BF16)
-    grad_hidden = gate * raw
-    ggp = (grad_hidden * pre_up * sigma * (1.0 + pre_gate - silu)).astype(BF16)
-    gup = (grad_hidden * silu).astype(BF16)
-    ggp_ref[...] = ggp
-    gup_ref[...] = gup
+    deep = chunk // bands
+    places = cuts([r.shape[1] for r in cot_refs[::bands]])
+    lines = [pl.ds(pl.multiple_of(step * chunk + k * deep, deep), deep) for k in range(bands)]
+    held = [slice(k * deep, (k + 1) * deep) for k in range(bands)]
+    gates = [meta_ref[line, 0:1] for line in lines]
+    scales = [meta_ref[line, 1:2] for line in lines]
+    raws, mixes, backs, grads = [], [], [], []
+    for k, line in enumerate(lines):
+        raw = 0.0
+        for n, (a, m) in enumerate(places):
+            cot = cot_refs[n * bands + k][...] if bands > 1 else cot_refs[n][line, :]
+            raw = raw + mm_t(cot, outer[:, a : a + m])
+        raws.append(raw)
+    for line, band, gate, raw in zip(lines, held, gates, raws):
+        pre_gate = pg_ref[line, :].astype(F32)
+        pre_up = pu_ref[line, :].astype(F32)
+        sigma = jax.nn.sigmoid(pre_gate)
+        silu = pre_gate * sigma
+        hidden = silu * pre_up
+        grad_gates = jnp.sum(raw * hidden, axis=1, keepdims=True)
+        hg_ref[band, :] = (gate * hidden).astype(BF16)
+        grad_hidden = gate * raw
+        ggp = (grad_hidden * pre_up * sigma * (1.0 + pre_gate - silu)).astype(BF16)
+        gup = (grad_hidden * silu).astype(BF16)
+        ggp_ref[band, :] = ggp
+        gup_ref[band, :] = gup
+        grad_logits = grad_gates * coef_ref[line, :]
+        high = grad_logits.astype(BF16)
+        low = (grad_logits - high.astype(F32)).astype(BF16)
+        lane = lax.broadcasted_iota(jnp.int32, grad_logits.shape, 1)
+        mix = jnp.where(lane < experts, high.astype(F32), low.astype(F32)).astype(BF16)
+        mixes.append(jnp.concatenate([ggp, gup, mix], axis=1))
     for save in saves[:3]:
         save.start()
-    grad_logits = grad_gates * coef_ref[here, :]
-    high = grad_logits.astype(BF16)
-    low = (grad_logits - high.astype(F32)).astype(BF16)
-    lane = lax.broadcasted_iota(jnp.int32, grad_logits.shape, 1)
-    mix = jnp.where(lane < experts, high.astype(F32), low.astype(F32)).astype(BF16)
-    back = mm_t(jnp.concatenate([ggp, gup, mix], axis=1), inner[...]) * gain_ref[...]
-    value = value_ref[here, :].astype(F32)
-    along = jnp.sum(back * value, axis=1, keepdims=True) * (scale * scale * scale) / model
-    grad = (scale * back - along * value).astype(BF16)
-    proj_ref[here, :] = mm_t(grad, stem_ref[...]).astype(BF16)
+    for mix in mixes:
+        backs.append(mm_t(mix, inner[...]))
+    for line, scale, back in zip(lines, scales, backs):
+        back = back * gain_ref[...]
+        value = value_ref[line, :].astype(F32)
+        along = jnp.sum(back * value, axis=1, keepdims=True) * (scale * scale * scale) / model
+        grads.append((scale * back - along * value).astype(BF16))
+    for line, grad in zip(lines, grads):
+        proj_ref[line, :] = mm_t(grad, stem_ref[...]).astype(BF16)
     for save in saves:
         save.wait()
 
@@ -739,14 +776,14 @@
         slots * (4 * model + 12 * size) + 6 * model * size,
         [near(a) for a in operands],
         [pltpu.HBM((slots, size), BF16)] * 3
-        + [pltpu.HBM((slots, part[0].shape[1]), BF16) for part in cots]
+        + [pltpu.HBM((slots, cots[0][0].shape[1]), BF16)]
         + [fast((slots, taps), BF16)]
         + [fast((chunk, size), BF16)] * 3,
         "backward",
         mib=20,
         steps=slots // chunk,
-        out_specs=[hbm()] * (3 + parts) + [vmem()] * 4,
-        scratch=[pltpu.SemaphoreType.DMA((3 + parts * bands,))],
+        out_specs=[hbm()] * 4 + [vmem()] * 4,
+        scratch=[pltpu.SemaphoreType.DMA((3 + bands,))],
     )
 
 
@@ -843,7 +880,7 @@
     half = cot.shape[1]
     size = ggp.shape[1]
     here = pl.multiple_of(place_ref[2] * size, LANES)
-    sources = (normed.at[:, pl.ds(0, half)], ggp, gup, hg, cot)
+    sources = (normed, ggp, gup, hg, cot)
     targets = (left.at[0], right.at[0], right.at[1], left.at[1], right.at[2])
     loads = [pltpu.make_async_copy(a, b, sem.at[n]) for n, (a, b) in enumerate(zip(sources, targets))]
     places = (
@@ -877,13 +914,13 @@
     half = cot.shape[1]
     return kernel_call(
         near_grads_kernel,
-        100_000_000_000,
+        20_000_000_000,
         LANES,
         [far_off(a) for a in (normed, ggp, gup, hg, cot)] + [after],
         [pltpu.HBM((half, 2 * size), F32)] * 2
         + [pltpu.HBM((2 * size, half), F32)],
         "near_grads",
-        mib=20,
+        mib=14,
         place=place,
         specs=[hbm()] * 6,
         out_specs=[hbm()] * 3,
@@ -929,9 +966,9 @@
     shape = away[0].shape
     return pl.pallas_call(
         fill_kernel,
-        compiler_params=pltpu.CompilerParams(vmem_limit_bytes=16 * MIB),
+        compiler_params=pltpu.CompilerParams(vmem_limit_bytes=12 * MIB),
         cost_estimate=pl.CostEstimate(
-            flops=100_000_000_000, bytes_accessed=LANES, transcendentals=0
+            flops=10_000_000_000, bytes_accessed=LANES, transcendentals=0
         ),
         grid_spec=pltpu.PrefetchScalarGridSpec(
             num_scalar_prefetch=1,
@@ -1016,7 +1053,8 @@
     if cores != 2:
         given = lax.dynamic_slice_in_dim(grad_mixed, column, half, 1)
     copies = 1 if paired else shards
-    packed, taken, cot = pack(place, latent, routes.T, given, experts, copies, half)
+    routes_t = routes.T
+    packed = pack(latent, routes_t, given, experts, copies, half)
     arrived = exchange(packed)
 
     stem, gain, router = stem_weight, norm_gain[None, :], router_weight
@@ -1037,15 +1075,17 @@
         gain = jnp.roll(gain, -column, 1)
         router = jnp.roll(router, -column, 0)
 
-    small = small_params(place, stem, gain, router, packed, cores == 2)
+    *small, taken, cot = small_params(
+        place, stem, gain, router, routes_t, given, half, copies, packed, cores == 2
+    )
     same_cot, image = unpack(arrived, half, channels + 2, small[1])
     size = down_parts[-1].shape[0]
     gathered = gather(place, small, gate_parts, size)
     if paired:
         joined = other_core(same_cot)
         image = weave(place, image, other_shard(image), joined, gathered[1])
-        cots = [same_cot, other_shard(same_cot)]
-        cots = [cots, [joined, other_core(cots[1])]]
+        cots = [[same_cot], [joined]]
+        far_cot = other_shard(same_cot)
     elif cores == 2:
         cots = [[same_cot], [other_core(same_cot)]]
     else:
@@ -1059,6 +1099,9 @@
     stem, gain, _ = gathered
     if paired:
         own, away = outputs(meta, hidden, outer)
+        far_cot, own = lax.optimization_barrier((far_cot, own))
+        cots[0].append(far_cot)
+        cots[1].append(other_core(far_cot))
         over = other_shard(add_up(outs[0], other_core(outs[1]), own))
         away = other_core(away)
     elif cores == 2:
@@ -1069,7 +1112,7 @@
         own = lax.psum_scatter(turned, "rep", scatter_dimension=1, tiled=True)
         away = over = jnp.zeros_like(own)
     acts = [value, meta, coef, pg, pu]
-    ggp, gup, hg, *held, proj, ggp_here, gup_here, hg_here = backward(
+    ggp, gup, hg, held, proj, ggp_here, gup_here, hg_here = backward(
         stem, gain, inner, outer, acts, cots, experts
     )
     terms = to_image(place, proj, sel, stem, cot, paired, width, channels)
@@ -1083,12 +1126,12 @@
     back = exchange(sent)
 
     if cores == 2:
-        grads = near_grads(place, kept, ggp, gup, hg, held[0], sent)
+        grads = near_grads(place, kept, ggp, gup, hg, held, sent)
         *grads, done = fill(place, away_grads, grads)
     else:
         done = jnp.zeros((8, LANES), F32)
         size = gate_weight.shape[1] // cores
-        grads = gathered_grads(column, size, kept, ggp, gup, hg, held[0])
+        grads = gathered_grads(column, size, kept, ggp, gup, hg, held)
     grad_gate, grad_up, grad_down = grads
 
     mixed, lat_sum = mix(own_stem, taken, back, done, channels)

time: 83.3 us -> 79.1 us (0.950)
  Pallas kernels: 50.4 us -> 48 us
  waiting for transfers between devices: 11.7 us -> 9.69 us
    pallas_call x15, Pallas kernels: 37.5 us -> 35.5 us  [kernel_call(): call(kernel, flops, moved, mib, grid_spec=pltpu.PrefetchScalarGridSpec(nu...]
    ppermute x4, waiting for transfers between devices: 1.4 us -> 0.22 us  [other_shard(): lax.ppermute(values, 'exp', [(i, i ^ 1) for i in range(lax.axis_size('exp...]
    all_to_all x2, waiting for transfers between devices: 9.35 us -> 8.46 us  [exchange(): lax.all_to_all(values, 'exp', split_axis=0, concat_axis=0, tiled=True, ax...]
  transfers between devices with their start and end apart: 18 -> 18, of which waited for: 4 -> 4; matrix products, arithmetic and copies ran while one was open for 2% -> 2% of each run, Pallas kernels for 54% -> 56%
where the time goes in v3:
time: 79.1 us; the launch traced here: 78.7 us
  Pallas kernels  48 us (61%)
  starting transfers between devices  18.2 us (23%)
  waiting for transfers between devices  9.69 us (12%)
  local copies, waits for them, and re-layouts  2.01 us (3%)
  between operations  0.85 us (1%)
    pallas_call x15, Pallas kernels, kernel_call(): call(kernel, flops, moved, mib, grid_spec=pltpu.PrefetchScalarGridSpec(nu...  35.5 us
    all_to_all x2, starting transfers between devices, exchange(): lax.all_to_all(values, 'exp', split_axis=0, concat_axis=0, tiled=True, ax...  10.9 us
    all_to_all x2, waiting for transfers between devices, exchange(): lax.all_to_all(values, 'exp', split_axis=0, concat_axis=0, tiled=True, ax...  8.46 us
    pallas_call x1, Pallas kernels, forward(): pl.pallas_call(functools.partial(forward_kernel, paired, parts, width, ex...  7.79 us
    ppermute x4, starting transfers between devices, other_shard(): lax.ppermute(values, 'exp', [(i, i ^ 1) for i in range(lax.axis_size('exp...  4.67 us
    pallas_call x1, Pallas kernels, fill(): pl.pallas_call(fill_kernel, compiler_params=pltpu.CompilerParams(vmem_lim...  4.65 us
    ppermute x12, starting transfers between devices, other_core(): return lax.ppermute(values, 'rep', [(0, 1), (1, 0)])  2.54 us
  transfers between devices with their start and end apart: 18, of which 4 were waited for; matrix products, arithmetic and copies ran while one was open for 2% of the time, Pallas kernels for 56%

profile of v3, /device:TPU:0, one launch (start us, length us, event | category | flops | bytes accessed | tf_op | source)
XLA Modules:
  0.0 78.7 jit_solution(3219767183133700189)
XLA Ops:
  0.6 2.2 %pack.1.after.after_ref = bf16[8,258,128]{2,1,0:T(8,128)(2,1)} custom-call(bf16[2,16,64]{2,1,0:T(8,128)(2,1)} %latent_ref.1, s32[2,128]{1,0:T(2,128)} %bitcast.4, bf16[128,1536]{1,0:T(8,128)(2,1)} %cot_ref.3), custom_call_target="tpu_custom_call" | custom-call | flops 62914560 | bytes 1056768 | tf_op jit(solution)/shard_map/pack/pallas_call | solution.py:107
  2.9 7.3 %all-to-all-start = ((bf16[8,258,128]{2,1,0:T(8,128)(2,1)}), bf16[8,258,128]{2,1,0:T(8,128)(2,1)S(1)}, u32[]{:S(2)}, u32[]{:S(2)}) async-start(bf16[8,258,128]{2,1,0:T(8,128)(2,1)} %pack.1.after.after_ref), calls=%async_computation | async-start | bytes 1081344 | tf_op jit(solution)/shard_map/all_to_all | solution.py:79
  10.1 0.1 pad_add_fusion.place_ref
  10.2 0.0 copy-start.5
  10.2 4.0 %far_weights.1 = (bf16[768,768]{1,0:T(8,128)(2,1)}, bf16[768,768]{1,0:T(8,128)(2,1)}, bf16[768,768]{1,0:T(8,128)(2,1)S(1)}) custom-call(s32[3]{0:T(128)S(1)} %pad_add_fusion.place_ref, bf16[768,1536]{1,0:T(8,128)(2,1)} %refs_0_.2, bf16[768,1536]{1,0:T(8,128)(2,1)} %refs_0_.3, bf16[1536,768]{1,0:T(8,128)(2,1)} %refs_2_.1, ...), custom_call_target="tpu_custom_call" | custom-call | bytes 128 | tf_op jit(solution)/shard_map/far_weights/pallas_call | solution.py:107
  14.2 0.1 collective-permute-start.2
  14.3 0.5 collective-permute-start.3
  14.8 0.1 collective-permute-start.4
  14.9 0.0 copy-done.5
  14.9 0.6 broadcast_in_dim.3.gain_in
  15.5 0.0 copy-done.4
  15.5 0.9 %copy.18.router_in = bf16[1536,8]{1,0:T(8,128)(2,1)} copy(bf16[1536,8]{0,1:T(8,128)(2,1)S(1)} %copy-done.4) | data formatting | bytes 49152 | tf_op args[3]
  16.4 3.1 %params.1 = (bf16[144,1536]{1,0:T(8,128)(2,1)}, f32[1,1536]{1,0:T(1,128)}, bf16[1536,128]{1,0:T(8,128)(2,1)}, bf16[320,128]{1,0:T(8,128)(2,1)}, bf16[128,768]{1,0:T(8,128)(2,1)}) custom-call(s32[3]{0:T(128)S(1)} %pad_add_fusion.place_ref, bf16[144,1536]{1,0:T(8,128)(2,1)} %stem_in.1, f32[1,1536]{1,0:T(1,128)} %broadcast_in_dim.3.gain_in, ...), custom_call_target="tpu_custom_call" | custom-call | bytes 128 | tf_op jit(solution)/shard_map/params/pallas_call | solution.py:107
  19.5 5.5 %all-to-all-done.packed_ref = bf16[8,258,128]{2,1,0:T(8,128)(2,1)S(1)} async-done(((bf16[8,258,128]{2,1,0:T(8,128)(2,1)}), bf16[8,258,128]{2,1,0:T(8,128)(2,1)S(1)}, u32[]{:S(2)}, u32[]{:S(2)}) %all-to-all-start) | async-done | bytes 528416 | tf_op jit(solution)/shard_map/all_to_all | solution.py:79
  25.0 0.1 collective-permute-start.1
  25.1 1.6 %collective-permute-start = (bf16[8,18,128]{2,1,0:T(8,128)(2,1)S(1)}, bf16[8,18,128]{2,1,0:T(8,128)(2,1)S(1)}, u32[]{:S(2)}, u32[]{:S(2)}) collective-permute-start(bf16[8,18,128]{2,1,0:T(8,128)(2,1)S(1)} %get-tuple-element.61.same_ref), channel_id=1, source_target_pairs={{0,2},{2,0},{4,6},{6,4},{8,10},{10,8},{12,14},{14,12},{16,18},{18,... | collective-permute-start | bytes 110600 | tf_op jit(solution)/shard_map/ppermute | solution.py:70
  26.7 0.0 collective-permute-done.2.refs_1_
  26.7 0.5 collective-permute-start.5
  27.2 0.5 copy-done.3
  27.7 2.5 %gather.1 = (bf16[144,1536]{1,0:T(8,128)(2,1)S(1)}, f32[1,1536]{1,0:T(1,128)S(1)}, bf16[1536,1664]{1,0:T(8,128)(2,1)S(1)}) custom-call(s32[3]{0:T(128)S(1)} %pad_add_fusion.place_ref, bf16[768,1536]{1,0:T(8,128)(2,1)} %refs_0_.2, bf16[768,768]{1,0:T(8,128)(2,1)} %copy-done.3, bf16[144,1536]{1,0:T(8,128)(2,1)} %get-tuple-element.64.refs_2_, ...), custom_call_target="tpu_custom_call" | custom-call | bytes 128 | tf_op jit(solution)/shard_map/gather/pallas_call | solution.py:107
  30.2 0.0 collective-permute-done.other_ref
  30.2 0.0 collective-permute-done.1.after_ref.refs_2_.refs_0_
  30.2 0.6 weave.1.image_ref
  30.8 0.0 collective-permute-done.3.refs_1_
  30.8 0.0 collective-permute-done.4.refs_3_
  30.8 7.8 %forward.1 = (bf16[640,768]{1,0:T(8,128)(2,1)}, bf16[128,768]{1,0:T(8,128)(2,1)}, bf16[640,1536]{1,0:T(8,128)(2,1)S(1)}, bf16[640,1536]{1,0:T(8,128)(2,1)S(1)}, ...) custom-call(s32[3]{0:T(128)S(1)} %pad_add_fusion.place_ref, ...), custom_call_target="tpu_custom_call", output_to_operand_aliasing={{10}: (4, {})} | custom-call | flops 99999997952 | bytes 128 | tf_op jit(solution)/shard_map/forward/pallas_call | solution.py:651
  38.6 0.2 collective-permute-start.7
  38.8 0.9 %outputs.1 = (bf16[320,768]{1,0:T(8,128)(2,1)S(1)}, bf16[320,768]{1,0:T(8,128)(2,1)S(1)}) custom-call(f32[640,128]{1,0:T(8,128)S(1)} %get-tuple-element.73.meta_ref, bf16[640,768]{1,0:T(8,128)(2,1)S(1)} %get-tuple-element.74.hidden_ref, bf16[768,1536]{1,0:T(8,128)(2,1)S(1)} %get-tuple-element.75.outer), custom_call_target="tpu_custom_call" | custom-call | bytes 128 | tf_op jit(solution)/shard_map/outputs/pallas_call | solution.py:107
  39.7 0.2 collective-permute-done.5.refs_1_
  40.0 0.2 collective-permute-start.9
  40.2 0.3 collective-permute-start.6
  40.5 0.0 collective-permute-done.7.b_ref
  40.5 0.1 add_up.1
  40.6 1.4 %collective-permute-start.8 = (bf16[320,768]{1,0:T(8,128)(2,1)S(1)}, bf16[320,768]{1,0:T(8,128)(2,1)S(1)}, u32[]{:S(2)}, u32[]{:S(2)}) collective-permute-start(bf16[320,768]{1,0:T(8,128)(2,1)S(1)} %add_up.1), channel_id=1, source_target_pairs={{0,2},{2,0},{4,6},{6,4},{8,10},{10,8},{12,14},{14,12},{16,18},{18,... | collective-permute-start | bytes 1474568 | tf_op jit(solution)/shard_map/ppermute | solution.py:70
  42.0 0.0 collective-permute-done.9.refs_3_.refs_1_
  42.0 7.4 %backward.1 = (bf16[640,768]{1,0:T(8,128)(2,1)}, bf16[640,768]{1,0:T(8,128)(2,1)}, bf16[640,768]{1,0:T(8,128)(2,1)}, bf16[640,768]{1,0:T(8,128)(2,1)}, bf16[640,...) custom-call(bf16[144,1536]{1,0:T(8,128)(2,1)S(1)} %get-tuple-element, ...), custom_call_target="tpu_custom_call" | custom-call | flops 6039797760 | bytes 16908288 | tf_op jit(solution)/shard_map/backward/pallas_call | solution.py:107
  49.4 0.0 copy-done
  49.4 1.1 %to_image.1 = (f32[8,16,128]{2,1,0:T(8,128)S(1)}, bf16[8,16,128]{2,1,0:T(8,128)(2,1)S(1)}) custom-call(s32[3]{0:T(128)S(1)} %pad_add_fusion.place_ref, bf16[640,144]{1,0:T(8,128)(2,1)S(1)} %get-tuple-element.87.proj_ref, bf16[8,80,256]{2,1,0:T(8,128)(2,1)S(1)} %get-tuple-element.88.sel_ref, bf16[144,1536]{1,0:T(8,128)(2,1)S(1)} %get-tuple-element.67.stem_ref, ...), custom_call_target="tpu_custom_call" | custom-call | flops 47185920 | bytes 1179648 | tf_op jit(solution)/shard_map/to_image/pallas_call | solution.py:107
  50.6 1.2 %collective-permute-start.10 = (bf16[8,16,128]{2,1,0:T(8,128)(2,1)S(1)}, bf16[8,16,128]{2,1,0:T(8,128)(2,1)S(1)}, u32[]{:S(2)}, u32[]{:S(2)}) collective-permute-start(bf16[8,16,128]{2,1,0:T(8,128)(2,1)S(1)} %get-tuple-element.91), channel_id=1, source_target_pairs={{0,2},{2,0},{4,6},{6,4},{8,10},{10,8},{12,14},{14,12},{16,18},{18,... | collective-permute-start | bytes 98312 | tf_op jit(solution)/shard_map/ppermute | solution.py:70
  51.8 3.4 %far_grads.1 = (bf16[768,768]{1,0:T(8,128)(2,1)S(1)}, bf16[768,768]{1,0:T(8,128)(2,1)}, bf16[768,768]{1,0:T(8,128)(2,1)S(1)}) custom-call(bf16[640,1536]{1,0:T(8,128)(2,1)S(1)} %get-tuple-element.92.normed, bf16[640,768]{1,0:T(8,128)(2,1)S(1)} %get-tuple-element.93.ggp, bf16[640,768]{1,0:T(8,128)(2,1)S(1)} %get-tuple-element.94.gup, ...), custom_call_target="tpu_custom_call" | custom-call | flops 2264924160 | bytes 9830400 | tf_op jit(solution)/shard_map/far_grads/pallas_call | solution.py:107
  55.2 0.0 collective-permute-start.12
  55.2 0.5 collective-permute-start.13
  55.7 0.0 collective-permute-done.6.b_ref
  55.7 0.0 collective-permute-start.11
  55.7 0.0 collective-permute-done.10.over_ref
  55.7 0.0 collective-permute-done.8.c_ref
  55.7 1.0 %pack_back.1.after_ref = bf16[8,256,128]{2,1,0:T(8,128)(2,1)} custom-call(bf16[320,768]{1,0:T(8,128)(2,1)S(1)} %get-tuple-element.77.after_ref.a_ref, bf16[320,768]{1,0:T(8,128)(2,1)S(1)} %collective-permute-done.6.b_ref, bf16[320,768]{1,0:T(8,128)(2,1)S(1)} %collective-permute-done.8.c_ref, f32[8,16,128]{2,1,0:T(8,128)S(1)} %get-tuple-element.90.terms_ref, ...), custom_call_target="tpu_custom_call" | custom-call | flops 245760 | bytes 1966080 | tf_op jit(solution)/shard_map/pack_back/pallas_call | solution.py:107
  56.7 3.6 %all-to-all-start.1 = ((bf16[8,256,128]{2,1,0:T(8,128)(2,1)}), bf16[8,256,128]{2,1,0:T(8,128)(2,1)S(1)}, u32[]{:S(2)}, u32[]{:S(2)}) async-start(bf16[8,256,128]{2,1,0:T(8,128)(2,1)} %pack_back.1.after_ref), calls=%async_computation.1 | async-start | bytes 1048576 | tf_op jit(solution)/shard_map/all_to_all | solution.py:79
  60.4 7.5 %near_grads.1 = (f32[768,1536]{1,0:T(8,128)}, f32[768,1536]{1,0:T(8,128)}, f32[1536,768]{1,0:T(8,128)}) custom-call(s32[3]{0:T(128)S(1)} %pad_add_fusion.place_ref, bf16[640,768]{1,0:T(8,128)(2,1)} %get-tuple-element.99.normed, bf16[640,768]{1,0:T(8,128)(2,1)} %get-tuple-element.100.ggp, bf16[640,768]{1,0:T(8,128)(2,1)} %get-tuple-element.101.gup, ...), custom_call_target="tpu_custom_call" | custom-call | flops 20000000000 | bytes 128 | tf_op jit(solution)/shard_map/near_grads/pallas_call | solution.py:107
  67.9 0.0 collective-permute-done.12.up_in
  67.9 0.0 collective-permute-done.13.down_in
  67.9 0.0 collective-permute-done.11.gate_in
  68.0 0.0 copy-start.1
  68.0 0.0 copy-start.2
  68.0 4.7 %fill.1 = (f32[768,1536]{1,0:T(8,128)}, f32[768,1536]{1,0:T(8,128)}, f32[1536,768]{1,0:T(8,128)}, f32[8,128]{1,0:T(8,128)S(1)}) custom-call(s32[3]{0:T(128)S(1)} %pad_add_fusion.place_ref, bf16[768,768]{1,0:T(8,128)(2,1)} %collective-permute-done.11.gate_in, ...), custom_call_target="tpu_custom_call", output_to_operand_aliasing={{0}: (4, {}), {1}: (5, {}), {2}: (6, {})} | custom-call | flops 10000000000 | bytes 128 | tf_op jit(solution)/shard_map/fill/pallas_call | solution.py:967
  72.6 2.9 %all-to-all-done.1.back_ref = bf16[8,256,128]{2,1,0:T(8,128)(2,1)S(1)} async-done(((bf16[8,256,128]{2,1,0:T(8,128)(2,1)}), bf16[8,256,128]{2,1,0:T(8,128)(2,1)S(1)}, u32[]{:S(2)}, u32[]{:S(2)}) %all-to-all-start.1) | async-done | bytes 524320 | tf_op jit(solution)/shard_map/all_to_all | solution.py:79
  75.6 0.0 copy-done.1
  75.6 0.0 copy-done.2
  75.6 0.3 mixed.1
  75.9 0.1 collective-permute-start.14
  76.0 0.5 collective-permute-start.15
  76.5 0.9 %collective-permute-done.15.b_ref = f32[16,128]{1,0:T(8,128)S(1)} collective-permute-done((f32[16,128]{1,0:T(8,128)S(1)}, f32[16,128]{1,0:T(8,128)S(1)}, u32[]{:S(2)}, u32[]{:S(2)}) %collective-permute-start.15) | collective-permute-done | bytes 8224 | tf_op jit(solution)/shard_map/ppermute | solution.py:66
  77.4 0.0 collective-permute-done.14.away_ref
  77.4 1.3 %join.1 = (bf16[128,1536]{1,0:T(8,128)(2,1)}, f32[2,16,64]{2,1,0:T(8,128)}) custom-call(s32[3]{0:T(128)S(1)} %pad_add_fusion.place_ref, bf16[128,768]{1,0:T(8,128)(2,1)S(1)} %get-tuple-element.108.own_ref, bf16[128,768]{1,0:T(8,128)(2,1)S(1)} %collective-permute-done.14.away_ref, f32[16,128]{1,0:T(8,128)S(1)} %get-tuple-element.109.a_ref, ...), custom_call_target="tpu_custom_call" | custom-call | bytes 786432 | tf_op jit(solution)/shard_map/join/pallas_call | solution.py:107
  (4 shorter events, 0.0 us)
Async XLA Ops:
  2.9 22.1 %all-to-all-start = ((bf16[8,258,128]{2,1,0:T(8,128)(2,1)}), bf16[8,258,128]{2,1,0:T(8,128)(2,1)S(1)}, u32[]{:S(2)}, u32[]{:S(2)}) async-start(bf16[8,258,128]{2,1,0:T(8,128)(2,1)} %pack.1.after.after_ref), calls=%async_computation | async-start | bytes 1081344 | tf_op jit(solution)/shard_map/all_to_all | solution.py:79
  10.2 4.7 %copy-start.5 = (f32[1536]{0:T(1024)S(1)}, f32[1536]{0:T(1024)}, u32[]{:S(2)}) copy-start(f32[1536]{0:T(1024)} %param.11) | copy-start | bytes 18436
  10.2 5.3 %copy-start.4 = (bf16[1536,8]{0,1:T(8,128)(2,1)S(1)}, bf16[1536,8]{0,1:T(8,128)(2,1)}, u32[]{:S(2)}) copy-start(bf16[1536,8]{0,1:T(8,128)(2,1)} %param.12) | copy-start | bytes 73732
  14.2 12.4 %collective-permute-start.2 = (bf16[768,768]{1,0:T(8,128)(2,1)}, bf16[768,768]{1,0:T(8,128)(2,1)S(1)}, u32[]{:S(2)}, u32[]{:S(2)}) collective-permute-start(bf16[768,768]{1,0:T(8,128)(2,1)} %get-tuple-element.63), channel_id=1, source_target_pairs={{0,1},{1,0},{2,3},{3,2},{4,5},{5,4},{6,7},{7,6},{8,9},{9,8},{10,11... | collective-permute-start | bytes 3538952 | tf_op jit(solution)/shard_map/ppermute | solution.py:66
  14.3 16.5 %collective-permute-start.3 = (bf16[768,768]{1,0:T(8,128)(2,1)}, bf16[768,768]{1,0:T(8,128)(2,1)}, u32[]{:S(2)}, u32[]{:S(2)}) collective-permute-start(bf16[768,768]{1,0:T(8,128)(2,1)} %get-tuple-element.69), channel_id=1, source_target_pairs={{0,1},{1,0},{2,3},{3,2},{4,5},{5,4},{6,7},{7,6},{8,9},{9,8},{10,11... | collective-permute-start | bytes 3538952 | tf_op jit(solution)/shard_map/ppermute | solution.py:66
  14.8 16.0 %collective-permute-start.4 = (bf16[768,768]{1,0:T(8,128)(2,1)S(1)}, bf16[768,768]{1,0:T(8,128)(2,1)}, u32[]{:S(2)}, u32[]{:S(2)}) collective-permute-start(bf16[768,768]{1,0:T(8,128)(2,1)S(1)} %get-tuple-element.70), channel_id=1, source_target_pairs={{0,1},{1,0},{2,3},{3,2},{4,5},{5,4},{6,7},{7,6},{8,9},{9,8},{10,11... | collective-permute-start | bytes 3538952 | tf_op jit(solution)/shard_map/ppermute | solution.py:66
  25.0 5.2 %collective-permute-start.1 = (bf16[320,768]{1,0:T(8,128)(2,1)S(1)}, bf16[320,768]{1,0:T(8,128)(2,1)S(1)}, u32[]{:S(2)}, u32[]{:S(2)}) collective-permute-start(bf16[320,768]{1,0:T(8,128)(2,1)S(1)} %get-tuple-element.62.refs_0_), channel_id=1, source_target_pairs={{0,1},{1,0},{2,3},{3,2},{4,5},{5,4},{6,7},{7,6},{8,9},{9,8},{10,11... | collective-permute-start | bytes 1474568 | tf_op jit(solution)/shard_map/ppermute | solution.py:66
  25.1 5.1 %collective-permute-start = (bf16[8,18,128]{2,1,0:T(8,128)(2,1)S(1)}, bf16[8,18,128]{2,1,0:T(8,128)(2,1)S(1)}, u32[]{:S(2)}, u32[]{:S(2)}) collective-permute-start(bf16[8,18,128]{2,1,0:T(8,128)(2,1)S(1)} %get-tuple-element.61.same_ref), channel_id=1, source_target_pairs={{0,2},{2,0},{4,6},{6,4},{8,10},{10,8},{12,14},{14,12},{16,18},{18,... | collective-permute-start | bytes 110600 | tf_op jit(solution)/shard_map/ppermute | solution.py:70
  26.7 1.0 %copy-start.3 = (bf16[768,768]{1,0:T(8,128)(2,1)}, bf16[768,768]{1,0:T(8,128)(2,1)S(1)}, u32[]{:S(2)}) copy-start(bf16[768,768]{1,0:T(8,128)(2,1)S(1)} %collective-permute-done.2.refs_1_) | copy-start | bytes 3538948
  26.7 13.3 %collective-permute-start.5 = (bf16[320,768]{1,0:T(8,128)(2,1)S(1)}, bf16[320,768]{1,0:T(8,128)(2,1)S(1)}, u32[]{:S(2)}, u32[]{:S(2)}) collective-permute-start(bf16[320,768]{1,0:T(8,128)(2,1)S(1)} %get-tuple-element.62.refs_0_), channel_id=1, source_target_pairs={{0,2},{2,0},{4,6},{6,4},{8,10},{10,8},{12,14},{14,12},{16,18},{18,... | collective-permute-start | bytes 1474568 | tf_op jit(solution)/shard_map/ppermute | solution.py:70
  38.6 1.9 %collective-permute-start.7 = (bf16[320,768]{1,0:T(8,128)(2,1)S(1)}, bf16[320,768]{1,0:T(8,128)(2,1)S(1)}, u32[]{:S(2)}, u32[]{:S(2)}) collective-permute-start(bf16[320,768]{1,0:T(8,128)(2,1)S(1)} %get-tuple-element.80), channel_id=1, source_target_pairs={{0,1},{1,0},{2,3},{3,2},{4,5},{5,4},{6,7},{7,6},{8,9},{9,8},{10,11... | collective-permute-start | bytes 1474568 | tf_op jit(solution)/shard_map/ppermute | solution.py:66
  40.0 2.0 %collective-permute-start.9 = (bf16[320,768]{1,0:T(8,128)(2,1)S(1)}, bf16[320,768]{1,0:T(8,128)(2,1)S(1)}, u32[]{:S(2)}, u32[]{:S(2)}) collective-permute-start(bf16[320,768]{1,0:T(8,128)(2,1)S(1)} %collective-permute-done.5.refs_1_), channel_id=1, source_target_pairs={{0,1},{1,0},{2,3},{3,2},{4,5},{5,4},{6,7},{7,6},{8,9},{9,8},{10,11... | collective-permute-start | bytes 1474568 | tf_op jit(solution)/shard_map/ppermute | solution.py:66
  40.2 15.5 %collective-permute-start.6 = (bf16[320,768]{1,0:T(8,128)(2,1)S(1)}, bf16[320,768]{1,0:T(8,128)(2,1)S(1)}, u32[]{:S(2)}, u32[]{:S(2)}) collective-permute-start(bf16[320,768]{1,0:T(8,128)(2,1)S(1)} %get-tuple-element.78), channel_id=1, source_target_pairs={{0,1},{1,0},{2,3},{3,2},{4,5},{5,4},{6,7},{7,6},{8,9},{9,8},{10,11... | collective-permute-start | bytes 1474568 | tf_op jit(solution)/shard_map/ppermute | solution.py:66
  40.6 15.1 %collective-permute-start.8 = (bf16[320,768]{1,0:T(8,128)(2,1)S(1)}, bf16[320,768]{1,0:T(8,128)(2,1)S(1)}, u32[]{:S(2)}, u32[]{:S(2)}) collective-permute-start(bf16[320,768]{1,0:T(8,128)(2,1)S(1)} %add_up.1), channel_id=1, source_target_pairs={{0,2},{2,0},{4,6},{6,4},{8,10},{10,8},{12,14},{14,12},{16,18},{18,... | collective-permute-start | bytes 1474568 | tf_op jit(solution)/shard_map/ppermute | solution.py:70
  42.0 7.4 %copy-start = (bf16[128,768]{1,0:T(8,128)(2,1)S(1)}, bf16[128,768]{1,0:T(8,128)(2,1)}, u32[]{:S(2)}) copy-start(bf16[128,768]{1,0:T(8,128)(2,1)} %get-tuple-element.89.cot_ref) | copy-start | bytes 589828
  50.6 5.2 %collective-permute-start.10 = (bf16[8,16,128]{2,1,0:T(8,128)(2,1)S(1)}, bf16[8,16,128]{2,1,0:T(8,128)(2,1)S(1)}, u32[]{:S(2)}, u32[]{:S(2)}) collective-permute-start(bf16[8,16,128]{2,1,0:T(8,128)(2,1)S(1)} %get-tuple-element.91), channel_id=1, source_target_pairs={{0,2},{2,0},{4,6},{6,4},{8,10},{10,8},{12,14},{14,12},{16,18},{18,... | collective-permute-start | bytes 98312 | tf_op jit(solution)/shard_map/ppermute | solution.py:70
  55.2 12.7 %collective-permute-start.12 = (bf16[768,768]{1,0:T(8,128)(2,1)}, bf16[768,768]{1,0:T(8,128)(2,1)}, u32[]{:S(2)}, u32[]{:S(2)}) collective-permute-start(bf16[768,768]{1,0:T(8,128)(2,1)} %get-tuple-element.97), channel_id=1, source_target_pairs={{0,1},{1,0},{2,3},{3,2},{4,5},{5,4},{6,7},{7,6},{8,9},{9,8},{10,11... | collective-permute-start | bytes 3538952 | tf_op jit(solution)/shard_map/ppermute | solution.py:66
  55.2 12.7 %collective-permute-start.13 = (bf16[768,768]{1,0:T(8,128)(2,1)S(1)}, bf16[768,768]{1,0:T(8,128)(2,1)}, u32[]{:S(2)}, u32[]{:S(2)}) collective-permute-start(bf16[768,768]{1,0:T(8,128)(2,1)S(1)} %get-tuple-element.98), channel_id=1, source_target_pairs={{0,1},{1,0},{2,3},{3,2},{4,5},{5,4},{6,7},{7,6},{8,9},{9,8},{10,11... | collective-permute-start | bytes 3538952 | tf_op jit(solution)/shard_map/ppermute | solution.py:66
  55.7 12.2 %collective-permute-start.11 = (bf16[768,768]{1,0:T(8,128)(2,1)S(1)}, bf16[768,768]{1,0:T(8,128)(2,1)}, u32[]{:S(2)}, u32[]{:S(2)}) collective-permute-start(bf16[768,768]{1,0:T(8,128)(2,1)S(1)} %get-tuple-element.96.after_ref), channel_id=1, source_target_pairs={{0,1},{1,0},{2,3},{3,2},{4,5},{5,4},{6,7},{7,6},{8,9},{9,8},{10,11... | collective-permute-start | bytes 3538952 | tf_op jit(solution)/shard_map/ppermute | solution.py:66
  56.7 18.8 %all-to-all-start.1 = ((bf16[8,256,128]{2,1,0:T(8,128)(2,1)}), bf16[8,256,128]{2,1,0:T(8,128)(2,1)S(1)}, u32[]{:S(2)}, u32[]{:S(2)}) async-start(bf16[8,256,128]{2,1,0:T(8,128)(2,1)} %pack_back.1.after_ref), calls=%async_computation.1 | async-start | bytes 1048576 | tf_op jit(solution)/shard_map/all_to_all | solution.py:79
  68.0 7.6 %copy-start.1 = (bf16[128,768]{1,0:T(8,128)(2,1)S(1)}, bf16[128,768]{1,0:T(8,128)(2,1)}, u32[]{:S(2)}) copy-start(bf16[128,768]{1,0:T(8,128)(2,1)} %get-tuple-element.71.stem_ref) | copy-start | bytes 589828
  68.0 7.6 %copy-start.2 = (bf16[320,128]{1,0:T(8,128)(2,1)S(1)}, bf16[320,128]{1,0:T(8,128)(2,1)}, u32[]{:S(2)}) copy-start(bf16[320,128]{1,0:T(8,128)(2,1)} %get-tuple-element.72.taken_ref) | copy-start | bytes 245764
  75.9 1.5 %collective-permute-start.14 = (bf16[128,768]{1,0:T(8,128)(2,1)S(1)}, bf16[128,768]{1,0:T(8,128)(2,1)S(1)}, u32[]{:S(2)}, u32[]{:S(2)}) collective-permute-start(bf16[128,768]{1,0:T(8,128)(2,1)S(1)} %get-tuple-element.108.own_ref), channel_id=1, source_target_pairs={{0,1},{1,0},{2,3},{3,2},{4,5},{5,4},{6,7},{7,6},{8,9},{9,8},{10,11... | collective-permute-start | bytes 589832 | tf_op jit(solution)/shard_map/ppermute | solution.py:66
  76.0 1.4 %collective-permute-start.15 = (f32[16,128]{1,0:T(8,128)S(1)}, f32[16,128]{1,0:T(8,128)S(1)}, u32[]{:S(2)}, u32[]{:S(2)}) collective-permute-start(f32[16,128]{1,0:T(8,128)S(1)} %get-tuple-element.109.a_ref), channel_id=1, source_target_pairs={{0,1},{1,0},{2,3},{3,2},{4,5},{5,4},{6,7},{7,6},{8,9},{9,8},{10,11... | collective-permute-start | bytes 24584 | tf_op jit(solution)/shard_map/ppermute | solution.py:66

commit v4 on v3

--- a/solution.py
+++ b/solution.py
@@ -226,27 +226,6 @@
     )
 
 
-def weave_kernel(place_ref, same_ref, other_ref, after_ref, then_ref, out_ref):
-    even = (place_ref[1] & 1) == 0
-    for e in range(same_ref.shape[0]):
-        same, other = same_ref[e], other_ref[e]
-        out_ref[2 * e] = jnp.where(even, same, other)
-        out_ref[2 * e + 1] = jnp.where(even, other, same)
-
-
-def weave(place, same, other, after, then):
-    shape = (2 * same.shape[0],) + same.shape[1:]
-    return kernel_call(
-        weave_kernel,
-        0,
-        8 * same.size,
-        [near(same), near(other), near(after), near(then)],
-        [fast(shape, same.dtype)],
-        "weave",
-        place=place,
-    )[0]
-
-
 def sum_kernel(a_ref, b_ref, after_ref, out_ref):
     out_ref[...] = (a_ref[...].astype(F32) + b_ref[...].astype(F32)).astype(out_ref.dtype)
 
@@ -257,16 +236,23 @@
     return kernel_call(sum_kernel, a.size, 6 * a.size, operands, outs, "add_up")[0]
 
 
-def pack_back_kernel(paired, a_ref, b_ref, c_ref, terms_ref, over_ref, after_ref, out_ref):
+def pack_back_kernel(
+    paired, a_ref, b_ref, c_ref, terms_ref, over_ref, after_ref, out_ref, held, sem
+):
     total = a_ref[...].astype(F32) + b_ref[...].astype(F32)
     if paired:
         total = total + c_ref[...].astype(F32)
+    copies = []
     for b in range(out_ref.shape[0]):
         slots = stacked(total[b * CAP : (b + 1) * CAP])
         terms = terms_ref[b]
         if paired:
             terms = terms + over_ref[b].astype(F32)
-        out_ref[b] = jnp.concatenate([slots, terms], axis=0).astype(BF16)
+        held[b] = jnp.concatenate([slots, terms], axis=0).astype(BF16)
+        copies.append(pltpu.make_async_copy(held.at[b], out_ref.at[b], sem.at[b]))
+        copies[-1].start()
+    for copy in copies:
+        copy.wait()
 
 
 def pack_back(a, b, c, terms, over, after, paired):
@@ -277,8 +263,10 @@
         a.size,
         8 * a.size,
         [near(x) for x in (a, b, c, terms, over, after)],
-        [shape_of((blocks, depth, LANES), BF16)],
+        [pltpu.HBM((blocks, depth, LANES), BF16)],
         "pack_back",
+        out_specs=[hbm()],
+        scratch=[pltpu.VMEM((blocks, depth, LANES), BF16), pltpu.SemaphoreType.DMA((blocks,))],
     )[0]
 
 
@@ -398,11 +386,11 @@
 def gather_kernel(parts, place_ref, *refs):
     gates, (stem_in, gain_in, router_in) = refs[:parts], refs[parts : parts + 3]
     stem, gain, inner, small_sem, sem = refs[parts + 3 :]
-    size = (inner.shape[1] - LANES) // 2
+    size = inner.shape[1] - LANES
     copies = [
         pltpu.make_async_copy(stem_in, stem, small_sem.at[0]),
         pltpu.make_async_copy(gain_in, gain, small_sem.at[1]),
-        pltpu.make_async_copy(router_in, inner.at[:, pl.ds(2 * size, LANES)], small_sem.at[2]),
+        pltpu.make_async_copy(router_in, inner.at[:, pl.ds(size, LANES)], small_sem.at[2]),
     ]
     copies += inner_copies(place_ref, gates, inner, size, 0, sem)
     for copy in copies:
@@ -414,7 +402,7 @@
 def gather(place, small, gates, size):
     stem, gain, router = small
     model = router.shape[0]
-    operands = [far_off(a) for a in list(gates) + list(small)]
+    operands = [far_off(gates[0])] + list(gates[1:]) + [far_off(a) for a in small]
     return kernel_call(
         functools.partial(gather_kernel, len(gates)),
         0,
@@ -423,7 +411,7 @@
         [
             fast(stem.shape, BF16),
             fast(gain.shape, F32),
-            fast((model, 2 * size + LANES), BF16),
+            fast((model, size + LANES), BF16),
         ],
         "gather",
         place=place,
@@ -478,28 +466,39 @@
     return jnp.where((place == slot) & (named > 0.0), 1.0, 0.0)
 
 
-def pair_patches(image_ref, top, first, width, channels):
-    blocks = image_ref.shape[0]
-    before = image_ref[jnp.maximum(first - 1, 0), top : top + channels, :].astype(F32)
-    after = image_ref[jnp.minimum(first + 2, blocks - 1), top : top + channels, :].astype(F32)
+def block_getter(paired, place_ref, image_refs):
+    if not paired:
+        return lambda pair, parity: image_refs[0][2 * pair + parity].astype(F32)
+    side = place_ref[1] & 1
+
+    def get(pair, parity):
+        same, other = [ref[pair].astype(F32) for ref in image_refs]
+        return jnp.where(side == parity, same, other)
+
+    return get
+
+
+def pair_patches(get, pair, pairs, width, channels):
+    before = get(jnp.maximum(pair - 1, 0), 1)[:channels]
+    after = get(jnp.minimum(pair + 1, pairs - 1), 0)[:channels]
     window = jnp.concatenate(
         [
-            jnp.where(first > 0, before, 0.0),
-            image_ref[first, top : top + channels, :].astype(F32),
-            image_ref[first + 1, top : top + channels, :].astype(F32),
-            jnp.where(first + 2 < blocks, after, 0.0),
+            jnp.where(pair > 0, before, 0.0),
+            get(pair, 0)[:channels],
+            get(pair, 1)[:channels],
+            jnp.where(pair + 1 < pairs, after, 0.0),
         ],
         axis=1,
     )
-    tok = image_ref.shape[2]
+    tok = window.shape[1] // 4
     column = lane_column((channels, 2 * tok), width)
-    pieces = []
+    pieces_of = []
     for i in range(3):
         for j in range(3):
             piece = shifted(window, (i - 1) * width + j - 1, tok, 2 * tok)
             source = column + (j - 1)
-            pieces.append(jnp.where((source >= 0) & (source < width), piece, 0.0))
-    return jnp.concatenate(pieces, axis=0)
+            pieces_of.append(jnp.where((source >= 0) & (source < width), piece, 0.0))
+    return jnp.concatenate(pieces_of, axis=0)
 
 
 def by_side(pairs, even):
@@ -509,16 +508,22 @@
 
 
 def forward_kernel(
-    paired, parts, width, experts, outs, place_ref, image_ref, stem_ref, gain_ref, _, *refs
+    paired, parts, width, experts, outs, place_ref, *refs
 ):
-    weights, refs = refs[: 2 * parts], refs[2 * parts :]
-    saved_ref, own_out, normed_ref, value_ref, meta_ref, coef_ref, sel_ref, pg_ref, pu_ref = refs[:9]
-    hidden_ref, inner, outer, *out_refs = refs[9:-4]
-    own_ref, save_sem, up_sem, down_sem = refs[-4:]
+    images = 2 if paired else 1
+    image_refs, (stem_ref, gain_ref, first_ref), refs = refs[:images], refs[images : images + 3], refs[images + 3 :]
+    weights, router_in, refs = refs[: 3 * parts], refs[3 * parts], refs[3 * parts + 1 :]
+    refs = refs[1:] if paired else refs
+    saved_ref, normed_ref, value_ref, meta_ref, coef_ref, sel_ref, pg_ref, pu_ref = refs[:8]
+    hidden_ref, inner, outer, *out_refs = refs[8:-4]
+    save_sem, up_sem, down_sem, gate_sem = refs[-4:]
     step = pl.program_id(0)
     size = outer.shape[0]
     up_copies = inner_copies(place_ref, weights[:parts], inner, size, size, up_sem)
-    down_copies = outer_copies(place_ref, weights[parts:], outer, down_sem)
+    down_copies = outer_copies(place_ref, weights[parts : 2 * parts], outer, down_sem)
+    later = inner_copies(place_ref, weights[2 * parts :], inner, size, 0, gate_sem)
+    wide = inner.at[:, pl.ds(2 * size, LANES)]
+    later.append(pltpu.make_async_copy(router_in, wide, gate_sem.at[parts * PIECES]))
 
     def arrive(copies):
         @pl.when(step == 0)
@@ -528,26 +533,27 @@
 
     @pl.when(step == 0)
     def _():
-        for copy in up_copies + down_copies:
+        for copy in up_copies + down_copies + later:
             copy.start()
 
     chunk = GROUP * CAP
     here = pl.ds(pl.multiple_of(step * chunk, chunk), chunk)
-    top = 0
-    channels = image_ref.shape[1] - 2
+    channels = image_refs[0].shape[1] - 2
+    pairs = images * image_refs[0].shape[0] // 2
+    get = block_getter(paired, place_ref, image_refs)
     mine = place_ref[0].astype(F32)
     even = (place_ref[1] & 1) == 0
     taken, others = [], []
     for q in range(GROUP // 2):
-        first = step * GROUP + 2 * q
-        lines = [image_ref[first + n, top + channels :, :].astype(F32) for n in range(2)]
+        pair = step * (GROUP // 2) + q
+        lines = [get(pair, n)[channels:] for n in range(2)]
         named_by = [jnp.concatenate([line[k : k + 1] for line in lines], axis=1) for k in range(2)]
         named = jnp.where((named_by[0] == mine) | (named_by[1] == mine), 1.0, 0.0)
         sel = pair_selection(named)
         sel_ref[step * (GROUP // 2) + q] = sel.astype(BF16)
         other = named_by[0] + named_by[1] - mine
         others.append(jnp.sum(sel * other, axis=1, keepdims=True))
-        patches = pair_patches(image_ref, top, first, width, channels)
+        patches = pair_patches(get, pair, pairs, width, channels)
         taken.append(mm_t(sel.astype(BF16), patches.astype(BF16)))
     bands = 2 if paired else 1
     deep = chunk // bands
@@ -573,22 +579,10 @@
     own_part = normed_ref.at[:, pl.ds(0, saved_ref.shape[1])]
     save = pltpu.make_async_copy(own_part, saved_ref.at[here, :], save_sem.at[0])
     save.start()
-    own_save = pltpu.make_async_copy(own_ref, own_out, save_sem.at[1])
-
-    @pl.when(step == 0)
-    def _():
-        me = place_ref[1]
-        first = me // 2 * 2
-        tok = image_ref.shape[2]
-        own = pair_patches(image_ref, top, first, width, channels)
-        own = jnp.where(me == first, own[:, :tok], own[:, tok:]).astype(BF16)
-        own_ref[...] = t_mm(own, stem_ref[:, : own_ref.shape[1]]).astype(BF16)
-        own_save.start()
-
     for normed in normeds:
-        gated.append(mm(normed, inner[:, :size]))
+        gated.append(mm(normed, first_ref[:, :size]))
     for line, normed, other, scale in zip(lines, normeds, others, scales):
-        logits = mm(normed, inner[:, 2 * size :])
+        logits = mm(normed, first_ref[:, size:])
         lane = lax.broadcasted_iota(jnp.int32, logits.shape, 1)
         again = jnp.where(lane >= experts, lane - experts, lane).astype(F32)
         lane = lane.astype(F32)
@@ -620,22 +614,25 @@
         else:
             ref[here, :] = part
     save.wait()
-
-    @pl.when(step == 0)
-    def _():
-        own_save.wait()
-
-
-def forward(place, image, gathered, weights, size, half, columns, paired, width, experts):
-    blocks, _, tok = image.shape
+    arrive(later)
+
+
+def forward(place, images, gathered, router, weights, size, columns, after, paired, width, experts):
+    blocks = sum(image.shape[0] for image in images)
+    tok = images[0].shape[2]
     slots, chunk = blocks * CAP, GROUP * CAP
     stem, gain, inner = gathered
     model = stem.shape[1]
-    parts = len(weights) // 2
-    operands = [near(image), near(stem), near(gain), near(inner)] + [far_off(w) for w in weights]
+    parts = len(weights) // 3
+    operands = [near(a) for a in list(images) + [stem, gain, inner]]
+    specs = [vmem()] * len(operands) + [hbm()] * (len(weights) + 1)
+    operands += [far_off(w) if k % parts == 0 else w for k, w in enumerate(weights)]
+    operands.append(far_off(router))
+    if paired:
+        operands.append(near(after))
+        specs.append(vmem())
     outs = [
         pltpu.HBM((slots, columns[0]), BF16),
-        pltpu.HBM((tok, half), BF16),
         fast((chunk, model), BF16),
         fast((slots, model), BF16),
         fast((slots, LANES), F32),
@@ -644,7 +641,7 @@
         fast((slots, size), BF16),
         fast((slots, size), BF16),
         fast((slots, size), BF16),
-        fast(inner.shape, BF16),
+        fast((model, 2 * size + LANES), BF16),
         fast((size, model), BF16),
     ]
     outs += [fast((slots // 2 if paired else slots, n), BF16) for n in columns]
@@ -657,22 +654,47 @@
         grid_spec=pltpu.PrefetchScalarGridSpec(
             num_scalar_prefetch=1,
             grid=(blocks // GROUP,),
-            in_specs=[vmem()] * 4 + [hbm()] * len(weights),
-            out_specs=[hbm()] * 2 + [vmem()] * (len(outs) - 2),
+            in_specs=specs,
+            out_specs=[hbm()] + [vmem()] * (len(outs) - 1),
             scratch_shapes=[
-                pltpu.VMEM((tok, half), BF16),
-                pltpu.SemaphoreType.DMA((2,)),
+                pltpu.SemaphoreType.DMA((1,)),
                 pltpu.SemaphoreType.DMA((parts * PIECES,)),
                 pltpu.SemaphoreType.DMA((parts * PIECES,)),
+                pltpu.SemaphoreType.DMA((parts * PIECES + 1,)),
             ],
         ),
         out_shape=outs,
-        input_output_aliases={4: 10},
         name="forward",
     )(place, *operands)
 
 
-def outputs_kernel(meta_ref, hidden_ref, outer, near_ref, far_ref):
+def own_stem_kernel(paired, width, place_ref, *refs):
+    image_refs, (stem_ref, own_ref) = refs[:-2], refs[-2:]
+    me = place_ref[1]
+    channels = image_refs[0].shape[1] - 2
+    tok = image_refs[0].shape[2]
+    pairs = len(image_refs) * image_refs[0].shape[0] // 2
+    own = pair_patches(block_getter(paired, place_ref, image_refs), me // 2, pairs, width, channels)
+    own = jnp.where(me % 2 == 0, own[:, :tok], own[:, tok:]).astype(BF16)
+    own_ref[...] = t_mm(own, stem_ref[:, : own_ref.shape[1]]).astype(BF16)
+
+
+def own_stem_of(place, images, stem, half, paired, width):
+    tok = images[0].shape[2]
+    return kernel_call(
+        functools.partial(own_stem_kernel, paired, width),
+        0,
+        LANES,
+        [near(a) for a in list(images) + [stem]],
+        [pltpu.HBM((tok, half), BF16)],
+        "own_stem",
+        place=place,
+        out_specs=[whole((tok, half))],
+    )[0]
+
+
+def outputs_kernel(width, place_ref, meta_ref, hidden_ref, outer, same_ref, other_ref, stem_ref, near_ref, far_ref, own_ref):
+    own_stem_kernel(True, width, place_ref, same_ref, other_ref, stem_ref, own_ref)
     count, half = near_ref.shape
     gate = meta_ref[:count, 0:1]
     hidden = hidden_ref[:count, :]
@@ -680,15 +702,18 @@
     far_ref[...] = (gate * mm(hidden, outer[:, half:])).astype(BF16)
 
 
-def outputs(meta, hidden, outer):
+def outputs(place, meta, hidden, outer, images, stem, width):
     count, half = hidden.shape[0] // 2, outer.shape[1] // 2
-    return kernel_call(
-        outputs_kernel,
+    tok = images[0].shape[2]
+    return kernel_call(
+        functools.partial(outputs_kernel, width),
         0,
         LANES,
-        [near(meta), near(hidden), near(outer)],
-        [fast((count, half), BF16)] * 2,
+        [near(a) for a in [meta, hidden, outer] + list(images) + [stem]],
+        [fast((count, half), BF16)] * 2 + [pltpu.HBM((tok, half), BF16)],
         "outputs",
+        place=place,
+        out_specs=[vmem()] * 2 + [whole((tok, half))],
     )
 
 
@@ -916,7 +941,7 @@
         near_grads_kernel,
         20_000_000_000,
         LANES,
-        [far_off(a) for a in (normed, ggp, gup, hg, cot)] + [after],
+        [far_off(a) for a in (normed, ggp, gup, hg, cot, after)],
         [pltpu.HBM((half, 2 * size), F32)] * 2
         + [pltpu.HBM((2 * size, half), F32)],
         "near_grads",
@@ -1083,22 +1108,24 @@
     gathered = gather(place, small, gate_parts, size)
     if paired:
         joined = other_core(same_cot)
-        image = weave(place, image, other_shard(image), joined, gathered[1])
+        images = [image, other_shard(image)]
         cots = [[same_cot], [joined]]
         far_cot = other_shard(same_cot)
     elif cores == 2:
-        cots = [[same_cot], [other_core(same_cot)]]
+        images, joined = [image], other_core(same_cot)
+        cots = [[same_cot], [joined]]
     else:
+        images = [image]
         joined = lax.all_gather(same_cot, "rep", axis=1, tiled=True)
         cots = [[jnp.roll(joined, -column, 1)]]
-    weights = list(up_parts) + list(down_parts)
+    weights = list(up_parts) + list(down_parts) + list(gate_parts)
     columns = [w.shape[1] for w in down_parts]
-    kept, own_stem, normed, value, meta, coef, sel, pg, pu, hidden, inner, outer, *outs = forward(
-        place, image, gathered, weights, size, half, columns, paired, width, experts
+    kept, normed, value, meta, coef, sel, pg, pu, hidden, inner, outer, *outs = forward(
+        place, images, gathered, small[2], weights, size, columns, joined, paired, width, experts
     )
     stem, gain, _ = gathered
     if paired:
-        own, away = outputs(meta, hidden, outer)
+        own, away, own_stem = outputs(place, meta, hidden, outer, images, stem, width)
         far_cot, own = lax.optimization_barrier((far_cot, own))
         cots[0].append(far_cot)
         cots[1].append(other_core(far_cot))
@@ -1107,10 +1134,12 @@
     elif cores == 2:
         own, away = outs[0], other_core(outs[1])
         over = own
+        own_stem = own_stem_of(place, images, stem, half, paired, width)
     else:
         turned = jnp.roll(outs[0], column, 1)
         own = lax.psum_scatter(turned, "rep", scatter_dimension=1, tiled=True)
         away = over = jnp.zeros_like(own)
+        own_stem = own_stem_of(place, images, stem, half, paired, width)
     acts = [value, meta, coef, pg, pu]
     ggp, gup, hg, held, proj, ggp_here, gup_here, hg_here = backward(
         stem, gain, inner, outer, acts, cots, experts

time: 79.1 us -> 78.9 us (level)
    pallas_call x15 -> x14, Pallas kernels: 35.5 us -> 35.5 us  [kernel_call(): call(kernel, flops, moved, mib, grid_spec=pltpu.PrefetchScalarGridSpec(nu...]
where the time goes in v4:
time: 78.9 us; the launch traced here: 78.5 us
  Pallas kernels  48.1 us (61%)
  starting transfers between devices  18 us (23%)
  waiting for transfers between devices  9.88 us (13%)
  local copies, waits for them, and re-layouts  1.54 us (2%)
  between operations  0.86 us (1%)
    pallas_call x14, Pallas kernels, kernel_call(): call(kernel, flops, moved, mib, grid_spec=pltpu.PrefetchScalarGridSpec(nu...  35.5 us
    all_to_all x2, starting transfers between devices, exchange(): lax.all_to_all(values, 'exp', split_axis=0, concat_axis=0, tiled=True, ax...  10.9 us
    all_to_all x2, waiting for transfers between devices, exchange(): lax.all_to_all(values, 'exp', split_axis=0, concat_axis=0, tiled=True, ax...  8.05 us
    pallas_call x1, Pallas kernels, forward(): pl.pallas_call(functools.partial(forward_kernel, paired, parts, width, ex...  7.97 us
    ppermute x4, starting transfers between devices, other_shard(): lax.ppermute(values, 'exp', [(i, i ^ 1) for i in range(lax.axis_size('exp...  4.71 us
    pallas_call x1, Pallas kernels, fill(): pl.pallas_call(fill_kernel, compiler_params=pltpu.CompilerParams(vmem_lim...  4.65 us
    ppermute x12, starting transfers between devices, other_core(): return lax.ppermute(values, 'rep', [(0, 1), (1, 0)])  2.38 us
  transfers between devices with their start and end apart: 18, of which 4 were waited for; matrix products, arithmetic and copies ran while one was open for 2% of the time, Pallas kernels for 56%

profile of v4, /device:TPU:0, one launch (start us, length us, event | category | flops | bytes accessed | tf_op | source)
XLA Modules:
  0.0 78.5 jit_solution(17210721343604729665)
XLA Ops:
  0.6 2.2 %pack.1.after.after_ref = bf16[8,258,128]{2,1,0:T(8,128)(2,1)} custom-call(bf16[2,16,64]{2,1,0:T(8,128)(2,1)} %latent_ref.1, s32[2,128]{1,0:T(2,128)} %bitcast.4, bf16[128,1536]{1,0:T(8,128)(2,1)} %cot_ref.3), custom_call_target="tpu_custom_call" | custom-call | flops 62914560 | bytes 1056768 | tf_op jit(solution)/shard_map/pack/pallas_call | solution.py:107
  2.9 7.3 %all-to-all-start = ((bf16[8,258,128]{2,1,0:T(8,128)(2,1)}), bf16[8,258,128]{2,1,0:T(8,128)(2,1)S(1)}, u32[]{:S(2)}, u32[]{:S(2)}) async-start(bf16[8,258,128]{2,1,0:T(8,128)(2,1)} %pack.1.after.after_ref), calls=%async_computation | async-start | bytes 1081344 | tf_op jit(solution)/shard_map/all_to_all | solution.py:79
  10.2 0.1 pad_add_fusion.place_ref
  10.2 0.0 copy-start.4
  10.2 0.0 copy-start.3
  10.2 4.4 %far_weights.1 = (bf16[768,768]{1,0:T(8,128)(2,1)}, bf16[768,768]{1,0:T(8,128)(2,1)}, bf16[768,768]{1,0:T(8,128)(2,1)}) custom-call(s32[3]{0:T(128)S(1)} %pad_add_fusion.place_ref, bf16[768,1536]{1,0:T(8,128)(2,1)} %refs_9_.1, bf16[768,1536]{1,0:T(8,128)(2,1)} %refs_5_.1, bf16[1536,768]{1,0:T(8,128)(2,1)} %refs_7_.1, bf16[8,258,128]{2,1,0:T(8,128)(2,1)} %pack.1.after.after_ref), custom_call_target="tpu_custom_call" | custom-call | bytes 128 | tf_op jit(solution)/shard_map/far_weights/pallas_call | solution.py:107
  14.6 0.1 collective-permute-start.1
  14.7 0.5 collective-permute-start.2
  15.2 0.1 collective-permute-start.3
  15.3 0.0 copy-done.4
  15.3 0.6 broadcast_in_dim.3.gain_in
  15.9 0.0 copy-done.3
  15.9 0.9 %copy.17.router_in = bf16[1536,8]{1,0:T(8,128)(2,1)} copy(bf16[1536,8]{0,1:T(8,128)(2,1)S(1)} %copy-done.3) | data formatting | bytes 49152 | tf_op args[3]
  16.8 3.1 %params.1 = (bf16[144,1536]{1,0:T(8,128)(2,1)}, f32[1,1536]{1,0:T(1,128)}, bf16[1536,128]{1,0:T(8,128)(2,1)}, bf16[320,128]{1,0:T(8,128)(2,1)}, bf16[128,768]{1,0:T(8,128)(2,1)}) custom-call(s32[3]{0:T(128)S(1)} %pad_add_fusion.place_ref, bf16[144,1536]{1,0:T(8,128)(2,1)} %stem_in.1, f32[1,1536]{1,0:T(1,128)} %broadcast_in_dim.3.gain_in, ...), custom_call_target="tpu_custom_call" | custom-call | bytes 128 | tf_op jit(solution)/shard_map/params/pallas_call | solution.py:107
  19.9 5.1 %all-to-all-done.packed_ref = bf16[8,258,128]{2,1,0:T(8,128)(2,1)S(1)} async-done(((bf16[8,258,128]{2,1,0:T(8,128)(2,1)}), bf16[8,258,128]{2,1,0:T(8,128)(2,1)S(1)}, u32[]{:S(2)}, u32[]{:S(2)}) %all-to-all-start) | async-done | bytes 528416 | tf_op jit(solution)/shard_map/all_to_all | solution.py:79
  25.0 0.1 collective-permute-start.4
  25.1 1.6 %collective-permute-start = (bf16[8,18,128]{2,1,0:T(8,128)(2,1)S(1)}, bf16[8,18,128]{2,1,0:T(8,128)(2,1)S(1)}, u32[]{:S(2)}, u32[]{:S(2)}) collective-permute-start(bf16[8,18,128]{2,1,0:T(8,128)(2,1)S(1)} %get-tuple-element.61.refs_0_.same_ref), channel_id=1, source_target_pairs={{0,2},{2,0},{4,6},{6,4},{8,10},{10,8},{12,14},{14,12},{16,18},{18,... | collective-permute-start | bytes 110600 | tf_op jit(solution)/shard_map/ppermute | solution.py:70
  26.7 0.0 collective-permute-done.1.refs_1_.refs_10_
  26.7 0.5 collective-permute-start.5
  27.2 2.1 %gather.1 = (bf16[144,1536]{1,0:T(8,128)(2,1)S(1)}, f32[1,1536]{1,0:T(1,128)S(1)}, bf16[1536,896]{1,0:T(8,128)(2,1)S(1)}) custom-call(s32[3]{0:T(128)S(1)} %pad_add_fusion.place_ref, bf16[768,1536]{1,0:T(8,128)(2,1)} %refs_9_.1, bf16[768,768]{1,0:T(8,128)(2,1)S(1)} %collective-permute-done.1.refs_1_.refs_10_, bf16[144,1536]{1,0:T(8,128)(2,1)} %get-tuple-element.63.refs_2_, ...), custom_call_target="tpu_custom_call" | custom-call | bytes 128 | tf_op jit(solution)/shard_map/gather/pallas_call | solution.py:107
  29.4 0.0 collective-permute-done.refs_1_.other_ref
  29.4 0.0 collective-permute-done.2.refs_6_
  29.4 0.0 collective-permute-done.3.refs_8_
  29.4 0.0 collective-permute-done.4.refs_12_.refs_2_.refs_0_
  29.4 8.0 %forward.1 = (bf16[640,768]{1,0:T(8,128)(2,1)}, bf16[640,1536]{1,0:T(8,128)(2,1)S(1)}, bf16[640,1536]{1,0:T(8,128)(2,1)S(1)}, f32[640,128]{1,0:T(8,128)S(1)}, f3...) custom-call(s32[3]{0:T(128)S(1)} %pad_add_fusion.place_ref, ...), custom_call_target="tpu_custom_call" | custom-call | flops 99999997952 | bytes 128 | tf_op jit(solution)/shard_map/forward/pallas_call | solution.py:648
  37.4 0.1 collective-permute-start.7
  37.5 1.7 %outputs.1 = (bf16[320,768]{1,0:T(8,128)(2,1)S(1)}, bf16[320,768]{1,0:T(8,128)(2,1)S(1)}, bf16[128,768]{1,0:T(8,128)(2,1)}) custom-call(s32[3]{0:T(128)S(1)} %pad_add_fusion.place_ref, f32[640,128]{1,0:T(8,128)S(1)} %get-tuple-element.71.meta_ref, bf16[640,768]{1,0:T(8,128)(2,1)S(1)} %get-tuple-element.72.hidden_ref, ...), custom_call_target="tpu_custom_call" | custom-call | bytes 128 | tf_op jit(solution)/shard_map/outputs/pallas_call | solution.py:107
  39.1 0.8 %collective-permute-done.5.refs_1_ = bf16[320,768]{1,0:T(8,128)(2,1)S(1)} collective-permute-done((bf16[320,768]{1,0:T(8,128)(2,1)S(1)}, bf16[320,768]{1,0:T(8,128)(2,1)S(1)}, u32[]{:S(2)}, u32[]{:S(2)}) %collective-permute-start.5) | collective-permute-done | bytes 491552 | tf_op jit(solution)/shard_map/ppermute | solution.py:70
  40.0 0.0 collective-permute-start.9
  40.0 0.5 collective-permute-start.6
  40.5 0.0 collective-permute-done.7.b_ref
  40.5 0.1 add_up.1
  40.6 1.4 %collective-permute-start.8 = (bf16[320,768]{1,0:T(8,128)(2,1)S(1)}, bf16[320,768]{1,0:T(8,128)(2,1)S(1)}, u32[]{:S(2)}, u32[]{:S(2)}) collective-permute-start(bf16[320,768]{1,0:T(8,128)(2,1)S(1)} %add_up.1), channel_id=1, source_target_pairs={{0,2},{2,0},{4,6},{6,4},{8,10},{10,8},{12,14},{14,12},{16,18},{18,... | collective-permute-start | bytes 1474568 | tf_op jit(solution)/shard_map/ppermute | solution.py:70
  42.0 0.0 collective-permute-done.9.refs_3_.refs_1_
  42.0 0.0 copy-start
  42.0 7.2 %backward.1 = (bf16[640,768]{1,0:T(8,128)(2,1)}, bf16[640,768]{1,0:T(8,128)(2,1)}, bf16[640,768]{1,0:T(8,128)(2,1)}, bf16[640,768]{1,0:T(8,128)(2,1)}, bf16[640,...) custom-call(bf16[144,1536]{1,0:T(8,128)(2,1)S(1)} %get-tuple-element, ...), custom_call_target="tpu_custom_call" | custom-call | flops 6039797760 | bytes 16908288 | tf_op jit(solution)/shard_map/backward/pallas_call | solution.py:107
  49.2 0.0 copy-done
  49.2 1.1 %to_image.1 = (f32[8,16,128]{2,1,0:T(8,128)S(1)}, bf16[8,16,128]{2,1,0:T(8,128)(2,1)S(1)}) custom-call(s32[3]{0:T(128)S(1)} %pad_add_fusion.place_ref, bf16[640,144]{1,0:T(8,128)(2,1)S(1)} %get-tuple-element.87.proj_ref, bf16[8,80,256]{2,1,0:T(8,128)(2,1)S(1)} %get-tuple-element.88.sel_ref, bf16[144,1536]{1,0:T(8,128)(2,1)S(1)} %get-tuple-element.65.refs_2_.stem_ref, ...), custom_call_target="tpu_custom_call" | custom-call | flops 47185920 | bytes 1179648 | tf_op jit(solution)/shard_map/to_image/pallas_call | solution.py:107
  50.4 1.2 %collective-permute-start.10 = (bf16[8,16,128]{2,1,0:T(8,128)(2,1)S(1)}, bf16[8,16,128]{2,1,0:T(8,128)(2,1)S(1)}, u32[]{:S(2)}, u32[]{:S(2)}) collective-permute-start(bf16[8,16,128]{2,1,0:T(8,128)(2,1)S(1)} %get-tuple-element.91), channel_id=1, source_target_pairs={{0,2},{2,0},{4,6},{6,4},{8,10},{10,8},{12,14},{14,12},{16,18},{18,... | collective-permute-start | bytes 98312 | tf_op jit(solution)/shard_map/ppermute | solution.py:70
  51.6 3.4 %far_grads.1 = (bf16[768,768]{1,0:T(8,128)(2,1)S(1)}, bf16[768,768]{1,0:T(8,128)(2,1)}, bf16[768,768]{1,0:T(8,128)(2,1)S(1)}) custom-call(bf16[640,1536]{1,0:T(8,128)(2,1)S(1)} %get-tuple-element.92.normed, bf16[640,768]{1,0:T(8,128)(2,1)S(1)} %get-tuple-element.93.ggp, bf16[640,768]{1,0:T(8,128)(2,1)S(1)} %get-tuple-element.94.gup, ...), custom_call_target="tpu_custom_call" | custom-call | flops 2264924160 | bytes 9830400 | tf_op jit(solution)/shard_map/far_grads/pallas_call | solution.py:107
  55.0 0.0 collective-permute-start.12
  55.0 0.5 collective-permute-start.13
  55.5 0.0 collective-permute-done.6.b_ref
  55.5 0.0 collective-permute-start.11
  55.5 0.0 collective-permute-done.10.over_ref
  55.5 0.0 collective-permute-done.8.c_ref
  55.5 0.9 %pack_back.1.after_ref = bf16[8,256,128]{2,1,0:T(8,128)(2,1)} custom-call(bf16[320,768]{1,0:T(8,128)(2,1)S(1)} %get-tuple-element.77.after_ref.a_ref, bf16[320,768]{1,0:T(8,128)(2,1)S(1)} %collective-permute-done.6.b_ref, bf16[320,768]{1,0:T(8,128)(2,1)S(1)} %collective-permute-done.8.c_ref, f32[8,16,128]{2,1,0:T(8,128)S(1)} %get-tuple-element.90.terms_ref, ...), custom_call_target="tpu_custom_call" | custom-call | flops 245760 | bytes 1966080 | tf_op jit(solution)/shard_map/pack_back/pallas_call | solution.py:107
  56.5 3.6 %all-to-all-start.1 = ((bf16[8,256,128]{2,1,0:T(8,128)(2,1)}), bf16[8,256,128]{2,1,0:T(8,128)(2,1)S(1)}, u32[]{:S(2)}, u32[]{:S(2)}) async-start(bf16[8,256,128]{2,1,0:T(8,128)(2,1)} %pack_back.1.after_ref), calls=%async_computation.1 | async-start | bytes 1048576 | tf_op jit(solution)/shard_map/all_to_all | solution.py:79
  60.1 7.5 %near_grads.1 = (f32[768,1536]{1,0:T(8,128)}, f32[768,1536]{1,0:T(8,128)}, f32[1536,768]{1,0:T(8,128)}) custom-call(s32[3]{0:T(128)S(1)} %pad_add_fusion.place_ref, bf16[640,768]{1,0:T(8,128)(2,1)} %get-tuple-element.99.normed, bf16[640,768]{1,0:T(8,128)(2,1)} %get-tuple-element.100.ggp, bf16[640,768]{1,0:T(8,128)(2,1)} %get-tuple-element.101.gup, ...), custom_call_target="tpu_custom_call" | custom-call | flops 20000000000 | bytes 128 | tf_op jit(solution)/shard_map/near_grads/pallas_call | solution.py:107
  67.7 0.0 collective-permute-done.12.up_in
  67.7 0.0 collective-permute-done.13.down_in
  67.7 0.0 collective-permute-done.11.gate_in
  67.7 0.0 copy-start.1
  67.7 0.0 copy-start.2
  67.7 4.7 %fill.1 = (f32[768,1536]{1,0:T(8,128)}, f32[768,1536]{1,0:T(8,128)}, f32[1536,768]{1,0:T(8,128)}, f32[8,128]{1,0:T(8,128)S(1)}) custom-call(s32[3]{0:T(128)S(1)} %pad_add_fusion.place_ref, bf16[768,768]{1,0:T(8,128)(2,1)} %collective-permute-done.11.gate_in, ...), custom_call_target="tpu_custom_call", output_to_operand_aliasing={{0}: (4, {}), {1}: (5, {}), {2}: (6, {})} | custom-call | flops 10000000000 | bytes 128 | tf_op jit(solution)/shard_map/fill/pallas_call | solution.py:992
  72.4 2.9 %all-to-all-done.1.back_ref = bf16[8,256,128]{2,1,0:T(8,128)(2,1)S(1)} async-done(((bf16[8,256,128]{2,1,0:T(8,128)(2,1)}), bf16[8,256,128]{2,1,0:T(8,128)(2,1)S(1)}, u32[]{:S(2)}, u32[]{:S(2)}) %all-to-all-start.1) | async-done | bytes 524320 | tf_op jit(solution)/shard_map/all_to_all | solution.py:79
  75.3 0.0 copy-done.1
  75.3 0.0 copy-done.2
  75.3 0.3 mixed.1
  75.6 0.1 collective-permute-start.14
  75.7 0.5 collective-permute-start.15
  76.2 0.9 %collective-permute-done.15.b_ref = f32[16,128]{1,0:T(8,128)S(1)} collective-permute-done((f32[16,128]{1,0:T(8,128)S(1)}, f32[16,128]{1,0:T(8,128)S(1)}, u32[]{:S(2)}, u32[]{:S(2)}) %collective-permute-start.15) | collective-permute-done | bytes 8224 | tf_op jit(solution)/shard_map/ppermute | solution.py:66
  77.2 0.0 collective-permute-done.14.away_ref
  77.2 1.3 %join.1 = (bf16[128,1536]{1,0:T(8,128)(2,1)}, f32[2,16,64]{2,1,0:T(8,128)}) custom-call(s32[3]{0:T(128)S(1)} %pad_add_fusion.place_ref, bf16[128,768]{1,0:T(8,128)(2,1)S(1)} %get-tuple-element.108.own_ref, bf16[128,768]{1,0:T(8,128)(2,1)S(1)} %collective-permute-done.14.away_ref, f32[16,128]{1,0:T(8,128)S(1)} %get-tuple-element.109.a_ref, ...), custom_call_target="tpu_custom_call" | custom-call | bytes 786432 | tf_op jit(solution)/shard_map/join/pallas_call | solution.py:107
  (1 shorter events, 0.0 us)
Async XLA Ops:
  2.9 22.1 %all-to-all-start = ((bf16[8,258,128]{2,1,0:T(8,128)(2,1)}), bf16[8,258,128]{2,1,0:T(8,128)(2,1)S(1)}, u32[]{:S(2)}, u32[]{:S(2)}) async-start(bf16[8,258,128]{2,1,0:T(8,128)(2,1)} %pack.1.after.after_ref), calls=%async_computation | async-start | bytes 1081344 | tf_op jit(solution)/shard_map/all_to_all | solution.py:79
  10.2 5.0 %copy-start.4 = (f32[1536]{0:T(1024)S(1)}, f32[1536]{0:T(1024)}, u32[]{:S(2)}) copy-start(f32[1536]{0:T(1024)} %param.11) | copy-start | bytes 18436
  10.2 5.6 %copy-start.3 = (bf16[1536,8]{0,1:T(8,128)(2,1)S(1)}, bf16[1536,8]{0,1:T(8,128)(2,1)}, u32[]{:S(2)}) copy-start(bf16[1536,8]{0,1:T(8,128)(2,1)} %param.12) | copy-start | bytes 73732
  14.6 12.1 %collective-permute-start.1 = (bf16[768,768]{1,0:T(8,128)(2,1)}, bf16[768,768]{1,0:T(8,128)(2,1)S(1)}, u32[]{:S(2)}, u32[]{:S(2)}) collective-permute-start(bf16[768,768]{1,0:T(8,128)(2,1)} %get-tuple-element.62), channel_id=1, source_target_pairs={{0,1},{1,0},{2,3},{3,2},{4,5},{5,4},{6,7},{7,6},{8,9},{9,8},{10,11... | collective-permute-start | bytes 3538952 | tf_op jit(solution)/shard_map/ppermute | solution.py:66
  14.7 14.7 %collective-permute-start.2 = (bf16[768,768]{1,0:T(8,128)(2,1)}, bf16[768,768]{1,0:T(8,128)(2,1)S(1)}, u32[]{:S(2)}, u32[]{:S(2)}) collective-permute-start(bf16[768,768]{1,0:T(8,128)(2,1)} %get-tuple-element.68), channel_id=1, source_target_pairs={{0,1},{1,0},{2,3},{3,2},{4,5},{5,4},{6,7},{7,6},{8,9},{9,8},{10,11... | collective-permute-start | bytes 3538952 | tf_op jit(solution)/shard_map/ppermute | solution.py:66
  15.2 14.2 %collective-permute-start.3 = (bf16[768,768]{1,0:T(8,128)(2,1)}, bf16[768,768]{1,0:T(8,128)(2,1)}, u32[]{:S(2)}, u32[]{:S(2)}) collective-permute-start(bf16[768,768]{1,0:T(8,128)(2,1)} %get-tuple-element.69), channel_id=1, source_target_pairs={{0,1},{1,0},{2,3},{3,2},{4,5},{5,4},{6,7},{7,6},{8,9},{9,8},{10,11... | collective-permute-start | bytes 3538952 | tf_op jit(solution)/shard_map/ppermute | solution.py:66
  25.0 4.4 %collective-permute-start.4 = (bf16[320,768]{1,0:T(8,128)(2,1)S(1)}, bf16[320,768]{1,0:T(8,128)(2,1)S(1)}, u32[]{:S(2)}, u32[]{:S(2)}) collective-permute-start(bf16[320,768]{1,0:T(8,128)(2,1)S(1)} %get-tuple-element.70.refs_0_), channel_id=1, source_target_pairs={{0,1},{1,0},{2,3},{3,2},{4,5},{5,4},{6,7},{7,6},{8,9},{9,8},{10,11... | collective-permute-start | bytes 1474568 | tf_op jit(solution)/shard_map/ppermute | solution.py:66
  25.1 4.2 %collective-permute-start = (bf16[8,18,128]{2,1,0:T(8,128)(2,1)S(1)}, bf16[8,18,128]{2,1,0:T(8,128)(2,1)S(1)}, u32[]{:S(2)}, u32[]{:S(2)}) collective-permute-start(bf16[8,18,128]{2,1,0:T(8,128)(2,1)S(1)} %get-tuple-element.61.refs_0_.same_ref), channel_id=1, source_target_pairs={{0,2},{2,0},{4,6},{6,4},{8,10},{10,8},{12,14},{14,12},{16,18},{18,... | collective-permute-start | bytes 110600 | tf_op jit(solution)/shard_map/ppermute | solution.py:70
  26.7 13.3 %collective-permute-start.5 = (bf16[320,768]{1,0:T(8,128)(2,1)S(1)}, bf16[320,768]{1,0:T(8,128)(2,1)S(1)}, u32[]{:S(2)}, u32[]{:S(2)}) collective-permute-start(bf16[320,768]{1,0:T(8,128)(2,1)S(1)} %get-tuple-element.70.refs_0_), channel_id=1, source_target_pairs={{0,2},{2,0},{4,6},{6,4},{8,10},{10,8},{12,14},{14,12},{16,18},{18,... | collective-permute-start | bytes 1474568 | tf_op jit(solution)/shard_map/ppermute | solution.py:70
  37.4 3.1 %collective-permute-start.7 = (bf16[320,768]{1,0:T(8,128)(2,1)S(1)}, bf16[320,768]{1,0:T(8,128)(2,1)S(1)}, u32[]{:S(2)}, u32[]{:S(2)}) collective-permute-start(bf16[320,768]{1,0:T(8,128)(2,1)S(1)} %get-tuple-element.80), channel_id=1, source_target_pairs={{0,1},{1,0},{2,3},{3,2},{4,5},{5,4},{6,7},{7,6},{8,9},{9,8},{10,11... | collective-permute-start | bytes 1474568 | tf_op jit(solution)/shard_map/ppermute | solution.py:66
  40.0 2.0 %collective-permute-start.9 = (bf16[320,768]{1,0:T(8,128)(2,1)S(1)}, bf16[320,768]{1,0:T(8,128)(2,1)S(1)}, u32[]{:S(2)}, u32[]{:S(2)}) collective-permute-start(bf16[320,768]{1,0:T(8,128)(2,1)S(1)} %collective-permute-done.5.refs_1_), channel_id=1, source_target_pairs={{0,1},{1,0},{2,3},{3,2},{4,5},{5,4},{6,7},{7,6},{8,9},{9,8},{10,11... | collective-permute-start | bytes 1474568 | tf_op jit(solution)/shard_map/ppermute | solution.py:66
  40.0 15.5 %collective-permute-start.6 = (bf16[320,768]{1,0:T(8,128)(2,1)S(1)}, bf16[320,768]{1,0:T(8,128)(2,1)S(1)}, u32[]{:S(2)}, u32[]{:S(2)}) collective-permute-start(bf16[320,768]{1,0:T(8,128)(2,1)S(1)} %get-tuple-element.78), channel_id=1, source_target_pairs={{0,1},{1,0},{2,3},{3,2},{4,5},{5,4},{6,7},{7,6},{8,9},{9,8},{10,11... | collective-permute-start | bytes 1474568 | tf_op jit(solution)/shard_map/ppermute | solution.py:66
  40.6 14.9 %collective-permute-start.8 = (bf16[320,768]{1,0:T(8,128)(2,1)S(1)}, bf16[320,768]{1,0:T(8,128)(2,1)S(1)}, u32[]{:S(2)}, u32[]{:S(2)}) collective-permute-start(bf16[320,768]{1,0:T(8,128)(2,1)S(1)} %add_up.1), channel_id=1, source_target_pairs={{0,2},{2,0},{4,6},{6,4},{8,10},{10,8},{12,14},{14,12},{16,18},{18,... | collective-permute-start | bytes 1474568 | tf_op jit(solution)/shard_map/ppermute | solution.py:70
  42.0 7.2 %copy-start = (bf16[128,768]{1,0:T(8,128)(2,1)S(1)}, bf16[128,768]{1,0:T(8,128)(2,1)}, u32[]{:S(2)}) copy-start(bf16[128,768]{1,0:T(8,128)(2,1)} %get-tuple-element.89.cot_ref) | copy-start | bytes 589828
  50.4 5.2 %collective-permute-start.10 = (bf16[8,16,128]{2,1,0:T(8,128)(2,1)S(1)}, bf16[8,16,128]{2,1,0:T(8,128)(2,1)S(1)}, u32[]{:S(2)}, u32[]{:S(2)}) collective-permute-start(bf16[8,16,128]{2,1,0:T(8,128)(2,1)S(1)} %get-tuple-element.91), channel_id=1, source_target_pairs={{0,2},{2,0},{4,6},{6,4},{8,10},{10,8},{12,14},{14,12},{16,18},{18,... | collective-permute-start | bytes 98312 | tf_op jit(solution)/shard_map/ppermute | solution.py:70
  55.0 12.7 %collective-permute-start.12 = (bf16[768,768]{1,0:T(8,128)(2,1)}, bf16[768,768]{1,0:T(8,128)(2,1)}, u32[]{:S(2)}, u32[]{:S(2)}) collective-permute-start(bf16[768,768]{1,0:T(8,128)(2,1)} %get-tuple-element.97), channel_id=1, source_target_pairs={{0,1},{1,0},{2,3},{3,2},{4,5},{5,4},{6,7},{7,6},{8,9},{9,8},{10,11... | collective-permute-start | bytes 3538952 | tf_op jit(solution)/shard_map/ppermute | solution.py:66
  55.0 12.7 %collective-permute-start.13 = (bf16[768,768]{1,0:T(8,128)(2,1)S(1)}, bf16[768,768]{1,0:T(8,128)(2,1)}, u32[]{:S(2)}, u32[]{:S(2)}) collective-permute-start(bf16[768,768]{1,0:T(8,128)(2,1)S(1)} %get-tuple-element.98), channel_id=1, source_target_pairs={{0,1},{1,0},{2,3},{3,2},{4,5},{5,4},{6,7},{7,6},{8,9},{9,8},{10,11... | collective-permute-start | bytes 3538952 | tf_op jit(solution)/shard_map/ppermute | solution.py:66
  55.5 12.2 %collective-permute-start.11 = (bf16[768,768]{1,0:T(8,128)(2,1)S(1)}, bf16[768,768]{1,0:T(8,128)(2,1)}, u32[]{:S(2)}, u32[]{:S(2)}) collective-permute-start(bf16[768,768]{1,0:T(8,128)(2,1)S(1)} %get-tuple-element.96.after_ref), channel_id=1, source_target_pairs={{0,1},{1,0},{2,3},{3,2},{4,5},{5,4},{6,7},{7,6},{8,9},{9,8},{10,11... | collective-permute-start | bytes 3538952 | tf_op jit(solution)/shard_map/ppermute | solution.py:66
  56.5 18.9 %all-to-all-start.1 = ((bf16[8,256,128]{2,1,0:T(8,128)(2,1)}), bf16[8,256,128]{2,1,0:T(8,128)(2,1)S(1)}, u32[]{:S(2)}, u32[]{:S(2)}) async-start(bf16[8,256,128]{2,1,0:T(8,128)(2,1)} %pack_back.1.after_ref), calls=%async_computation.1 | async-start | bytes 1048576 | tf_op jit(solution)/shard_map/all_to_all | solution.py:79
  67.7 7.6 %copy-start.1 = (bf16[128,768]{1,0:T(8,128)(2,1)S(1)}, bf16[128,768]{1,0:T(8,128)(2,1)}, u32[]{:S(2)}) copy-start(bf16[128,768]{1,0:T(8,128)(2,1)} %get-tuple-element.74.stem_ref) | copy-start | bytes 589828
  67.7 7.6 %copy-start.2 = (bf16[320,128]{1,0:T(8,128)(2,1)S(1)}, bf16[320,128]{1,0:T(8,128)(2,1)}, u32[]{:S(2)}) copy-start(bf16[320,128]{1,0:T(8,128)(2,1)} %get-tuple-element.75.taken_ref) | copy-start | bytes 245764
  75.6 1.5 %collective-permute-start.14 = (bf16[128,768]{1,0:T(8,128)(2,1)S(1)}, bf16[128,768]{1,0:T(8,128)(2,1)S(1)}, u32[]{:S(2)}, u32[]{:S(2)}) collective-permute-start(bf16[128,768]{1,0:T(8,128)(2,1)S(1)} %get-tuple-element.108.own_ref), channel_id=1, source_target_pairs={{0,1},{1,0},{2,3},{3,2},{4,5},{5,4},{6,7},{7,6},{8,9},{9,8},{10,11... | collective-permute-start | bytes 589832 | tf_op jit(solution)/shard_map/ppermute | solution.py:66
  75.7 1.4 %collective-permute-start.15 = (f32[16,128]{1,0:T(8,128)S(1)}, f32[16,128]{1,0:T(8,128)S(1)}, u32[]{:S(2)}, u32[]{:S(2)}) collective-permute-start(f32[16,128]{1,0:T(8,128)S(1)} %get-tuple-element.109.a_ref), channel_id=1, source_target_pairs={{0,1},{1,0},{2,3},{3,2},{4,5},{5,4},{6,7},{7,6},{8,9},{9,8},{10,11... | collective-permute-start | bytes 24584 | tf_op jit(solution)/shard_map/ppermute | solution.py:66

commit v5 on v4

--- a/solution.py
+++ b/solution.py
@@ -939,7 +939,7 @@
     half = cot.shape[1]
     return kernel_call(
         near_grads_kernel,
-        20_000_000_000,
+        14_000_000_000,
         LANES,
         [far_off(a) for a in (normed, ggp, gup, hg, cot, after)],
         [pltpu.HBM((half, 2 * size), F32)] * 2
@@ -993,7 +993,7 @@
         fill_kernel,
         compiler_params=pltpu.CompilerParams(vmem_limit_bytes=12 * MIB),
         cost_estimate=pl.CostEstimate(
-            flops=10_000_000_000, bytes_accessed=LANES, transcendentals=0
+            flops=7_000_000_000, bytes_accessed=LANES, transcendentals=0
         ),
         grid_spec=pltpu.PrefetchScalarGridSpec(
             num_scalar_prefetch=1,

time: 78.9 us -> 78.9 us (level)
  no operation moved by 1% of the time
where the time goes in v5:
time: 78.9 us; the launch traced here: 78.5 us
  Pallas kernels  48.1 us (61%)
  starting transfers between devices  18 us (23%)
  waiting for transfers between devices  9.88 us (13%)
  local copies, waits for them, and re-layouts  1.54 us (2%)
  between operations  0.86 us (1%)
    pallas_call x14, Pallas kernels, kernel_call(): call(kernel, flops, moved, mib, grid_spec=pltpu.PrefetchScalarGridSpec(nu...  35.5 us
    all_to_all x2, starting transfers between devices, exchange(): lax.all_to_all(values, 'exp', split_axis=0, concat_axis=0, tiled=True, ax...  10.9 us
    all_to_all x2, waiting for transfers between devices, exchange(): lax.all_to_all(values, 'exp', split_axis=0, concat_axis=0, tiled=True, ax...  8.05 us
    pallas_call x1, Pallas kernels, forward(): pl.pallas_call(functools.partial(forward_kernel, paired, parts, width, ex...  7.97 us
    ppermute x4, starting transfers between devices, other_shard(): lax.ppermute(values, 'exp', [(i, i ^ 1) for i in range(lax.axis_size('exp...  4.71 us
    pallas_call x1, Pallas kernels, fill(): pl.pallas_call(fill_kernel, compiler_params=pltpu.CompilerParams(vmem_lim...  4.65 us
    ppermute x12, starting transfers between devices, other_core(): return lax.ppermute(values, 'rep', [(0, 1), (1, 0)])  2.38 us
  transfers between devices with their start and end apart: 18, of which 4 were waited for; matrix products, arithmetic and copies ran while one was open for 2% of the time, Pallas kernels for 56%

profile of v5, /device:TPU:0, one launch (start us, length us, event | category | flops | bytes accessed | tf_op | source)
XLA Modules:
  0.0 78.5 jit_solution(17210721343604729665)
XLA Ops:
  0.6 2.2 %pack.1.after.after_ref = bf16[8,258,128]{2,1,0:T(8,128)(2,1)} custom-call(bf16[2,16,64]{2,1,0:T(8,128)(2,1)} %latent_ref.1, s32[2,128]{1,0:T(2,128)} %bitcast.4, bf16[128,1536]{1,0:T(8,128)(2,1)} %cot_ref.3), custom_call_target="tpu_custom_call" | custom-call | flops 62914560 | bytes 1056768 | tf_op jit(solution)/shard_map/pack/pallas_call | solution.py:107
  2.9 7.3 %all-to-all-start = ((bf16[8,258,128]{2,1,0:T(8,128)(2,1)}), bf16[8,258,128]{2,1,0:T(8,128)(2,1)S(1)}, u32[]{:S(2)}, u32[]{:S(2)}) async-start(bf16[8,258,128]{2,1,0:T(8,128)(2,1)} %pack.1.after.after_ref), calls=%async_computation | async-start | bytes 1081344 | tf_op jit(solution)/shard_map/all_to_all | solution.py:79
  10.2 0.1 pad_add_fusion.place_ref
  10.2 0.0 copy-start.4
  10.2 0.0 copy-start.3
  10.2 4.4 %far_weights.1 = (bf16[768,768]{1,0:T(8,128)(2,1)}, bf16[768,768]{1,0:T(8,128)(2,1)}, bf16[768,768]{1,0:T(8,128)(2,1)}) custom-call(s32[3]{0:T(128)S(1)} %pad_add_fusion.place_ref, bf16[768,1536]{1,0:T(8,128)(2,1)} %refs_9_.1, bf16[768,1536]{1,0:T(8,128)(2,1)} %refs_5_.1, bf16[1536,768]{1,0:T(8,128)(2,1)} %refs_7_.1, bf16[8,258,128]{2,1,0:T(8,128)(2,1)} %pack.1.after.after_ref), custom_call_target="tpu_custom_call" | custom-call | bytes 128 | tf_op jit(solution)/shard_map/far_weights/pallas_call | solution.py:107
  14.6 0.1 collective-permute-start.1
  14.7 0.5 collective-permute-start.2
  15.2 0.1 collective-permute-start.3
  15.3 0.0 copy-done.4
  15.3 0.6 broadcast_in_dim.3.gain_in
  15.9 0.0 copy-done.3
  15.9 0.9 %copy.17.router_in = bf16[1536,8]{1,0:T(8,128)(2,1)} copy(bf16[1536,8]{0,1:T(8,128)(2,1)S(1)} %copy-done.3) | data formatting | bytes 49152 | tf_op args[3]
  16.8 3.1 %params.1 = (bf16[144,1536]{1,0:T(8,128)(2,1)}, f32[1,1536]{1,0:T(1,128)}, bf16[1536,128]{1,0:T(8,128)(2,1)}, bf16[320,128]{1,0:T(8,128)(2,1)}, bf16[128,768]{1,0:T(8,128)(2,1)}) custom-call(s32[3]{0:T(128)S(1)} %pad_add_fusion.place_ref, bf16[144,1536]{1,0:T(8,128)(2,1)} %stem_in.1, f32[1,1536]{1,0:T(1,128)} %broadcast_in_dim.3.gain_in, ...), custom_call_target="tpu_custom_call" | custom-call | bytes 128 | tf_op jit(solution)/shard_map/params/pallas_call | solution.py:107
  19.9 5.1 %all-to-all-done.packed_ref = bf16[8,258,128]{2,1,0:T(8,128)(2,1)S(1)} async-done(((bf16[8,258,128]{2,1,0:T(8,128)(2,1)}), bf16[8,258,128]{2,1,0:T(8,128)(2,1)S(1)}, u32[]{:S(2)}, u32[]{:S(2)}) %all-to-all-start) | async-done | bytes 528416 | tf_op jit(solution)/shard_map/all_to_all | solution.py:79
  25.0 0.1 collective-permute-start.4
  25.1 1.6 %collective-permute-start = (bf16[8,18,128]{2,1,0:T(8,128)(2,1)S(1)}, bf16[8,18,128]{2,1,0:T(8,128)(2,1)S(1)}, u32[]{:S(2)}, u32[]{:S(2)}) collective-permute-start(bf16[8,18,128]{2,1,0:T(8,128)(2,1)S(1)} %get-tuple-element.61.refs_0_.same_ref), channel_id=1, source_target_pairs={{0,2},{2,0},{4,6},{6,4},{8,10},{10,8},{12,14},{14,12},{16,18},{18,... | collective-permute-start | bytes 110600 | tf_op jit(solution)/shard_map/ppermute | solution.py:70
  26.7 0.0 collective-permute-done.1.refs_1_.refs_10_
  26.7 0.5 collective-permute-start.5
  27.2 2.1 %gather.1 = (bf16[144,1536]{1,0:T(8,128)(2,1)S(1)}, f32[1,1536]{1,0:T(1,128)S(1)}, bf16[1536,896]{1,0:T(8,128)(2,1)S(1)}) custom-call(s32[3]{0:T(128)S(1)} %pad_add_fusion.place_ref, bf16[768,1536]{1,0:T(8,128)(2,1)} %refs_9_.1, bf16[768,768]{1,0:T(8,128)(2,1)S(1)} %collective-permute-done.1.refs_1_.refs_10_, bf16[144,1536]{1,0:T(8,128)(2,1)} %get-tuple-element.63.refs_2_, ...), custom_call_target="tpu_custom_call" | custom-call | bytes 128 | tf_op jit(solution)/shard_map/gather/pallas_call | solution.py:107
  29.4 0.0 collective-permute-done.refs_1_.other_ref
  29.4 0.0 collective-permute-done.2.refs_6_
  29.4 0.0 collective-permute-done.3.refs_8_
  29.4 0.0 collective-permute-done.4.refs_12_.refs_2_.refs_0_
  29.4 8.0 %forward.1 = (bf16[640,768]{1,0:T(8,128)(2,1)}, bf16[640,1536]{1,0:T(8,128)(2,1)S(1)}, bf16[640,1536]{1,0:T(8,128)(2,1)S(1)}, f32[640,128]{1,0:T(8,128)S(1)}, f3...) custom-call(s32[3]{0:T(128)S(1)} %pad_add_fusion.place_ref, ...), custom_call_target="tpu_custom_call" | custom-call | flops 99999997952 | bytes 128 | tf_op jit(solution)/shard_map/forward/pallas_call | solution.py:648
  37.4 0.1 collective-permute-start.7
  37.5 1.7 %outputs.1 = (bf16[320,768]{1,0:T(8,128)(2,1)S(1)}, bf16[320,768]{1,0:T(8,128)(2,1)S(1)}, bf16[128,768]{1,0:T(8,128)(2,1)}) custom-call(s32[3]{0:T(128)S(1)} %pad_add_fusion.place_ref, f32[640,128]{1,0:T(8,128)S(1)} %get-tuple-element.71.meta_ref, bf16[640,768]{1,0:T(8,128)(2,1)S(1)} %get-tuple-element.72.hidden_ref, ...), custom_call_target="tpu_custom_call" | custom-call | bytes 128 | tf_op jit(solution)/shard_map/outputs/pallas_call | solution.py:107
  39.1 0.8 %collective-permute-done.5.refs_1_ = bf16[320,768]{1,0:T(8,128)(2,1)S(1)} collective-permute-done((bf16[320,768]{1,0:T(8,128)(2,1)S(1)}, bf16[320,768]{1,0:T(8,128)(2,1)S(1)}, u32[]{:S(2)}, u32[]{:S(2)}) %collective-permute-start.5) | collective-permute-done | bytes 491552 | tf_op jit(solution)/shard_map/ppermute | solution.py:70
  40.0 0.0 collective-permute-start.9
  40.0 0.5 collective-permute-start.6
  40.5 0.0 collective-permute-done.7.b_ref
  40.5 0.1 add_up.1
  40.6 1.4 %collective-permute-start.8 = (bf16[320,768]{1,0:T(8,128)(2,1)S(1)}, bf16[320,768]{1,0:T(8,128)(2,1)S(1)}, u32[]{:S(2)}, u32[]{:S(2)}) collective-permute-start(bf16[320,768]{1,0:T(8,128)(2,1)S(1)} %add_up.1), channel_id=1, source_target_pairs={{0,2},{2,0},{4,6},{6,4},{8,10},{10,8},{12,14},{14,12},{16,18},{18,... | collective-permute-start | bytes 1474568 | tf_op jit(solution)/shard_map/ppermute | solution.py:70
  42.0 0.0 collective-permute-done.9.refs_3_.refs_1_
  42.0 0.0 copy-start
  42.0 7.2 %backward.1 = (bf16[640,768]{1,0:T(8,128)(2,1)}, bf16[640,768]{1,0:T(8,128)(2,1)}, bf16[640,768]{1,0:T(8,128)(2,1)}, bf16[640,768]{1,0:T(8,128)(2,1)}, bf16[640,...) custom-call(bf16[144,1536]{1,0:T(8,128)(2,1)S(1)} %get-tuple-element, ...), custom_call_target="tpu_custom_call" | custom-call | flops 6039797760 | bytes 16908288 | tf_op jit(solution)/shard_map/backward/pallas_call | solution.py:107
  49.2 0.0 copy-done
  49.2 1.1 %to_image.1 = (f32[8,16,128]{2,1,0:T(8,128)S(1)}, bf16[8,16,128]{2,1,0:T(8,128)(2,1)S(1)}) custom-call(s32[3]{0:T(128)S(1)} %pad_add_fusion.place_ref, bf16[640,144]{1,0:T(8,128)(2,1)S(1)} %get-tuple-element.87.proj_ref, bf16[8,80,256]{2,1,0:T(8,128)(2,1)S(1)} %get-tuple-element.88.sel_ref, bf16[144,1536]{1,0:T(8,128)(2,1)S(1)} %get-tuple-element.65.refs_2_.stem_ref, ...), custom_call_target="tpu_custom_call" | custom-call | flops 47185920 | bytes 1179648 | tf_op jit(solution)/shard_map/to_image/pallas_call | solution.py:107
  50.4 1.2 %collective-permute-start.10 = (bf16[8,16,128]{2,1,0:T(8,128)(2,1)S(1)}, bf16[8,16,128]{2,1,0:T(8,128)(2,1)S(1)}, u32[]{:S(2)}, u32[]{:S(2)}) collective-permute-start(bf16[8,16,128]{2,1,0:T(8,128)(2,1)S(1)} %get-tuple-element.91), channel_id=1, source_target_pairs={{0,2},{2,0},{4,6},{6,4},{8,10},{10,8},{12,14},{14,12},{16,18},{18,... | collective-permute-start | bytes 98312 | tf_op jit(solution)/shard_map/ppermute | solution.py:70
  51.6 3.4 %far_grads.1 = (bf16[768,768]{1,0:T(8,128)(2,1)S(1)}, bf16[768,768]{1,0:T(8,128)(2,1)}, bf16[768,768]{1,0:T(8,128)(2,1)S(1)}) custom-call(bf16[640,1536]{1,0:T(8,128)(2,1)S(1)} %get-tuple-element.92.normed, bf16[640,768]{1,0:T(8,128)(2,1)S(1)} %get-tuple-element.93.ggp, bf16[640,768]{1,0:T(8,128)(2,1)S(1)} %get-tuple-element.94.gup, ...), custom_call_target="tpu_custom_call" | custom-call | flops 2264924160 | bytes 9830400 | tf_op jit(solution)/shard_map/far_grads/pallas_call | solution.py:107
  55.0 0.0 collective-permute-start.12
  55.0 0.5 collective-permute-start.13
  55.5 0.0 collective-permute-done.6.b_ref
  55.5 0.0 collective-permute-start.11
  55.5 0.0 collective-permute-done.10.over_ref
  55.5 0.0 collective-permute-done.8.c_ref
  55.5 0.9 %pack_back.1.after_ref = bf16[8,256,128]{2,1,0:T(8,128)(2,1)} custom-call(bf16[320,768]{1,0:T(8,128)(2,1)S(1)} %get-tuple-element.77.after_ref.a_ref, bf16[320,768]{1,0:T(8,128)(2,1)S(1)} %collective-permute-done.6.b_ref, bf16[320,768]{1,0:T(8,128)(2,1)S(1)} %collective-permute-done.8.c_ref, f32[8,16,128]{2,1,0:T(8,128)S(1)} %get-tuple-element.90.terms_ref, ...), custom_call_target="tpu_custom_call" | custom-call | flops 245760 | bytes 1966080 | tf_op jit(solution)/shard_map/pack_back/pallas_call | solution.py:107
  56.5 3.6 %all-to-all-start.1 = ((bf16[8,256,128]{2,1,0:T(8,128)(2,1)}), bf16[8,256,128]{2,1,0:T(8,128)(2,1)S(1)}, u32[]{:S(2)}, u32[]{:S(2)}) async-start(bf16[8,256,128]{2,1,0:T(8,128)(2,1)} %pack_back.1.after_ref), calls=%async_computation.1 | async-start | bytes 1048576 | tf_op jit(solution)/shard_map/all_to_all | solution.py:79
  60.1 7.5 %near_grads.1 = (f32[768,1536]{1,0:T(8,128)}, f32[768,1536]{1,0:T(8,128)}, f32[1536,768]{1,0:T(8,128)}) custom-call(s32[3]{0:T(128)S(1)} %pad_add_fusion.place_ref, bf16[640,768]{1,0:T(8,128)(2,1)} %get-tuple-element.99.normed, bf16[640,768]{1,0:T(8,128)(2,1)} %get-tuple-element.100.ggp, bf16[640,768]{1,0:T(8,128)(2,1)} %get-tuple-element.101.gup, ...), custom_call_target="tpu_custom_call" | custom-call | flops 14000000000 | bytes 128 | tf_op jit(solution)/shard_map/near_grads/pallas_call | solution.py:107
  67.7 0.0 collective-permute-done.12.up_in
  67.7 0.0 collective-permute-done.13.down_in
  67.7 0.0 collective-permute-done.11.gate_in
  67.7 0.0 copy-start.1
  67.7 0.0 copy-start.2
  67.7 4.7 %fill.1 = (f32[768,1536]{1,0:T(8,128)}, f32[768,1536]{1,0:T(8,128)}, f32[1536,768]{1,0:T(8,128)}, f32[8,128]{1,0:T(8,128)S(1)}) custom-call(s32[3]{0:T(128)S(1)} %pad_add_fusion.place_ref, bf16[768,768]{1,0:T(8,128)(2,1)} %collective-permute-done.11.gate_in, ...), custom_call_target="tpu_custom_call", output_to_operand_aliasing={{0}: (4, {}), {1}: (5, {}), {2}: (6, {})} | custom-call | flops 7000000000 | bytes 128 | tf_op jit(solution)/shard_map/fill/pallas_call | solution.py:992
  72.4 2.9 %all-to-all-done.1.back_ref = bf16[8,256,128]{2,1,0:T(8,128)(2,1)S(1)} async-done(((bf16[8,256,128]{2,1,0:T(8,128)(2,1)}), bf16[8,256,128]{2,1,0:T(8,128)(2,1)S(1)}, u32[]{:S(2)}, u32[]{:S(2)}) %all-to-all-start.1) | async-done | bytes 524320 | tf_op jit(solution)/shard_map/all_to_all | solution.py:79
  75.3 0.0 copy-done.1
  75.3 0.0 copy-done.2
  75.3 0.3 mixed.1
  75.6 0.1 collective-permute-start.14
  75.7 0.5 collective-permute-start.15
  76.2 0.9 %collective-permute-done.15.b_ref = f32[16,128]{1,0:T(8,128)S(1)} collective-permute-done((f32[16,128]{1,0:T(8,128)S(1)}, f32[16,128]{1,0:T(8,128)S(1)}, u32[]{:S(2)}, u32[]{:S(2)}) %collective-permute-start.15) | collective-permute-done | bytes 8224 | tf_op jit(solution)/shard_map/ppermute | solution.py:66
  77.2 0.0 collective-permute-done.14.away_ref
  77.2 1.3 %join.1 = (bf16[128,1536]{1,0:T(8,128)(2,1)}, f32[2,16,64]{2,1,0:T(8,128)}) custom-call(s32[3]{0:T(128)S(1)} %pad_add_fusion.place_ref, bf16[128,768]{1,0:T(8,128)(2,1)S(1)} %get-tuple-element.108.own_ref, bf16[128,768]{1,0:T(8,128)(2,1)S(1)} %collective-permute-done.14.away_ref, f32[16,128]{1,0:T(8,128)S(1)} %get-tuple-element.109.a_ref, ...), custom_call_target="tpu_custom_call" | custom-call | bytes 786432 | tf_op jit(solution)/shard_map/join/pallas_call | solution.py:107
  (1 shorter events, 0.0 us)
Async XLA Ops:
  2.9 22.1 %all-to-all-start = ((bf16[8,258,128]{2,1,0:T(8,128)(2,1)}), bf16[8,258,128]{2,1,0:T(8,128)(2,1)S(1)}, u32[]{:S(2)}, u32[]{:S(2)}) async-start(bf16[8,258,128]{2,1,0:T(8,128)(2,1)} %pack.1.after.after_ref), calls=%async_computation | async-start | bytes 1081344 | tf_op jit(solution)/shard_map/all_to_all | solution.py:79
  10.2 5.0 %copy-start.4 = (f32[1536]{0:T(1024)S(1)}, f32[1536]{0:T(1024)}, u32[]{:S(2)}) copy-start(f32[1536]{0:T(1024)} %param.11) | copy-start | bytes 18436
  10.2 5.6 %copy-start.3 = (bf16[1536,8]{0,1:T(8,128)(2,1)S(1)}, bf16[1536,8]{0,1:T(8,128)(2,1)}, u32[]{:S(2)}) copy-start(bf16[1536,8]{0,1:T(8,128)(2,1)} %param.12) | copy-start | bytes 73732
  14.6 12.1 %collective-permute-start.1 = (bf16[768,768]{1,0:T(8,128)(2,1)}, bf16[768,768]{1,0:T(8,128)(2,1)S(1)}, u32[]{:S(2)}, u32[]{:S(2)}) collective-permute-start(bf16[768,768]{1,0:T(8,128)(2,1)} %get-tuple-element.62), channel_id=1, source_target_pairs={{0,1},{1,0},{2,3},{3,2},{4,5},{5,4},{6,7},{7,6},{8,9},{9,8},{10,11... | collective-permute-start | bytes 3538952 | tf_op jit(solution)/shard_map/ppermute | solution.py:66
  14.7 14.7 %collective-permute-start.2 = (bf16[768,768]{1,0:T(8,128)(2,1)}, bf16[768,768]{1,0:T(8,128)(2,1)S(1)}, u32[]{:S(2)}, u32[]{:S(2)}) collective-permute-start(bf16[768,768]{1,0:T(8,128)(2,1)} %get-tuple-element.68), channel_id=1, source_target_pairs={{0,1},{1,0},{2,3},{3,2},{4,5},{5,4},{6,7},{7,6},{8,9},{9,8},{10,11... | collective-permute-start | bytes 3538952 | tf_op jit(solution)/shard_map/ppermute | solution.py:66
  15.2 14.2 %collective-permute-start.3 = (bf16[768,768]{1,0:T(8,128)(2,1)}, bf16[768,768]{1,0:T(8,128)(2,1)}, u32[]{:S(2)}, u32[]{:S(2)}) collective-permute-start(bf16[768,768]{1,0:T(8,128)(2,1)} %get-tuple-element.69), channel_id=1, source_target_pairs={{0,1},{1,0},{2,3},{3,2},{4,5},{5,4},{6,7},{7,6},{8,9},{9,8},{10,11... | collective-permute-start | bytes 3538952 | tf_op jit(solution)/shard_map/ppermute | solution.py:66
  25.0 4.4 %collective-permute-start.4 = (bf16[320,768]{1,0:T(8,128)(2,1)S(1)}, bf16[320,768]{1,0:T(8,128)(2,1)S(1)}, u32[]{:S(2)}, u32[]{:S(2)}) collective-permute-start(bf16[320,768]{1,0:T(8,128)(2,1)S(1)} %get-tuple-element.70.refs_0_), channel_id=1, source_target_pairs={{0,1},{1,0},{2,3},{3,2},{4,5},{5,4},{6,7},{7,6},{8,9},{9,8},{10,11... | collective-permute-start | bytes 1474568 | tf_op jit(solution)/shard_map/ppermute | solution.py:66
  25.1 4.2 %collective-permute-start = (bf16[8,18,128]{2,1,0:T(8,128)(2,1)S(1)}, bf16[8,18,128]{2,1,0:T(8,128)(2,1)S(1)}, u32[]{:S(2)}, u32[]{:S(2)}) collective-permute-start(bf16[8,18,128]{2,1,0:T(8,128)(2,1)S(1)} %get-tuple-element.61.refs_0_.same_ref), channel_id=1, source_target_pairs={{0,2},{2,0},{4,6},{6,4},{8,10},{10,8},{12,14},{14,12},{16,18},{18,... | collective-permute-start | bytes 110600 | tf_op jit(solution)/shard_map/ppermute | solution.py:70
  26.7 13.3 %collective-permute-start.5 = (bf16[320,768]{1,0:T(8,128)(2,1)S(1)}, bf16[320,768]{1,0:T(8,128)(2,1)S(1)}, u32[]{:S(2)}, u32[]{:S(2)}) collective-permute-start(bf16[320,768]{1,0:T(8,128)(2,1)S(1)} %get-tuple-element.70.refs_0_), channel_id=1, source_target_pairs={{0,2},{2,0},{4,6},{6,4},{8,10},{10,8},{12,14},{14,12},{16,18},{18,... | collective-permute-start | bytes 1474568 | tf_op jit(solution)/shard_map/ppermute | solution.py:70
  37.4 3.1 %collective-permute-start.7 = (bf16[320,768]{1,0:T(8,128)(2,1)S(1)}, bf16[320,768]{1,0:T(8,128)(2,1)S(1)}, u32[]{:S(2)}, u32[]{:S(2)}) collective-permute-start(bf16[320,768]{1,0:T(8,128)(2,1)S(1)} %get-tuple-element.80), channel_id=1, source_target_pairs={{0,1},{1,0},{2,3},{3,2},{4,5},{5,4},{6,7},{7,6},{8,9},{9,8},{10,11... | collective-permute-start | bytes 1474568 | tf_op jit(solution)/shard_map/ppermute | solution.py:66
  40.0 2.0 %collective-permute-start.9 = (bf16[320,768]{1,0:T(8,128)(2,1)S(1)}, bf16[320,768]{1,0:T(8,128)(2,1)S(1)}, u32[]{:S(2)}, u32[]{:S(2)}) collective-permute-start(bf16[320,768]{1,0:T(8,128)(2,1)S(1)} %collective-permute-done.5.refs_1_), channel_id=1, source_target_pairs={{0,1},{1,0},{2,3},{3,2},{4,5},{5,4},{6,7},{7,6},{8,9},{9,8},{10,11... | collective-permute-start | bytes 1474568 | tf_op jit(solution)/shard_map/ppermute | solution.py:66
  40.0 15.5 %collective-permute-start.6 = (bf16[320,768]{1,0:T(8,128)(2,1)S(1)}, bf16[320,768]{1,0:T(8,128)(2,1)S(1)}, u32[]{:S(2)}, u32[]{:S(2)}) collective-permute-start(bf16[320,768]{1,0:T(8,128)(2,1)S(1)} %get-tuple-element.78), channel_id=1, source_target_pairs={{0,1},{1,0},{2,3},{3,2},{4,5},{5,4},{6,7},{7,6},{8,9},{9,8},{10,11... | collective-permute-start | bytes 1474568 | tf_op jit(solution)/shard_map/ppermute | solution.py:66
  40.6 14.9 %collective-permute-start.8 = (bf16[320,768]{1,0:T(8,128)(2,1)S(1)}, bf16[320,768]{1,0:T(8,128)(2,1)S(1)}, u32[]{:S(2)}, u32[]{:S(2)}) collective-permute-start(bf16[320,768]{1,0:T(8,128)(2,1)S(1)} %add_up.1), channel_id=1, source_target_pairs={{0,2},{2,0},{4,6},{6,4},{8,10},{10,8},{12,14},{14,12},{16,18},{18,... | collective-permute-start | bytes 1474568 | tf_op jit(solution)/shard_map/ppermute | solution.py:70
  42.0 7.2 %copy-start = (bf16[128,768]{1,0:T(8,128)(2,1)S(1)}, bf16[128,768]{1,0:T(8,128)(2,1)}, u32[]{:S(2)}) copy-start(bf16[128,768]{1,0:T(8,128)(2,1)} %get-tuple-element.89.cot_ref) | copy-start | bytes 589828
  50.4 5.2 %collective-permute-start.10 = (bf16[8,16,128]{2,1,0:T(8,128)(2,1)S(1)}, bf16[8,16,128]{2,1,0:T(8,128)(2,1)S(1)}, u32[]{:S(2)}, u32[]{:S(2)}) collective-permute-start(bf16[8,16,128]{2,1,0:T(8,128)(2,1)S(1)} %get-tuple-element.91), channel_id=1, source_target_pairs={{0,2},{2,0},{4,6},{6,4},{8,10},{10,8},{12,14},{14,12},{16,18},{18,... | collective-permute-start | bytes 98312 | tf_op jit(solution)/shard_map/ppermute | solution.py:70
  55.0 12.7 %collective-permute-start.12 = (bf16[768,768]{1,0:T(8,128)(2,1)}, bf16[768,768]{1,0:T(8,128)(2,1)}, u32[]{:S(2)}, u32[]{:S(2)}) collective-permute-start(bf16[768,768]{1,0:T(8,128)(2,1)} %get-tuple-element.97), channel_id=1, source_target_pairs={{0,1},{1,0},{2,3},{3,2},{4,5},{5,4},{6,7},{7,6},{8,9},{9,8},{10,11... | collective-permute-start | bytes 3538952 | tf_op jit(solution)/shard_map/ppermute | solution.py:66
  55.0 12.7 %collective-permute-start.13 = (bf16[768,768]{1,0:T(8,128)(2,1)S(1)}, bf16[768,768]{1,0:T(8,128)(2,1)}, u32[]{:S(2)}, u32[]{:S(2)}) collective-permute-start(bf16[768,768]{1,0:T(8,128)(2,1)S(1)} %get-tuple-element.98), channel_id=1, source_target_pairs={{0,1},{1,0},{2,3},{3,2},{4,5},{5,4},{6,7},{7,6},{8,9},{9,8},{10,11... | collective-permute-start | bytes 3538952 | tf_op jit(solution)/shard_map/ppermute | solution.py:66
  55.5 12.2 %collective-permute-start.11 = (bf16[768,768]{1,0:T(8,128)(2,1)S(1)}, bf16[768,768]{1,0:T(8,128)(2,1)}, u32[]{:S(2)}, u32[]{:S(2)}) collective-permute-start(bf16[768,768]{1,0:T(8,128)(2,1)S(1)} %get-tuple-element.96.after_ref), channel_id=1, source_target_pairs={{0,1},{1,0},{2,3},{3,2},{4,5},{5,4},{6,7},{7,6},{8,9},{9,8},{10,11... | collective-permute-start | bytes 3538952 | tf_op jit(solution)/shard_map/ppermute | solution.py:66
  56.5 18.9 %all-to-all-start.1 = ((bf16[8,256,128]{2,1,0:T(8,128)(2,1)}), bf16[8,256,128]{2,1,0:T(8,128)(2,1)S(1)}, u32[]{:S(2)}, u32[]{:S(2)}) async-start(bf16[8,256,128]{2,1,0:T(8,128)(2,1)} %pack_back.1.after_ref), calls=%async_computation.1 | async-start | bytes 1048576 | tf_op jit(solution)/shard_map/all_to_all | solution.py:79
  67.7 7.6 %copy-start.1 = (bf16[128,768]{1,0:T(8,128)(2,1)S(1)}, bf16[128,768]{1,0:T(8,128)(2,1)}, u32[]{:S(2)}) copy-start(bf16[128,768]{1,0:T(8,128)(2,1)} %get-tuple-element.74.stem_ref) | copy-start | bytes 589828
  67.7 7.6 %copy-start.2 = (bf16[320,128]{1,0:T(8,128)(2,1)S(1)}, bf16[320,128]{1,0:T(8,128)(2,1)}, u32[]{:S(2)}) copy-start(bf16[320,128]{1,0:T(8,128)(2,1)} %get-tuple-element.75.taken_ref) | copy-start | bytes 245764
  75.6 1.5 %collective-permute-start.14 = (bf16[128,768]{1,0:T(8,128)(2,1)S(1)}, bf16[128,768]{1,0:T(8,128)(2,1)S(1)}, u32[]{:S(2)}, u32[]{:S(2)}) collective-permute-start(bf16[128,768]{1,0:T(8,128)(2,1)S(1)} %get-tuple-element.108.own_ref), channel_id=1, source_target_pairs={{0,1},{1,0},{2,3},{3,2},{4,5},{5,4},{6,7},{7,6},{8,9},{9,8},{10,11... | collective-permute-start | bytes 589832 | tf_op jit(solution)/shard_map/ppermute | solution.py:66
  75.7 1.4 %collective-permute-start.15 = (f32[16,128]{1,0:T(8,128)S(1)}, f32[16,128]{1,0:T(8,128)S(1)}, u32[]{:S(2)}, u32[]{:S(2)}) collective-permute-start(f32[16,128]{1,0:T(8,128)S(1)} %get-tuple-element.109.a_ref), channel_id=1, source_target_pairs={{0,1},{1,0},{2,3},{3,2},{4,5},{5,4},{6,7},{7,6},{8,9},{9,8},{10,11... | collective-permute-start | bytes 24584 | tf_op jit(solution)/shard_map/ppermute | solution.py:66
